TPU v7x, 32 devices: a whole 2x2x4 slice. The times are simulated.
32 devices in a mesh: grp: 8 (over y, x, core), tp: 4 (over z).
Axes of the slice: x: 2, y: 2, z: 4, core: 2. Of those that a mesh axis runs over, the one named last changes fastest.
Arguments:
- tokens: bfloat16 [4096, 8192], P('grp', 'tp'), may hold values from -6 to 6
- base_weight: bfloat16 [8192, 2048], P('tp'), may hold values from -0.0625 to 0.0625
- down_tables: bfloat16 [1024, 8192, 16], P('grp', 'tp'), may hold values from -0.0625 to 0.0625
- up_tables: bfloat16 [1024, 16, 2048], P('grp', None, 'tp'), may hold values from -1.5 to 1.5
- block_owner: int32 [32, 1], P('grp'), may hold values from 0 to 7; in each aligned block of 4 rows (0 to 3, 4 to 7, ...) at most 2 rows name the same one
- block_local: int32 [32], P('grp'), may hold values from 0 to 127
- block_count: int32 [32], P('grp'), may hold values from 1 to 128
Outputs:
- projected: bfloat16 [4096, 2048], P('grp', 'tp')
Inputs may be any that keep to these rules, and one draw needn't show every extreme that they name: `block_owner`: among the 4 blocks of one group (an aligned run of 4 entries) no owner is named more than 2 times, a bound that some block reaches.
All inputs are finite; a program needn't handle non-finite values.
Results may differ from a plain program's by a relative error of at most 0.001.
Values may be sent and summed in bfloat16 or wider, within the bound.
No kernel may reach another device: no remote copies, remote signals or barrier semaphores. Data moves between devices by JAX's collectives and lax.ppermute only.
A program may use at most 64 MiB of HBM per device.

v0:
```python
import jax
import jax.numpy as jnp
from jax import lax
from jax.sharding import PartitionSpec as P

R = 16
BLOCK = 128
CAP = 2


adapter_scale = 2.0


def slot_plan(block_owner):
    owners = block_owner[:, 0]
    block_total = owners.shape[0]
    order = jnp.arange(block_total, dtype=jnp.int32)
    earlier = (owners[None, :] == owners[:, None]) & (order[None, :] < order[:, None])
    ranked = jnp.sum(earlier.astype(jnp.int32), axis=1)
    return owners * CAP + ranked


def body(tokens, base_weight, down_tables, up_tables, block_owner, block_local, block_count):
    group_count = lax.axis_size("grp")
    block_total = block_owner.shape[0]
    feature_cols = tokens.shape[1]
    slot_total = group_count * CAP
    block_slot = slot_plan(block_owner)
    slot_match = block_slot[:, None] == jnp.arange(slot_total, dtype=jnp.int32)[None, :]
    wanted_ids = jnp.sum(jnp.where(slot_match, block_local[:, None], 0), axis=0)
    wanted_ids = wanted_ids.reshape(group_count, CAP)
    partial_value = jnp.dot(tokens, base_weight, preferred_element_type=jnp.float32)
    base_projection = lax.psum_scatter(partial_value, "tp", scatter_dimension=1, tiled=True)
    local_ids = lax.all_to_all(wanted_ids, "grp", split_axis=0, concat_axis=0, tiled=True)
    down_sel = jnp.take(down_tables, local_ids, axis=0)
    up_sel = jnp.take(up_tables, local_ids, axis=0)
    down_got = lax.all_to_all(down_sel, "grp", split_axis=0, concat_axis=0, tiled=True)
    up_got = lax.all_to_all(up_sel, "grp", split_axis=0, concat_axis=0, tiled=True)
    down_block = jnp.take(down_got.reshape(slot_total, feature_cols, R), block_slot, axis=0)
    up_block = jnp.take(up_got.reshape(slot_total, R, up_got.shape[-1]), block_slot, axis=0)
    blocked = tokens.reshape(block_total, BLOCK, feature_cols)
    reduced = jnp.einsum("nbd,ndr->nbr", blocked, down_block, preferred_element_type=jnp.float32)
    reduced = lax.psum(reduced, "tp")
    adapter_output = jnp.einsum(
        "nbr,nro->nbo", reduced, up_block.astype(jnp.float32), precision=lax.Precision.HIGHEST
    )
    row_total = block_total * BLOCK
    adapter_output = adapter_output.reshape(row_total, adapter_output.shape[-1])
    offsets = jnp.arange(BLOCK, dtype=jnp.int32)
    live_rows = (offsets[None, :] < block_count[:, None]).reshape(row_total, 1)
    combined_output = base_projection + adapter_scale * adapter_output
    return jnp.where(live_rows, combined_output, jnp.float32(0.0)).astype(jnp.bfloat16)


def solution(mesh):
    placed = (
        P("grp", "tp"),
        P("tp", None),
        P("grp", "tp", None),
        P("grp", None, "tp"),
        P("grp", None),
        P("grp"),
        P("grp"),
    )
    return jax.shard_map(
        body, mesh=mesh, in_specs=placed, out_specs=P("grp", "tp"), check_vma=False
    )
```

profile of v0, /device:TPU:0, one launch (start us, length us, event | category | flops | bytes accessed | tf_op | source)
XLA Modules:
  0.0 107.3 jit_solution(8055788047387857914)
XLA Ops:
  6.5 0.0 copy-start
  6.5 0.0 reduce-scatter.2.cloned.1.call-start
  6.5 1.6 %copy-done = bf16[512,2048]{1,0:T(8,128)(2,1)S(1)} copy-done((bf16[512,2048]{1,0:T(8,128)(2,1)S(1)}, bf16[512,2048]{1,0:T(8,128)(2,1)}, u32[]{:S(2)}) %copy-start) | copy-done | bytes 2097176
  8.1 9.4 %fusion.14 = f32[512,2048]{1,0:T(8,128)} fusion(bf16[512,2048]{1,0:T(8,128)(2,1)S(1)} %copy-done, bf16[2048,2048]{1,0:T(8,128)(2,1)} %param.8), kind=kOutput, calls=%fused_computation.36 | convolution fusion | flops 4294967296 | bytes 14680064 | tf_op jit(solution)/shard_map/dot_general | solution.py:32
  17.5 0.0 copy-start.1
  17.5 0.0 copy-start.2
  17.5 0.0 reduce-scatter.2.cloned.1.call-update
  17.5 0.6 copy-done.1
  18.1 0.2 convert_reduce_fusion
  18.3 0.0 copy-done.2
  18.3 0.1 select_reduce_fusion
  18.4 0.1 all_to_all.16
  18.5 9.6 %all_to_all.25 = s32[8,1,2]{2,1,0:T(1,128)S(1)} all-to-all(s32[8,1,2]{2,1,0:T(1,128)S(1)} %bitcast.46), channel_id=1, replica_groups=mesh['grp'=8,'tp'=4] {'grp'}, dimensions={0} | all-to-all | bytes 128 | tf_op jit(solution)/shard_map/all_to_all | solution.py:34
  28.1 0.1 copy.25
  28.2 0.1 copy.28
  28.3 0.1 reshape.80
  28.4 0.1 copy.26
  28.5 4.0 %gather_fusion = bf16[16,2048,16]{1,2,0:T(8,128)(2,1)S(1)} fusion(bf16[128,2048,16]{1,2,0:T(8,128)(2,1)} %param.9, s32[1024]{0:T(1024)S(1)} %pad_clamp_fusion.1), kind=kCustom, calls=%fused_computation | custom fusion | bytes 2097216 | tf_op jit(solution)/shard_map/jit(_take)/gather | solution.py:35
  32.5 2.2 %gather_fusion.2 = bf16[16,16,512]{2,1,0:T(8,128)(2,1)S(1)} fusion(bf16[128,16,512]{2,1,0:T(8,128)(2,1)} %param.10, s32[1024]{0:T(1024)S(1)} %pad_clamp_fusion.1), kind=kCustom, calls=%fused_computation.2 | custom fusion | bytes 524352 | tf_op jit(solution)/shard_map/jit(_take)/gather | solution.py:36
  34.7 0.8 broadcast_select_fusion.1
  35.5 3.4 %all-to-all-start.2 = ((bf16[8,2,16,512]{3,2,1,0:T(8,128)(2,1)}), bf16[8,2,16,512]{3,2,1,0:T(8,128)(2,1)S(1)}, u32[]{:S(2)}, u32[]{:S(2)}) async-start(bf16[8,2,16,512]{3,2,1,0:T(8,128)(2,1)} %broadcast_select_fusion.1), calls=%async_computation.3 | async-start | bytes 524288 | tf_op jit(solution)/shard_map/all_to_all | solution.py:38
  38.9 0.0 copy-start.3
  38.9 1.2 %broadcast_select_fusion = bf16[8,2,2048,16]{2,3,1,0:T(8,128)(2,1)} fusion(bf16[8,2,2048,16]{2,3,1,0:T(8,128)(2,1)S(1)} %bitcast.42, pred[8,2]{1,0:T(8,128)(4,1)S(1)} %copy.26), kind=kLoop, calls=%fused_computation.9 | loop fusion | flops 524288 | bytes 2097168 | tf_op jit(solution)/shard_map/jit(_take)/select_n | solution.py:35
  40.1 5.7 %all-to-all-done.2 = bf16[8,2,16,512]{3,2,1,0:T(8,128)(2,1)S(1)} async-done(((bf16[8,2,16,512]{3,2,1,0:T(8,128)(2,1)}), bf16[8,2,16,512]{3,2,1,0:T(8,128)(2,1)S(1)}, u32[]{:S(2)}, u32[]{:S(2)}) %all-to-all-start.2) | async-done | bytes 262176 | tf_op jit(solution)/shard_map/all_to_all | solution.py:38
  45.7 3.6 %all-to-all-start.1 = ((bf16[8,2,2048,16]{2,3,1,0:T(8,128)(2,1)}), bf16[8,2,2048,16]{2,3,1,0:T(8,128)(2,1)S(1)}, u32[]{:S(2)}, u32[]{:S(2)}) async-start(bf16[8,2,2048,16]{2,3,1,0:T(8,128)(2,1)} %broadcast_select_fusion), calls=%async_computation.2 | async-start | bytes 2097152 | tf_op jit(solution)/shard_map/all_to_all | solution.py:37
  49.3 0.0 copy-done.3
  49.3 0.1 fusion.8
  49.4 0.6 gather_fusion.3
  50.0 14.7 %all-to-all-done.1 = bf16[8,2,2048,16]{2,3,1,0:T(8,128)(2,1)S(1)} async-done(((bf16[8,2,2048,16]{2,3,1,0:T(8,128)(2,1)}), bf16[8,2,2048,16]{2,3,1,0:T(8,128)(2,1)S(1)}, u32[]{:S(2)}, u32[]{:S(2)}) %all-to-all-start.1) | async-done | bytes 1048608 | tf_op jit(solution)/shard_map/all_to_all | solution.py:37
  64.7 0.6 gather_fusion.1
  65.2 0.7 convolution_bitcast_fusion
  65.9 21.0 %psum.7 = f32[4,128,16]{1,2,0:T(8,128)S(1)} all-reduce(f32[4,128,16]{1,2,0:T(8,128)S(1)} %convolution_bitcast_fusion), channel_id=1, replica_groups=mesh['grp'=8,'tp'=4] {'tp'}, use_global_device_ids=true, to_apply=%region_3.4 | all-reduce | flops 8192 | bytes 65536 | tf_op jit(solution)/shard_map/psum | solution.py:43
  86.9 0.6 convolution_multiply_fusion
  87.6 10.7 %reduce-scatter.2.cloned.1.call-done = f32[512,512]{1,0:T(8,128)} async-done(((f32[512,2048]{1,0:T(8,128)}), f32[512,512]{1,0:T(8,128)}) %reduce-scatter.2.cloned.1.call-update) | async-done | bytes 1048592 | tf_op jit(solution)/shard_map/reduce_scatter | solution.py:33
  98.2 2.2 %fusion.1 = bf16[512,512]{1,0:T(8,128)(2,1)} fusion(f32[512,512]{1,0:T(8,128)} %reduce-scatter.2.cloned.1.call-done, f32[4,128,512]{2,1,0:T(8,128)S(1)} %convolution_multiply_fusion, pred[512]{0:T(512)(128)(4,1)S(1)} %fusion.8), kind=kLoop, calls=%fused_computation.8 | loop fusion | flops 786432 | bytes 2621952 | tf_op jit(solution)/shard_map/convert_element_type | solution.py:52
  (6 shorter events, 0.0 us)
Async XLA Ops:
  6.5 1.6 %copy-start = (bf16[512,2048]{1,0:T(8,128)(2,1)S(1)}, bf16[512,2048]{1,0:T(8,128)(2,1)}, u32[]{:S(2)}) copy-start(bf16[512,2048]{1,0:T(8,128)(2,1)} %param.7) | copy-start | bytes 6291460
  6.5 91.7 %reduce-scatter.2.cloned.1.call-start = ((), (), s32[]{:S(2)}) async-start(), calls=%async_computation.4 | async-start | bytes 5242880 | tf_op jit(solution)/shard_map/reduce_scatter | solution.py:33
  17.5 0.7 copy-start.1
  17.5 0.8 copy-start.2
  35.5 10.3 %all-to-all-start.2 = ((bf16[8,2,16,512]{3,2,1,0:T(8,128)(2,1)}), bf16[8,2,16,512]{3,2,1,0:T(8,128)(2,1)S(1)}, u32[]{:S(2)}, u32[]{:S(2)}) async-start(bf16[8,2,16,512]{3,2,1,0:T(8,128)(2,1)} %broadcast_select_fusion.1), calls=%async_computation.3 | async-start | bytes 524288 | tf_op jit(solution)/shard_map/all_to_all | solution.py:38
  38.9 10.4 %copy-start.3 = (s32[4]{0:T(128)S(1)}, s32[4]{0:T(128)}, u32[]{:S(2)}) copy-start(s32[4]{0:T(128)} %param.13) | copy-start | bytes 52
  45.7 18.9 %all-to-all-start.1 = ((bf16[8,2,2048,16]{2,3,1,0:T(8,128)(2,1)}), bf16[8,2,2048,16]{2,3,1,0:T(8,128)(2,1)S(1)}, u32[]{:S(2)}, u32[]{:S(2)}) async-start(bf16[8,2,2048,16]{2,3,1,0:T(8,128)(2,1)} %broadcast_select_fusion), calls=%async_computation.2 | async-start | bytes 2097152 | tf_op jit(solution)/shard_map/all_to_all | solution.py:37
Sparse Core Ops, SparseCore 0:
  17.6 80.5 reduce-scatter.1
where the time goes:
time: 108 us; the launch traced here: 107 us
  waiting for transfers between devices  31 us (29%)
  blocking collectives  30.6 us (28%)
  between operations  13.5 us (12%)
  matrix products  10.7 us (10%)
  local copies, waits for them, and re-layouts  9.92 us (9%)
  starting transfers between devices  6.97 us (6%)
  other arithmetic  4.55 us (4%)
    psum x1, blocking collectives, body(): reduced = lax.psum(reduced, 'tp')  21 us
    all_to_all x1, waiting for transfers between devices, body(): lax.all_to_all(down_sel, 'grp', split_axis=0, concat_axis=0, tiled=True)  14.7 us
    reduce_scatter x1, waiting for transfers between devices, body(): lax.psum_scatter(partial_value, 'tp', scatter_dimension=1, tiled=True)  10.7 us
    all_to_all x1, blocking collectives, body(): lax.all_to_all(wanted_ids, 'grp', split_axis=0, concat_axis=0, tiled=True)  9.62 us
    dot_general x1, matrix products, body(): jnp.dot(tokens, base_weight, preferred_element_type=jnp.float32)  9.36 us
    all_to_all x1, waiting for transfers between devices, body(): lax.all_to_all(up_sel, 'grp', split_axis=0, concat_axis=0, tiled=True)  5.68 us
    gather x1, local copies, waits for them, and re-layouts, body(): down_sel = jnp.take(down_tables, local_ids, axis=0)  4 us
    all_to_all x1, starting transfers between devices, body(): lax.all_to_all(down_sel, 'grp', split_axis=0, concat_axis=0, tiled=True)  3.56 us
  transfers between devices with their start and end apart: 3, of which 3 were waited for; matrix products, arithmetic and copies ran while one was open for 11% of the time, Pallas kernels for 0%

commit v1 on v0

v1 whole, which is shorter than its diff:
```python
import functools

import jax
import jax.numpy as jnp
from jax import lax
from jax.experimental import pallas as pl
from jax.experimental.pallas import tpu as pltpu
from jax.sharding import PartitionSpec as P

BLOCK = 128
CAP = 2
adapter_scale = 2.0
SEND_SCALE = 16.0
HBM = pl.BlockSpec(memory_space=pl.ANY)


def pack_kernel(group_count, ids_ref, me_ref, down_ref, up_ref, *rest):
    outs, sems = rest[:group_count], rest[group_count]
    local_total, _, cols = down_ref.shape
    blocks = ids_ref.shape[1]
    low = me_ref[0] * local_total
    copies = []
    for j in range(group_count):
        slots, seen = [jnp.int32(0)] * CAP, jnp.int32(0)
        for b in range(blocks):
            local = ids_ref[j, b] - low
            mine = (local >= 0) & (local < local_total)
            slots = [jnp.where(mine & (seen == r), local, s) for r, s in enumerate(slots)]
            seen = seen + mine.astype(jnp.int32)
        for r, slot in enumerate(slots):
            copies += [
                pltpu.make_async_copy(down_ref.at[slot], outs[j].at[r, :, pl.ds(0, cols)], sems.at[0, j, r]),
                pltpu.make_async_copy(up_ref.at[slot], outs[j].at[r, :, pl.ds(cols, up_ref.shape[2])], sems.at[1, j, r]),
            ]
            copies[-2].start()
            copies[-1].start()
    for copy in copies:
        copy.wait()


def reduce_kernel(group_count, owner_ref, me_ref, tokens_ref, *rest):
    got, (reduced_ref, up_ref, held, sems) = rest[:group_count], rest[group_count:]
    blocks, rank, cols = held.shape[0], held.shape[1], tokens_ref.shape[1]
    for b in range(blocks):
        earlier = jnp.int32(0)
        for a in range(b):
            earlier = earlier + (owner_ref[a] == owner_ref[b]).astype(jnp.int32)
        away = owner_ref[b] ^ me_ref[0]
        for j in range(group_count):

            @pl.when(away == j)
            def _():
                pltpu.make_async_copy(got[j].at[earlier], held.at[b], sems.at[b]).start()

    for b in range(blocks):
        pltpu.make_async_copy(got[0].at[0], held.at[b], sems.at[b]).wait()
        reduced_ref[b] = lax.dot_general(
            held[b, :, :cols],
            tokens_ref[b * BLOCK : (b + 1) * BLOCK, :],
            (((1,), (1,)), ((), ())),
            preferred_element_type=jnp.float32,
        )
        up_ref[b] = held[b, :, cols:]


def adapter_part(tokens, down_tables, up_tables, block_owner, block_local):
    group_count, tp_count = lax.axis_size("grp"), lax.axis_size("tp")
    me = lax.axis_index("grp").astype(jnp.int32).reshape(1)
    owners = block_owner[:, 0]
    blocks = owners.shape[0]
    local_total, cols, rank = down_tables.shape
    out_cols = up_tables.shape[2]
    down_rows = jnp.transpose(down_tables, (0, 2, 1))
    ids = (owners * local_total + block_local).reshape(1, blocks)
    step = 1
    while step < group_count:
        there = lax.ppermute(ids, "grp", [(i, i ^ step) for i in range(group_count)])
        ids = jnp.concatenate([ids, there], axis=0)
        step *= 2
    wide = cols + out_cols
    packed = pl.pallas_call(
        functools.partial(pack_kernel, group_count),
        out_shape=[jax.ShapeDtypeStruct((CAP, rank, wide), jnp.bfloat16)] * group_count,
        grid_spec=pltpu.PrefetchScalarGridSpec(
            num_scalar_prefetch=2,
            in_specs=[HBM, HBM],
            out_specs=[HBM] * group_count,
            scratch_shapes=[pltpu.SemaphoreType.DMA((2, group_count, CAP))],
        ),
    )(ids, me, down_rows, up_tables)
    got = [packed[0]] + [
        lax.ppermute(packed[j], "grp", [(i, i ^ j) for i in range(group_count)]) for j in range(1, group_count)
    ]
    reduced, up_block = pl.pallas_call(
        functools.partial(reduce_kernel, group_count),
        out_shape=[
            jax.ShapeDtypeStruct((blocks, rank, BLOCK), jnp.float32),
            jax.ShapeDtypeStruct((blocks, rank, out_cols), jnp.bfloat16),
        ],
        grid_spec=pltpu.PrefetchScalarGridSpec(
            num_scalar_prefetch=2,
            in_specs=[pl.BlockSpec(memory_space=pltpu.VMEM)] + [HBM] * group_count,
            out_specs=[pl.BlockSpec(memory_space=pltpu.VMEM)] * 2,
            scratch_shapes=[
                pltpu.VMEM((blocks, rank, wide), jnp.bfloat16),
                pltpu.SemaphoreType.DMA((blocks,)),
            ],
        ),
    )(owners, me, tokens, *got)
    total = reduced
    for j in range(1, tp_count):
        total = total + lax.ppermute(reduced, "tp", [(i, i ^ j) for i in range(tp_count)])
    lowrank = jnp.einsum(
        "nrb,nro->nbo", total, up_block.astype(jnp.float32), precision=lax.Precision.HIGHEST
    )
    return lowrank.reshape(blocks * BLOCK, out_cols)


def base_part(tokens, base_weight):
    tp_count = lax.axis_size("tp")
    if tp_count != 4:
        partial_value = jnp.dot(tokens, base_weight, preferred_element_type=jnp.float32)
        return lax.psum_scatter(partial_value, "tp", scatter_dimension=1, tiled=True)
    z = lax.axis_index("tp")
    width = base_weight.shape[1] // tp_count

    def product(block):
        columns = lax.dynamic_slice_in_dim(base_weight, block * width, width, 1)
        return jnp.dot(tokens, columns, preferred_element_type=jnp.float32)

    def code(value):
        return (value * SEND_SCALE).astype(jnp.float16)

    def plain(value):
        return value.astype(jnp.float32) * (1.0 / SEND_SCALE)

    far = code(product(z ^ 3))
    to_inner = lax.ppermute(far, "tp", [(0, 1), (3, 2)])
    from_inner = lax.ppermute(far, "tp", [(1, 2), (2, 1)])
    near = lax.ppermute(code(product(z ^ 1)), "tp", [(0, 1), (1, 0), (2, 3), (3, 2)])
    middle = code(product(z ^ 2) + plain(to_inner))
    middle = lax.ppermute(middle, "tp", [(0, 2), (2, 0), (1, 3), (3, 1)])
    return product(z) + (plain(from_inner) + plain(near) + plain(middle))


def body(tokens, base_weight, down_tables, up_tables, block_owner, block_local, block_count):
    base_projection = base_part(tokens, base_weight)
    lowrank = adapter_part(tokens, down_tables, up_tables, block_owner, block_local)
    offsets = jnp.arange(BLOCK, dtype=jnp.int32)
    live_rows = (offsets[None, :] < block_count[:, None]).reshape(tokens.shape[0], 1)
    combined_output = base_projection + adapter_scale * lowrank
    return jnp.where(live_rows, combined_output, jnp.float32(0.0)).astype(jnp.bfloat16)


def solution(mesh):
    placed = (
        P("grp", "tp"),
        P("tp", None),
        P("grp", "tp", None),
        P("grp", None, "tp"),
        P("grp", None),
        P("grp"),
        P("grp"),
    )
    return jax.shard_map(body, mesh=mesh, in_specs=placed, out_specs=P("grp", "tp"), check_vma=False)
```

time: 108 us -> 129 us (1.19)
  Pallas kernels: 0 us -> 47.3 us
  blocking collectives: 30.6 us -> 0 us
  starting transfers between devices: 6.97 us -> 23.2 us
  between operations: 13.5 us -> 0.16 us
  local copies, waits for them, and re-layouts: 9.92 us -> 2.05 us
  waiting for transfers between devices: 31 us -> 37.5 us
  matrix products: 10.7 us -> 15.4 us
  other arithmetic: 4.55 us -> 3.15 us
    pallas_call x0 -> x2, Pallas kernels: none -> 47.3 us  [the longest x1 42 us: adapter_part(): pl.pallas_call(functools.partial(pack_kernel, group_count), out_shape=[ja...]
    ppermute x0 -> x17, waiting for transfers between devices: none -> 37.5 us  [the longest x3 20.4 us: adapter_part(): lax.ppermute(reduced, 'tp', [(i, i ^ j) for i in range(tp_count)])]
    ppermute x0 -> x17, starting transfers between devices: none -> 23.2 us  [the longest x7 6.45 us: adapter_part(): lax.ppermute(packed[j], 'grp', [(i, i ^ j) for i in range(group_count)])]
    psum x1 -> x0, blocking collectives: 21 us -> none  [body(): reduced = lax.psum(reduced, 'tp')]
    all_to_all x2 -> x0, waiting for transfers between devices: 20.4 us -> none  [the longest x1 14.7 us: body(): lax.all_to_all(down_sel, 'grp', split_axis=0, concat_axis=0, tiled=True)]
    reduce_scatter x1 -> x0, waiting for transfers between devices: 10.7 us -> none  [body(): lax.psum_scatter(partial_value, 'tp', scatter_dimension=1, tiled=True)]
    all_to_all x1 -> x0, blocking collectives: 9.62 us -> none  [body(): lax.all_to_all(wanted_ids, 'grp', split_axis=0, concat_axis=0, tiled=True)]
    gather x4 -> x0, local copies, waits for them, and re-layouts: 7.27 us -> none  [the longest x1 4 us: body(): down_sel = jnp.take(down_tables, local_ids, axis=0)]
  transfers between devices with their start and end apart: 3 -> 17, of which waited for: 3 -> 6; matrix products, arithmetic and copies ran while one was open for 11% -> 13% of each run, Pallas kernels for 0% -> 37%
where the time goes in v1:
time: 129 us
  Pallas kernels  47.3 us (37%)
  waiting for transfers between devices  37.5 us (29%)
  starting transfers between devices  23.2 us (18%)
  matrix products  15.4 us (12%)
  other arithmetic  3.15 us (2%)
  local copies, waits for them, and re-layouts  2.05 us (2%)
    pallas_call x1, Pallas kernels, adapter_part(): pl.pallas_call(functools.partial(pack_kernel, group_count), out_shape=[ja...  42 us
    ppermute x3, waiting for transfers between devices, adapter_part(): lax.ppermute(reduced, 'tp', [(i, i ^ j) for i in range(tp_count)])  20.4 us
    dot_general x4, matrix products, product(): return jnp.dot(tokens, columns, preferred_element_type=jnp.float32)  14.7 us
    ppermute x7, waiting for transfers between devices, adapter_part(): lax.ppermute(packed[j], 'grp', [(i, i ^ j) for i in range(group_count)])  12.9 us
    ppermute x7, starting transfers between devices, adapter_part(): lax.ppermute(packed[j], 'grp', [(i, i ^ j) for i in range(group_count)])  6.45 us
    pallas_call x1, Pallas kernels, adapter_part(): pl.pallas_call(functools.partial(reduce_kernel, group_count), out_shape=[...  5.34 us
    ppermute x1, starting transfers between devices, base_part(): to_inner = lax.ppermute(far, 'tp', [(0, 1), (3, 2)])  5.3 us
    ppermute x3, waiting for transfers between devices, adapter_part(): lax.ppermute(ids, 'grp', [(i, i ^ step) for i in range(group_count)])  4.14 us
  transfers between devices with their start and end apart: 17, of which 6 were waited for; matrix products, arithmetic and copies ran while one was open for 13% of the time, Pallas kernels for 37%

profile of v1, /device:TPU:0, one launch (start us, length us, event | category | flops | bytes accessed | tf_op | source)
XLA Modules:
  0.0 128.7 jit_solution(17793077498655771191)
XLA Ops:
  0.0 0.7 add_bitcast_fusion
  0.7 0.5 collective-permute-start.4
  1.1 4.3 %fusion.26 = f16[512,512]{0,1:T(8,128)(2,1)} fusion(bf16[512,2048]{1,0:T(8,128)(2,1)} %tokens_ref.1, bf16[2048,2048]{1,0:T(8,128)(2,1)} %param.8, s32[]{:T(128)S(6)} %select_n.17), kind=kOutput, calls=%fused_computation.15 | convolution fusion | flops 1074266112 | bytes 4718596 | tf_op jit(solution)/shard_map/dot_general | solution.py:129
  5.5 5.3 %collective-permute-start.2 = (f16[512,512]{0,1:T(8,128)(2,1)}, f16[512,512]{0,1:T(8,128)(2,1)}, u32[]{:S(2)}, u32[]{:S(2)}) collective-permute-start(f16[512,512]{0,1:T(8,128)(2,1)} %fusion.26), channel_id=1, source_target_pairs={{0,1},{3,2},{4,5},{7,6},{8,9},{11,10},{12,13},{15,14},{16,17},{19,... | collective-permute-start | bytes 1572872 | tf_op jit(solution)/shard_map/ppermute | solution.py:138
  10.8 0.0 collective-permute-done.4
  10.8 1.6 %collective-permute-start.5 = (s32[2,4]{1,0:T(2,128)S(1)}, s32[2,4]{1,0:T(2,128)S(1)}, u32[]{:S(2)}, u32[]{:S(2)}) collective-permute-start(s32[2,4]{1,0:T(2,128)S(1)} %pad_add_fusion.2), channel_id=1, source_target_pairs={{0,8},{4,12},{8,0},{12,4},{16,24},{20,28},{24,16},{28,20},{1,9},{5... | collective-permute-start | bytes 104 | tf_op jit(solution)/shard_map/ppermute | solution.py:77
  12.3 2.1 %collective-permute-done.5 = s32[2,4]{1,0:T(2,128)S(1)} collective-permute-done((s32[2,4]{1,0:T(2,128)S(1)}, s32[2,4]{1,0:T(2,128)S(1)}, u32[]{:S(2)}, u32[]{:S(2)}) %collective-permute-start.5) | collective-permute-done | bytes 64 | tf_op jit(solution)/shard_map/ppermute | solution.py:77
  14.4 1.6 %collective-permute-start.6 = (s32[4,4]{1,0:T(4,128)S(1)}, s32[4,4]{1,0:T(4,128)S(1)}, u32[]{:S(2)}, u32[]{:S(2)}) collective-permute-start(s32[4,4]{1,0:T(4,128)S(1)} %pad_add_fusion.1), channel_id=1, source_target_pairs={{0,16},{4,20},{8,24},{12,28},{16,0},{20,4},{24,8},{28,12},{1,17},{... | collective-permute-start | bytes 200 | tf_op jit(solution)/shard_map/ppermute | solution.py:77
  16.0 2.1 %collective-permute-done.6 = s32[4,4]{1,0:T(4,128)S(1)} collective-permute-done((s32[4,4]{1,0:T(4,128)S(1)}, s32[4,4]{1,0:T(4,128)S(1)}, u32[]{:S(2)}, u32[]{:S(2)}) %collective-permute-start.6) | collective-permute-done | bytes 96 | tf_op jit(solution)/shard_map/ppermute | solution.py:77
  18.1 0.6 pad_add_fusion.ids_ref
  18.6 0.0 copy-start
  18.7 42.0 %shard_map.73 = (bf16[2,16,2560]{2,1,0:T(8,128)(2,1)}, bf16[2,16,2560]{2,1,0:T(8,128)(2,1)}, bf16[2,16,2560]{2,1,0:T(8,128)(2,1)}, bf16[2,16,2560]{2,1,0:T(8,128...) custom-call(s32[8,4]{1,0:T(8,128)} %pad_add_fusion.ids_ref, ...), custom_call_target="tpu_custom_call" | custom-call | tf_op jit(solution)/shard_map/pallas_call | solution.py:81
  60.6 1.6 %collective-permute-start.10 = (bf16[2,16,2560]{2,1,0:T(8,128)(2,1)}, bf16[2,16,2560]{2,1,0:T(8,128)(2,1)S(1)}, u32[]{:S(2)}, u32[]{:S(2)}) collective-permute-start(bf16[2,16,2560]{2,1,0:T(8,128)(2,1)} %get-tuple-element.19), channel_id=1, source_target_pairs={{0,16},{4,20},{8,24},{12,28},{16,0},{20,4},{24,8},{28,12},{1,17},{... | collective-permute-start | bytes 491528 | tf_op jit(solution)/shard_map/ppermute | solution.py:92
  62.2 0.0 collective-permute-start.11
  62.2 1.4 %collective-permute-start.12 = (bf16[2,16,2560]{2,1,0:T(8,128)(2,1)}, bf16[2,16,2560]{2,1,0:T(8,128)(2,1)S(1)}, u32[]{:S(2)}, u32[]{:S(2)}) collective-permute-start(bf16[2,16,2560]{2,1,0:T(8,128)(2,1)} %get-tuple-element.21), channel_id=1, source_target_pairs={{0,24},{4,28},{8,16},{12,20},{16,8},{20,12},{24,0},{28,4},{1,25},{... | collective-permute-start | bytes 491528 | tf_op jit(solution)/shard_map/ppermute | solution.py:92
  63.6 1.4 %collective-permute-start.13 = (bf16[2,16,2560]{2,1,0:T(8,128)(2,1)}, bf16[2,16,2560]{2,1,0:T(8,128)(2,1)S(1)}, u32[]{:S(2)}, u32[]{:S(2)}) collective-permute-start(bf16[2,16,2560]{2,1,0:T(8,128)(2,1)} %get-tuple-element.22), channel_id=1, source_target_pairs={{0,28},{4,24},{8,20},{12,16},{16,12},{20,8},{24,4},{28,0},{1,29},{... | collective-permute-start | bytes 491528 | tf_op jit(solution)/shard_map/ppermute | solution.py:92
  65.1 9.0 %collective-permute-done.10.rest_4_ = bf16[2,16,2560]{2,1,0:T(8,128)(2,1)S(1)} collective-permute-done((bf16[2,16,2560]{2,1,0:T(8,128)(2,1)}, bf16[2,16,2560]{2,1,0:T(8,128)(2,1)S(1)}, u32[]{:S(2)}, u32[]{:S(2)}) %collective-permute-start.10) | collective-permute-done | bytes 163872 | tf_op jit(solution)/shard_map/ppermute | solution.py:92
  74.1 0.0 copy-start.2
  74.1 0.0 collective-permute-start.7
  74.1 1.9 %collective-permute-done.11.rest_5_ = bf16[2,16,2560]{2,1,0:T(8,128)(2,1)S(1)} collective-permute-done((bf16[2,16,2560]{2,1,0:T(8,128)(2,1)}, bf16[2,16,2560]{2,1,0:T(8,128)(2,1)S(1)}, u32[]{:S(2)}, u32[]{:S(2)}) %collective-permute-start.11) | collective-permute-done | bytes 163872 | tf_op jit(solution)/shard_map/ppermute | solution.py:92
  75.9 0.0 copy-start.3
  75.9 1.5 %collective-permute-start.8 = (bf16[2,16,2560]{2,1,0:T(8,128)(2,1)}, bf16[2,16,2560]{2,1,0:T(8,128)(2,1)S(1)}, u32[]{:S(2)}, u32[]{:S(2)}) collective-permute-start(bf16[2,16,2560]{2,1,0:T(8,128)(2,1)} %get-tuple-element.17), channel_id=1, source_target_pairs={{0,8},{4,12},{8,0},{12,4},{16,24},{20,28},{24,16},{28,20},{1,9},{5... | collective-permute-start | bytes 491528 | tf_op jit(solution)/shard_map/ppermute | solution.py:92
  77.4 0.0 collective-permute-done.12.rest_6_
  77.4 0.5 collective-permute-start.9
  77.9 0.0 copy-done
  77.9 3.7 %fusion.29 = f16[512,512]{0,1:T(8,128)(2,1)} fusion(bf16[512,2048]{1,0:T(8,128)(2,1)S(1)} %copy-done, bf16[2048,2048]{1,0:T(8,128)(2,1)} %param.8, s32[]{:T(128)S(6)} %select_n.18), kind=kOutput, calls=%fused_computation.16 | convolution fusion | flops 1074266112 | bytes 4718596 | tf_op jit(solution)/shard_map/dot_general | solution.py:129
  81.6 0.0 copy-done.2
  81.6 0.0 copy-done.3
  81.6 0.0 copy-done.4
  81.6 0.0 copy-start.1
  81.7 0.0 collective-permute-done.13.rest_7_
  81.7 0.0 copy-start.5
  81.7 1.6 %collective-permute-start = (f16[512,512]{0,1:T(8,128)(2,1)}, f16[512,512]{0,1:T(8,128)(2,1)}, u32[]{:S(2)}, u32[]{:S(2)}) collective-permute-start(f16[512,512]{0,1:T(8,128)(2,1)} %fusion.26), channel_id=1, source_target_pairs={{1,2},{2,1},{5,6},{6,5},{9,10},{10,9},{13,14},{14,13},{17,18},{18,... | collective-permute-start | bytes 1572872 | tf_op jit(solution)/shard_map/ppermute | solution.py:139
  83.3 0.0 collective-permute-done.7.rest_1_
  83.3 0.7 collective-permute-start.1
  84.0 0.0 collective-permute-done.8.rest_2_
  84.0 2.1 %collective-permute-done.9.rest_3_ = bf16[2,16,2560]{2,1,0:T(8,128)(2,1)S(1)} collective-permute-done((bf16[2,16,2560]{2,1,0:T(8,128)(2,1)}, bf16[2,16,2560]{2,1,0:T(8,128)(2,1)S(1)}, u32[]{:S(2)}, u32[]{:S(2)}) %collective-permute-start.9) | collective-permute-done | bytes 163872 | tf_op jit(solution)/shard_map/ppermute | solution.py:92
  86.1 0.0 copy-done.5
  86.1 0.0 copy-done.6
  86.1 0.0 copy-done.7
  86.1 0.7 copy-done.8
  86.7 5.3 %shard_map.74 = (f32[4,16,128]{2,1,0:T(8,128)}, bf16[4,16,512]{2,1,0:T(8,128)(2,1)}) custom-call(s32[4]{0:T(128)} %bitcast.26, s32[1]{0:T(128)} %bitcast.6.me_ref, bf16[512,2048]{1,0:T(8,128)(2,1)} %tokens_ref.1, bf16[2,16,2560]{2,1,0:T(8,128)(2,1)} %get-tuple-element.15.rest_0_, bf16[2,16,2560]{2,1,0:T(8,128)(2,1)} %copy-done.6, ...), custom_call_target="tpu_custom_call" | custom-call | tf_op jit(solution)/shard_map/pallas_call | solution.py:94
  92.1 0.1 collective-permute-start.14
  92.2 0.0 collective-permute-done.2
  92.2 0.0 copy-done.1
  92.2 3.8 %multiply_convert_fusion = f16[512,512]{0,1:T(8,128)(2,1)} fusion(f16[512,512]{0,1:T(8,128)(2,1)} %collective-permute-done.2, bf16[512,2048]{1,0:T(8,128)(2,1)S(1)} %copy-done.1, bf16[2048,2048]{1,0:T(8,128)(2,1)} %param.8, s32[]{:T(128)S(6)} %select_n.19), kind=kOutput, calls=%fused_computation.18 | convolution fusion | flops 1075052544 | bytes 5242884 | tf_op jit(solution)/shard_map/dot_general | solution.py:129
  96.0 3.0 %collective-permute-start.3 = (f16[512,512]{0,1:T(8,128)(2,1)}, f16[512,512]{0,1:T(8,128)(2,1)}, u32[]{:S(2)}, u32[]{:S(2)}) collective-permute-start(f16[512,512]{0,1:T(8,128)(2,1)} %multiply_convert_fusion), channel_id=1, source_target_pairs={{0,2},{2,0},{1,3},{3,1},{4,6},{6,4},{5,7},{7,5},{8,10},{10,8},{9,1... | collective-permute-start | bytes 1572872 | tf_op jit(solution)/shard_map/ppermute | solution.py:142
  99.0 2.9 %fusion.8 = f32[512,512]{0,1:T(8,128)S(1)} fusion(bf16[512,2048]{1,0:T(8,128)(2,1)S(1)} %copy-done.1, bf16[2048,2048]{1,0:T(8,128)(2,1)} %param.8, s32[]{:T(128)S(6)} %select_n.16), kind=kOutput, calls=%fused_computation.8 | convolution fusion | flops 1073741824 | bytes 5242884 | tf_op jit(solution)/shard_map/dot_general | solution.py:129
  101.9 0.0 copy-done.10
  101.9 0.1 collective-permute-start.15
  102.0 0.0 collective-permute-done.14
  102.1 2.3 %collective-permute-start.16 = (f32[4,16,128]{2,1,0:T(8,128)S(1)}, f32[4,16,128]{2,1,0:T(8,128)S(1)}, u32[]{:S(2)}, u32[]{:S(2)}) collective-permute-start(f32[4,16,128]{2,1,0:T(8,128)S(1)} %copy-done.10), channel_id=1, source_target_pairs={{0,3},{1,2},{2,1},{3,0},{4,7},{5,6},{6,5},{7,4},{8,11},{9,10},{10,... | collective-permute-start | bytes 98312 | tf_op jit(solution)/shard_map/ppermute | solution.py:112
  104.4 0.0 copy-done.11
  104.4 0.1 fusion.35
  104.5 20.4 %collective-permute-done.15 = f32[4,16,128]{2,1,0:T(8,128)S(1)} collective-permute-done((f32[4,16,128]{2,1,0:T(8,128)S(1)}, f32[4,16,128]{2,1,0:T(8,128)S(1)}, u32[]{:S(2)}, u32[]{:S(2)}) %collective-permute-start.15) | collective-permute-done | bytes 32800 | tf_op jit(solution)/shard_map/ppermute | solution.py:112
  124.9 0.0 collective-permute-done.16
  124.9 0.0 copy-done.9
  124.9 0.6 convolution_multiply_fusion
  125.5 0.3 copy.11
  125.9 0.0 collective-permute-done
  125.9 0.0 collective-permute-done.1
  125.9 0.0 collective-permute-done.3
  125.9 1.8 %select_convert_fusion = bf16[512,512]{0,1:T(8,128)(2,1)S(1)} fusion(f32[512,512]{0,1:T(8,128)S(1)} %copy.11, f32[512,512]{0,1:T(8,128)S(1)} %fusion.8, f16[512,512]{0,1:T(8,128)(2,1)} %collective-permute-done.3, f16[512,512]{0,1:T(8,128)(2,1)} %collective-permute-done.1, f16[512,512]{0,1:T(8,128)(2,1)} %collective-permute-done, pred[512]{0:T(512)(128)(4,1)S(1)} %fusion.35), kind=kLoop, calls=%fused_computation.17 | loop fusion | flops 2621440 | bytes 4194816 | tf_op jit(solution)/shard_map/convert_element_type | solution.py:152
  127.7 1.0 copy.10
  (9 shorter events, 0.0 us)
Async XLA Ops:
  0.7 10.1 %collective-permute-start.4 = (s32[1,4]{1,0:T(1,128)S(1)}, s32[1,4]{1,0:T(1,128)S(1)}, u32[]{:S(2)}, u32[]{:S(2)}) collective-permute-start(s32[1,4]{1,0:T(1,128)S(1)} %add_bitcast_fusion), channel_id=1, source_target_pairs={{0,4},{4,0},{8,12},{12,8},{16,20},{20,16},{24,28},{28,24},{1,5},{5... | collective-permute-start | bytes 56 | tf_op jit(solution)/shard_map/ppermute | solution.py:77
  5.5 86.7 %collective-permute-start.2 = (f16[512,512]{0,1:T(8,128)(2,1)}, f16[512,512]{0,1:T(8,128)(2,1)}, u32[]{:S(2)}, u32[]{:S(2)}) collective-permute-start(f16[512,512]{0,1:T(8,128)(2,1)} %fusion.26), channel_id=1, source_target_pairs={{0,1},{3,2},{4,5},{7,6},{8,9},{11,10},{12,13},{15,14},{16,17},{19,... | collective-permute-start | bytes 1572872 | tf_op jit(solution)/shard_map/ppermute | solution.py:138
  10.8 3.6 %collective-permute-start.5 = (s32[2,4]{1,0:T(2,128)S(1)}, s32[2,4]{1,0:T(2,128)S(1)}, u32[]{:S(2)}, u32[]{:S(2)}) collective-permute-start(s32[2,4]{1,0:T(2,128)S(1)} %pad_add_fusion.2), channel_id=1, source_target_pairs={{0,8},{4,12},{8,0},{12,4},{16,24},{20,28},{24,16},{28,20},{1,9},{5... | collective-permute-start | bytes 104 | tf_op jit(solution)/shard_map/ppermute | solution.py:77
  14.4 3.7 %collective-permute-start.6 = (s32[4,4]{1,0:T(4,128)S(1)}, s32[4,4]{1,0:T(4,128)S(1)}, u32[]{:S(2)}, u32[]{:S(2)}) collective-permute-start(s32[4,4]{1,0:T(4,128)S(1)} %pad_add_fusion.1), channel_id=1, source_target_pairs={{0,16},{4,20},{8,24},{12,28},{16,0},{20,4},{24,8},{28,12},{1,17},{... | collective-permute-start | bytes 200 | tf_op jit(solution)/shard_map/ppermute | solution.py:77
  18.6 59.3 %copy-start = (bf16[512,2048]{1,0:T(8,128)(2,1)S(1)}, bf16[512,2048]{1,0:T(8,128)(2,1)}, u32[]{:S(2)}) copy-start(bf16[512,2048]{1,0:T(8,128)(2,1)} %tokens_ref.1) | copy-start | bytes 6291460
  60.6 13.4 %collective-permute-start.10 = (bf16[2,16,2560]{2,1,0:T(8,128)(2,1)}, bf16[2,16,2560]{2,1,0:T(8,128)(2,1)S(1)}, u32[]{:S(2)}, u32[]{:S(2)}) collective-permute-start(bf16[2,16,2560]{2,1,0:T(8,128)(2,1)} %get-tuple-element.19), channel_id=1, source_target_pairs={{0,16},{4,20},{8,24},{12,28},{16,0},{20,4},{24,8},{28,12},{1,17},{... | collective-permute-start | bytes 491528 | tf_op jit(solution)/shard_map/ppermute | solution.py:92
  62.2 13.7 %collective-permute-start.11 = (bf16[2,16,2560]{2,1,0:T(8,128)(2,1)}, bf16[2,16,2560]{2,1,0:T(8,128)(2,1)S(1)}, u32[]{:S(2)}, u32[]{:S(2)}) collective-permute-start(bf16[2,16,2560]{2,1,0:T(8,128)(2,1)} %get-tuple-element.20), channel_id=1, source_target_pairs={{0,20},{4,16},{8,28},{12,24},{16,4},{20,0},{24,12},{28,8},{1,21},{... | collective-permute-start | bytes 491528 | tf_op jit(solution)/shard_map/ppermute | solution.py:92
  62.2 15.2 %collective-permute-start.12 = (bf16[2,16,2560]{2,1,0:T(8,128)(2,1)}, bf16[2,16,2560]{2,1,0:T(8,128)(2,1)S(1)}, u32[]{:S(2)}, u32[]{:S(2)}) collective-permute-start(bf16[2,16,2560]{2,1,0:T(8,128)(2,1)} %get-tuple-element.21), channel_id=1, source_target_pairs={{0,24},{4,28},{8,16},{12,20},{16,8},{20,12},{24,0},{28,4},{1,25},{... | collective-permute-start | bytes 491528 | tf_op jit(solution)/shard_map/ppermute | solution.py:92
  63.6 18.0 %collective-permute-start.13 = (bf16[2,16,2560]{2,1,0:T(8,128)(2,1)}, bf16[2,16,2560]{2,1,0:T(8,128)(2,1)S(1)}, u32[]{:S(2)}, u32[]{:S(2)}) collective-permute-start(bf16[2,16,2560]{2,1,0:T(8,128)(2,1)} %get-tuple-element.22), channel_id=1, source_target_pairs={{0,28},{4,24},{8,20},{12,16},{16,12},{20,8},{24,4},{28,0},{1,29},{... | collective-permute-start | bytes 491528 | tf_op jit(solution)/shard_map/ppermute | solution.py:92
  74.1 7.6 %copy-start.2 = (bf16[2,16,2560]{2,1,0:T(8,128)(2,1)}, bf16[2,16,2560]{2,1,0:T(8,128)(2,1)S(1)}, u32[]{:S(2)}) copy-start(bf16[2,16,2560]{2,1,0:T(8,128)(2,1)S(1)} %collective-permute-done.10.rest_4_) | copy-start | bytes 491524
  74.1 9.2 %collective-permute-start.7 = (bf16[2,16,2560]{2,1,0:T(8,128)(2,1)}, bf16[2,16,2560]{2,1,0:T(8,128)(2,1)S(1)}, u32[]{:S(2)}, u32[]{:S(2)}) collective-permute-start(bf16[2,16,2560]{2,1,0:T(8,128)(2,1)} %get-tuple-element.16), channel_id=1, source_target_pairs={{0,4},{4,0},{8,12},{12,8},{16,20},{20,16},{24,28},{28,24},{1,5},{5... | collective-permute-start | bytes 491528 | tf_op jit(solution)/shard_map/ppermute | solution.py:92
  75.9 5.7 %copy-start.3 = (bf16[2,16,2560]{2,1,0:T(8,128)(2,1)}, bf16[2,16,2560]{2,1,0:T(8,128)(2,1)S(1)}, u32[]{:S(2)}) copy-start(bf16[2,16,2560]{2,1,0:T(8,128)(2,1)S(1)} %collective-permute-done.11.rest_5_) | copy-start | bytes 491524
  75.9 8.0 %collective-permute-start.8 = (bf16[2,16,2560]{2,1,0:T(8,128)(2,1)}, bf16[2,16,2560]{2,1,0:T(8,128)(2,1)S(1)}, u32[]{:S(2)}, u32[]{:S(2)}) collective-permute-start(bf16[2,16,2560]{2,1,0:T(8,128)(2,1)} %get-tuple-element.17), channel_id=1, source_target_pairs={{0,8},{4,12},{8,0},{12,4},{16,24},{20,28},{24,16},{28,20},{1,9},{5... | collective-permute-start | bytes 491528 | tf_op jit(solution)/shard_map/ppermute | solution.py:92
  77.4 4.2 %copy-start.4 = (bf16[2,16,2560]{2,1,0:T(8,128)(2,1)}, bf16[2,16,2560]{2,1,0:T(8,128)(2,1)S(1)}, u32[]{:S(2)}) copy-start(bf16[2,16,2560]{2,1,0:T(8,128)(2,1)S(1)} %collective-permute-done.12.rest_6_) | copy-start | bytes 491524
  77.4 8.6 %collective-permute-start.9 = (bf16[2,16,2560]{2,1,0:T(8,128)(2,1)}, bf16[2,16,2560]{2,1,0:T(8,128)(2,1)S(1)}, u32[]{:S(2)}, u32[]{:S(2)}) collective-permute-start(bf16[2,16,2560]{2,1,0:T(8,128)(2,1)} %get-tuple-element.18), channel_id=1, source_target_pairs={{0,12},{4,8},{8,4},{12,0},{16,28},{20,24},{24,20},{28,16},{1,13},{... | collective-permute-start | bytes 491528 | tf_op jit(solution)/shard_map/ppermute | solution.py:92
  81.6 10.5 %copy-start.1 = (bf16[512,2048]{1,0:T(8,128)(2,1)S(1)}, bf16[512,2048]{1,0:T(8,128)(2,1)}, u32[]{:S(2)}) copy-start(bf16[512,2048]{1,0:T(8,128)(2,1)} %tokens_ref.1) | copy-start | bytes 6291460
  81.7 4.4 %copy-start.5 = (bf16[2,16,2560]{2,1,0:T(8,128)(2,1)}, bf16[2,16,2560]{2,1,0:T(8,128)(2,1)S(1)}, u32[]{:S(2)}) copy-start(bf16[2,16,2560]{2,1,0:T(8,128)(2,1)S(1)} %collective-permute-done.13.rest_7_) | copy-start | bytes 491524
  81.7 44.2 %collective-permute-start = (f16[512,512]{0,1:T(8,128)(2,1)}, f16[512,512]{0,1:T(8,128)(2,1)}, u32[]{:S(2)}, u32[]{:S(2)}) collective-permute-start(f16[512,512]{0,1:T(8,128)(2,1)} %fusion.26), channel_id=1, source_target_pairs={{1,2},{2,1},{5,6},{6,5},{9,10},{10,9},{13,14},{14,13},{17,18},{18,... | collective-permute-start | bytes 1572872 | tf_op jit(solution)/shard_map/ppermute | solution.py:139
  83.3 2.8 %copy-start.6 = (bf16[2,16,2560]{2,1,0:T(8,128)(2,1)}, bf16[2,16,2560]{2,1,0:T(8,128)(2,1)S(1)}, u32[]{:S(2)}) copy-start(bf16[2,16,2560]{2,1,0:T(8,128)(2,1)S(1)} %collective-permute-done.7.rest_1_) | copy-start | bytes 491524
  83.3 42.6 %collective-permute-start.1 = (f16[512,512]{0,1:T(8,128)(2,1)}, f16[512,512]{0,1:T(8,128)(2,1)}, u32[]{:S(2)}, u32[]{:S(2)}) collective-permute-start(f16[512,512]{0,1:T(8,128)(2,1)} %fusion.29), channel_id=1, source_target_pairs={{0,1},{1,0},{2,3},{3,2},{4,5},{5,4},{6,7},{7,6},{8,9},{9,8},{10,11... | collective-permute-start | bytes 1572872 | tf_op jit(solution)/shard_map/ppermute | solution.py:140
  84.0 2.1 %copy-start.7 = (bf16[2,16,2560]{2,1,0:T(8,128)(2,1)}, bf16[2,16,2560]{2,1,0:T(8,128)(2,1)S(1)}, u32[]{:S(2)}) copy-start(bf16[2,16,2560]{2,1,0:T(8,128)(2,1)S(1)} %collective-permute-done.8.rest_2_) | copy-start | bytes 491524
  86.1 0.7 copy-start.8
  92.1 10.0 %collective-permute-start.14 = (f32[4,16,128]{2,1,0:T(8,128)}, f32[4,16,128]{2,1,0:T(8,128)S(1)}, u32[]{:S(2)}, u32[]{:S(2)}) collective-permute-start(f32[4,16,128]{2,1,0:T(8,128)} %get-tuple-element.23), channel_id=1, source_target_pairs={{0,1},{1,0},{2,3},{3,2},{4,5},{5,4},{6,7},{7,6},{8,9},{9,8},{10,11... | collective-permute-start | bytes 98312 | tf_op jit(solution)/shard_map/ppermute | solution.py:112
  96.0 5.9 %copy-start.10 = (f32[4,16,128]{2,1,0:T(8,128)S(1)}, f32[4,16,128]{2,1,0:T(8,128)}, u32[]{:S(2)}) copy-start(f32[4,16,128]{2,1,0:T(8,128)} %get-tuple-element.23) | copy-start | bytes 98308
  96.0 8.4 %copy-start.11 = (s32[4]{0:T(128)S(1)}, s32[4]{0:T(128)}, u32[]{:S(2)}) copy-start(s32[4]{0:T(128)} %param.13) | copy-start | bytes 52
  96.0 28.9 %copy-start.9 = (bf16[4,16,512]{2,1,0:T(8,128)(2,1)S(1)}, bf16[4,16,512]{2,1,0:T(8,128)(2,1)}, u32[]{:S(2)}) copy-start(bf16[4,16,512]{2,1,0:T(8,128)(2,1)} %get-tuple-element.24) | copy-start | bytes 196612
  96.0 29.9 %collective-permute-start.3 = (f16[512,512]{0,1:T(8,128)(2,1)}, f16[512,512]{0,1:T(8,128)(2,1)}, u32[]{:S(2)}, u32[]{:S(2)}) collective-permute-start(f16[512,512]{0,1:T(8,128)(2,1)} %multiply_convert_fusion), channel_id=1, source_target_pairs={{0,2},{2,0},{1,3},{3,1},{4,6},{6,4},{5,7},{7,5},{8,10},{10,8},{9,1... | collective-permute-start | bytes 1572872 | tf_op jit(solution)/shard_map/ppermute | solution.py:142
  101.9 23.0 %collective-permute-start.15 = (f32[4,16,128]{2,1,0:T(8,128)S(1)}, f32[4,16,128]{2,1,0:T(8,128)S(1)}, u32[]{:S(2)}, u32[]{:S(2)}) collective-permute-start(f32[4,16,128]{2,1,0:T(8,128)S(1)} %copy-done.10), channel_id=1, source_target_pairs={{0,2},{1,3},{2,0},{3,1},{4,6},{5,7},{6,4},{7,5},{8,10},{9,11},{10,... | collective-permute-start | bytes 98312 | tf_op jit(solution)/shard_map/ppermute | solution.py:112
  102.1 22.8 %collective-permute-start.16 = (f32[4,16,128]{2,1,0:T(8,128)S(1)}, f32[4,16,128]{2,1,0:T(8,128)S(1)}, u32[]{:S(2)}, u32[]{:S(2)}) collective-permute-start(f32[4,16,128]{2,1,0:T(8,128)S(1)} %copy-done.10), channel_id=1, source_target_pairs={{0,3},{1,2},{2,1},{3,0},{4,7},{5,6},{6,5},{7,4},{8,11},{9,10},{10,... | collective-permute-start | bytes 98312 | tf_op jit(solution)/shard_map/ppermute | solution.py:112

commit v2 on v0

v2 whole, which is shorter than its diff:
```python
import functools

import jax
import jax.numpy as jnp
from jax import lax
from jax.experimental import pallas as pl
from jax.experimental.pallas import tpu as pltpu
from jax.experimental.layout import Layout, with_layout_constraint
from jax.sharding import PartitionSpec as P

BLOCK = 128
CAP = 2
adapter_scale = 2.0
SEND_SCALE = 16.0
HBM = pl.BlockSpec(memory_space=pl.ANY)


def pack_kernel(ids_ref, me_ref, down_ref, up_ref, out_ref, held, read_sems, write_sem):
    groups, blocks = ids_ref.shape
    local_total, _, cols = down_ref.shape
    low = me_ref[0] * local_total
    wanted = []
    for j in range(groups):
        slots, seen = [jnp.int32(0)] * CAP, jnp.int32(0)
        for b in range(blocks):
            local = ids_ref[j, b] - low
            mine = (local >= 0) & (local < local_total)
            slots = [jnp.where(mine & (seen == r), local, s) for r, s in enumerate(slots)]
            seen = seen + mine.astype(jnp.int32)
        for r, slot in enumerate(slots):
            k = j * CAP + r
            reads = [
                pltpu.make_async_copy(down_ref.at[slot], held.at[k, :, pl.ds(0, cols)], read_sems.at[k]),
                pltpu.make_async_copy(up_ref.at[slot], held.at[k, :, pl.ds(cols, up_ref.shape[2])], read_sems.at[k]),
            ]
            write = pltpu.make_async_copy(held.at[k], out_ref.at[me_ref[0] ^ j, r], write_sem)
            wanted.append((seen > r, reads, write))

            @pl.when(seen > r)
            def _():
                reads[0].start()
                reads[1].start()

    for there, reads, write in wanted:

        @pl.when(there)
        def _():
            reads[0].wait()
            reads[1].wait()
            write.start()

    for there, reads, write in wanted:

        @pl.when(there)
        def _():
            write.wait()


def later_kernel(value_ref, out_ref, sem):
    copy = pltpu.make_async_copy(value_ref, out_ref, sem)
    copy.start()
    copy.wait()


LONG = pl.CostEstimate(flops=100_000_000_000, bytes_accessed=1, transcendentals=0)
CHEAP = pl.CostEstimate(flops=1, bytes_accessed=1, transcendentals=0)


def adapter_ids(block_owner, block_local, local_total):
    group_count = lax.axis_size("grp")
    ids = (block_owner[:, 0] * local_total + block_local).reshape(1, block_owner.shape[0])
    step = 1
    while step < group_count:
        there = lax.ppermute(ids, "grp", [(i, i ^ step) for i in range(group_count)])
        ids = jnp.concatenate([ids, there], axis=0)
        yield ids
        step *= 2


def fetch_adapters(ids, down_tables, up_tables):
    group_count = lax.axis_size("grp")
    me = lax.axis_index("grp").astype(jnp.int32).reshape(1)
    _, cols, rank = down_tables.shape
    wide = cols + up_tables.shape[2]
    packed = pl.pallas_call(
        pack_kernel,
        out_shape=jax.ShapeDtypeStruct((group_count, CAP, rank, wide), jnp.bfloat16),
        grid_spec=pltpu.PrefetchScalarGridSpec(
            num_scalar_prefetch=2,
            in_specs=[HBM, HBM],
            out_specs=HBM,
            scratch_shapes=[
                pltpu.VMEM((group_count * CAP, rank, wide), jnp.bfloat16),
                pltpu.SemaphoreType.DMA((group_count * CAP,)),
                pltpu.SemaphoreType.DMA,
            ],
        ),
        cost_estimate=CHEAP,
    )(ids, me, jnp.transpose(down_tables, (0, 2, 1)), up_tables)
    got = lax.all_to_all(packed, "grp", split_axis=0, concat_axis=0, tiled=True)
    return got.reshape(group_count * CAP, rank, wide)


def later(value, *others):
    value = lax.optimization_barrier((value, *others))[0]
    return pl.pallas_call(
        later_kernel,
        out_shape=jax.ShapeDtypeStruct(value.shape, value.dtype),
        in_specs=[HBM],
        out_specs=HBM,
        scratch_shapes=[pltpu.SemaphoreType.DMA],
        cost_estimate=LONG,
    )(value)


def reduce_tokens(tokens, got, owners):
    blocks, cols = owners.shape[0], tokens.shape[1]
    order = jnp.arange(blocks, dtype=jnp.int32)
    earlier = (owners[None, :] == owners[:, None]) & (order[None, :] < order[:, None])
    block_slot = owners * CAP + jnp.sum(earlier.astype(jnp.int32), axis=1)
    mine = jnp.take(got, block_slot, axis=0, mode="clip")
    blocked = tokens.reshape(blocks, BLOCK, cols)
    reduced = jnp.einsum("nbd,nrd->nrb", blocked, mine[:, :, :cols], preferred_element_type=jnp.float32)
    return reduced, mine[:, :, cols:]


def body(tokens, base_weight, down_tables, up_tables, block_owner, block_local, block_count):
    tp_count = lax.axis_size("tp")
    z = lax.axis_index("tp")
    width = base_weight.shape[1] // tp_count
    owners = block_owner[:, 0]
    offsets = jnp.arange(BLOCK, dtype=jnp.int32)
    live_rows = (offsets[None, :] < block_count[:, None]).reshape(tokens.shape[0], 1)

    def product(block):
        columns = lax.dynamic_slice_in_dim(base_weight, block * width, width, 1)
        value = jnp.dot(tokens, columns, preferred_element_type=jnp.float32)
        return with_layout_constraint(value, Layout((0, 1)))

    def code(value):
        return (value * SEND_SCALE).astype(jnp.float16)

    def plain(value):
        return value.astype(jnp.float32) * (1.0 / SEND_SCALE)

    def after(value, *others):
        return lax.optimization_barrier((value, *others))[0]

    id_steps = list(adapter_ids(block_owner, block_local, down_tables.shape[0]))
    got = fetch_adapters(id_steps[-1], down_tables, up_tables)
    if tp_count == 4:
        far = code(product(z ^ 3))
        to_inner = lax.ppermute(far, "tp", [(0, 1), (3, 2)])
        from_inner = lax.ppermute(far, "tp", [(1, 2), (2, 1)])
        middle = product(after(z, id_steps[0]) ^ 2)
        middle, middle_code = lax.optimization_barrier((middle, code(middle)))
        from_middle = lax.ppermute(middle_code, "tp", [(0, 2), (3, 1)])
        near = code(product(after(z, id_steps[1]) ^ 1))
        from_near = lax.ppermute(near, "tp", [(0, 1), (1, 0), (2, 3), (3, 2)])
        inner_sum = code(middle + plain(to_inner))
        from_far = lax.ppermute(inner_sum, "tp", [(1, 3), (2, 0)])
        base_projection = lax.optimization_barrier(product(z) + plain(from_inner) + plain(from_middle))
        reduced, up_block = reduce_tokens(tokens, got, later(owners, base_projection))
        base_projection = lax.optimization_barrier(base_projection + (plain(from_near) + plain(from_far)))
    else:
        partial_value = jnp.dot(tokens, base_weight, preferred_element_type=jnp.float32)
        base_projection = lax.psum_scatter(partial_value, "tp", scatter_dimension=1, tiled=True)
        reduced, up_block = reduce_tokens(tokens, got, owners)
    total = reduced
    for j in range(1, tp_count):
        total = total + lax.ppermute(reduced, "tp", [(i, i ^ j) for i in range(tp_count)])
    lowrank = jnp.einsum(
        "nrb,nro->nbo", total, up_block.astype(jnp.float32), precision=lax.Precision.HIGHEST
    )
    combined_output = base_projection + adapter_scale * lowrank.reshape(base_projection.shape)
    return jnp.where(live_rows, combined_output, jnp.float32(0.0)).astype(jnp.bfloat16)


def solution(mesh):
    placed = (
        P("grp", "tp"),
        P("tp", None),
        P("grp", "tp", None),
        P("grp", None, "tp"),
        P("grp", None),
        P("grp"),
        P("grp"),
    )
    return jax.shard_map(body, mesh=mesh, in_specs=placed, out_specs=P("grp", "tp"), check_vma=False)
```

time: 108 us -> 66.9 us (0.62)
  blocking collectives: 30.6 us -> 0 us
  waiting for transfers between devices: 31 us -> 10.2 us
  starting transfers between devices: 6.97 us -> 23.8 us
  between operations: 13.5 us -> 0.13 us
  matrix products: 10.7 us -> 18.6 us
  local copies, waits for them, and re-layouts: 9.92 us -> 2.9 us
  Pallas kernels: 0 us -> 3.62 us
  other arithmetic: 4.55 us -> 7.08 us
    psum x1 -> x0, blocking collectives: 21 us -> none  [body(): reduced = lax.psum(reduced, 'tp')]
    ppermute x0 -> x11, starting transfers between devices: none -> 20.2 us  [the longest x1 7.75 us: body(): to_inner = lax.ppermute(far, 'tp', [(0, 1), (3, 2)])]
    all_to_all x2 -> x1, waiting for transfers between devices: 20.4 us -> 7.63 us  [fetch_adapters(): got = lax.all_to_all(packed, 'grp', split_axis=0, concat_axis=0, tiled=True)]
    reduce_scatter x1 -> x0, waiting for transfers between devices: 10.7 us -> none  [body(): lax.psum_scatter(partial_value, 'tp', scatter_dimension=1, tiled=True)]
    all_to_all x1 -> x0, blocking collectives: 9.62 us -> none  [body(): lax.all_to_all(wanted_ids, 'grp', split_axis=0, concat_axis=0, tiled=True)]
    dot_general x3 -> x6, matrix products: 10.7 us -> 18.6 us  [the longest x4 15.4 us: product(): value = jnp.dot(tokens, columns, preferred_element_type=jnp.float32)]
    gather x4 -> x1, local copies, waits for them, and re-layouts: 7.27 us -> 1.29 us  [reduce_tokens(): mine = jnp.take(got, block_slot, axis=0, mode='clip')]
    pallas_call x0 -> x2, Pallas kernels: none -> 3.62 us  [the longest x1 2.5 us: fetch_adapters(): pl.pallas_call(pack_kernel, out_shape=jax.ShapeDtypeStruct((group_count,...]
  transfers between devices with their start and end apart: 3 -> 12, of which waited for: 3 -> 4; matrix products, arithmetic and copies ran while one was open for 11% -> 31% of each run, Pallas kernels for 0% -> 5%
where the time goes in v2:
time: 66.9 us; the launch traced here: 66.3 us
  starting transfers between devices  23.8 us (36%)
  matrix products  18.6 us (28%)
  waiting for transfers between devices  10.2 us (15%)
  other arithmetic  7.08 us (11%)
  Pallas kernels  3.62 us (5%)
  local copies, waits for them, and re-layouts  2.9 us (4%)
    dot_general x4, matrix products, product(): value = jnp.dot(tokens, columns, preferred_element_type=jnp.float32)  15.4 us
    ppermute x1, starting transfers between devices, body(): to_inner = lax.ppermute(far, 'tp', [(0, 1), (3, 2)])  7.75 us
    all_to_all x1, waiting for transfers between devices, fetch_adapters(): got = lax.all_to_all(packed, 'grp', split_axis=0, concat_axis=0, tiled=True)  7.63 us
    ppermute x3, starting transfers between devices, body(): lax.ppermute(reduced, 'tp', [(i, i ^ j) for i in range(tp_count)])  4.4 us
    all_to_all x1, starting transfers between devices, fetch_adapters(): got = lax.all_to_all(packed, 'grp', split_axis=0, concat_axis=0, tiled=True)  3.58 us
    ppermute x3, starting transfers between devices, adapter_ids(): lax.ppermute(ids, 'grp', [(i, i ^ step) for i in range(group_count)])  3.19 us
    pallas_call x1, Pallas kernels, fetch_adapters(): pl.pallas_call(pack_kernel, out_shape=jax.ShapeDtypeStruct((group_count,...  2.5 us
    convert_element_type x1, other arithmetic, code(): return (value * SEND_SCALE).astype(jnp.float16)  2.37 us
  transfers between devices with their start and end apart: 12, of which 4 were waited for; matrix products, arithmetic and copies ran while one was open for 31% of the time, Pallas kernels for 5%

profile of v2, /device:TPU:0, one launch (start us, length us, event | category | flops | bytes accessed | tf_op | source)
XLA Modules:
  0.0 66.3 jit_solution(12643953526009456727)
XLA Ops:
  0.0 0.0 copy-start
  0.0 1.6 %copy-done = bf16[512,2048]{1,0:T(8,128)(2,1)S(1)} copy-done((bf16[512,2048]{1,0:T(8,128)(2,1)S(1)}, bf16[512,2048]{1,0:T(8,128)(2,1)}, u32[]{:S(2)}) %copy-start) | copy-done | bytes 2097176
  1.6 0.0 copy-start.2
  1.6 0.0 copy-start.4
  1.6 0.0 copy-start.3
  1.6 3.7 %fusion.29 = f16[512,512]{1,0:T(8,128)(2,1)} fusion(bf16[512,2048]{1,0:T(8,128)(2,1)S(1)} %copy-done, bf16[2048,2048]{1,0:T(8,128)(2,1)} %param.8, s32[]{:T(128)S(6)} %select_n.17), kind=kOutput, calls=%fused_computation.17 | convolution fusion | flops 1074266112 | bytes 4718596 | tf_op jit(solution)/shard_map/dot_general | solution.py:137
  5.3 1.5 %collective-permute-start = (f16[512,512]{1,0:T(8,128)(2,1)}, f16[512,512]{1,0:T(8,128)(2,1)}, u32[]{:S(2)}, u32[]{:S(2)}) collective-permute-start(f16[512,512]{1,0:T(8,128)(2,1)} %fusion.29), channel_id=1, source_target_pairs={{1,2},{2,1},{5,6},{6,5},{9,10},{10,9},{13,14},{14,13},{17,18},{18,... | collective-permute-start | bytes 1572872 | tf_op jit(solution)/shard_map/ppermute | solution.py:154
  6.8 7.8 %collective-permute-start.5 = (f16[512,512]{1,0:T(8,128)(2,1)}, f16[512,512]{1,0:T(8,128)(2,1)}, u32[]{:S(2)}, u32[]{:S(2)}) collective-permute-start(f16[512,512]{1,0:T(8,128)(2,1)} %fusion.29), channel_id=1, source_target_pairs={{0,1},{3,2},{4,5},{7,6},{8,9},{11,10},{12,13},{15,14},{16,17},{19,... | collective-permute-start | bytes 1572872 | tf_op jit(solution)/shard_map/ppermute | solution.py:153
  14.5 0.0 copy-done.2
  14.5 0.0 copy-done.4
  14.5 0.1 collective-permute-start.1
  14.6 0.0 copy-done.3
  14.6 0.1 fusion.40
  14.7 1.0 %collective-permute-done.1 = s32[1,4]{1,0:T(1,128)S(1)} collective-permute-done((s32[1,4]{1,0:T(1,128)S(1)}, s32[1,4]{1,0:T(1,128)S(1)}, u32[]{:S(2)}, u32[]{:S(2)}) %collective-permute-start.1) | collective-permute-done | bytes 48 | tf_op jit(solution)/shard_map/ppermute | solution.py:74
  15.7 1.6 %collective-permute-start.3 = (s32[2,4]{1,0:T(2,128)S(1)}, s32[2,4]{1,0:T(2,128)S(1)}, u32[]{:S(2)}, u32[]{:S(2)}) collective-permute-start(s32[2,4]{1,0:T(2,128)S(1)} %pad_add_fusion.2), channel_id=1, source_target_pairs={{0,8},{4,12},{8,0},{12,4},{16,24},{20,28},{24,16},{28,20},{1,9},{5... | collective-permute-start | bytes 104 | tf_op jit(solution)/shard_map/ppermute | solution.py:74
  17.3 4.0 %multiply_convert_fusion.1 = (f16[512,512]{1,0:T(8,128)(2,1)}, f32[512,512]{1,0:T(8,128)}) fusion(bf16[512,2048]{1,0:T(8,128)(2,1)S(1)} %copy-done, bf16[2048,2048]{1,0:T(8,128)(2,1)} %param.8, s32[]{:T(128)S(6)} %select_n.18), kind=kOutput, calls=%fused_computation.24 | convolution fusion | flops 1074266112 | bytes 5767172 | tf_op jit(solution)/shard_map/dot_general | solution.py:137
  21.3 2.1 %collective-permute-start.2 = (f16[512,512]{1,0:T(8,128)(2,1)}, f16[512,512]{1,0:T(8,128)(2,1)}, u32[]{:S(2)}, u32[]{:S(2)}) collective-permute-start(f16[512,512]{1,0:T(8,128)(2,1)} %get-tuple-element.11), channel_id=1, source_target_pairs={{0,2},{3,1},{4,6},{7,5},{8,10},{11,9},{12,14},{15,13},{16,18},{19,... | collective-permute-start | bytes 1572872 | tf_op jit(solution)/shard_map/ppermute | solution.py:157
  23.4 0.0 collective-permute-done.3
  23.4 1.6 %collective-permute-start.7 = (s32[4,4]{1,0:T(4,128)S(1)}, s32[4,4]{1,0:T(4,128)S(1)}, u32[]{:S(2)}, u32[]{:S(2)}) collective-permute-start(s32[4,4]{1,0:T(4,128)S(1)} %pad_add_fusion.1), channel_id=1, source_target_pairs={{0,16},{4,20},{8,24},{12,28},{16,0},{20,4},{24,8},{28,12},{1,17},{... | collective-permute-start | bytes 200 | tf_op jit(solution)/shard_map/ppermute | solution.py:74
  24.9 3.6 %fusion.26 = f16[512,512]{1,0:T(8,128)(2,1)} fusion(bf16[512,2048]{1,0:T(8,128)(2,1)S(1)} %copy-done, bf16[2048,2048]{1,0:T(8,128)(2,1)} %param.8, s32[]{:T(128)S(6)} %select_n.19), kind=kOutput, calls=%fused_computation.16 | convolution fusion | flops 1074266112 | bytes 4718596 | tf_op jit(solution)/shard_map/dot_general | solution.py:137
  28.6 0.0 collective-permute-start.4
  28.6 0.0 collective-permute-done.7
  28.6 0.6 pad_add_fusion.ids_ref
  29.2 2.5 %shard_map.73 = bf16[8,2,16,2560]{3,2,1,0:T(8,128)(2,1)} custom-call(s32[8,4]{1,0:T(8,128)} %pad_add_fusion.ids_ref, s32[1]{0:T(128)} %bitcast.7.me_ref, bf16[128,16,2048]{2,1,0:T(8,128)(2,1)} %bitcast.40, bf16[128,16,512]{2,1,0:T(8,128)(2,1)} %up_ref.1), custom_call_target="tpu_custom_call" | custom-call | flops 1 | bytes 1 | tf_op jit(solution)/shard_map/pallas_call | solution.py:85
  31.7 3.6 %all-to-all-start = ((bf16[8,2,16,2560]{3,2,1,0:T(8,128)(2,1)}), bf16[8,2,16,2560]{3,2,1,0:T(8,128)(2,1)S(1)}, u32[]{:S(2)}, u32[]{:S(2)}) async-start(bf16[8,2,16,2560]{3,2,1,0:T(8,128)(2,1)} %shard_map.73), calls=%async_computation | async-start | bytes 2621440 | tf_op jit(solution)/shard_map/all_to_all | solution.py:100
  35.3 0.0 collective-permute-done.5
  35.3 2.4 %multiply_convert_fusion = f16[512,512]{1,0:T(8,128)(2,1)} fusion(f32[512,512]{1,0:T(8,128)} %get-tuple-element.13, f16[512,512]{1,0:T(8,128)(2,1)} %collective-permute-done.5), kind=kLoop, calls=%fused_computation.22 | loop fusion | flops 1310720 | bytes 2097152 | tf_op jit(solution)/shard_map/convert_element_type | solution.py:141
  37.7 1.3 %collective-permute-start.6 = (f16[512,512]{1,0:T(8,128)(2,1)}, f16[512,512]{1,0:T(8,128)(2,1)}, u32[]{:S(2)}, u32[]{:S(2)}) collective-permute-start(f16[512,512]{1,0:T(8,128)(2,1)} %multiply_convert_fusion), channel_id=1, source_target_pairs={{1,3},{2,0},{5,7},{6,4},{9,11},{10,8},{13,15},{14,12},{17,19},{18,... | collective-permute-start | bytes 1572872 | tf_op jit(solution)/shard_map/ppermute | solution.py:161
  38.9 0.0 collective-permute-done
  39.0 0.0 collective-permute-done.2
  39.0 4.1 %multiply_add_fusion.1 = f32[512,512]{1,0:T(8,128)} fusion(f16[512,512]{1,0:T(8,128)(2,1)} %collective-permute-done.2, f16[512,512]{1,0:T(8,128)(2,1)} %collective-permute-done, bf16[512,2048]{1,0:T(8,128)(2,1)S(1)} %copy-done, bf16[2048,2048]{1,0:T(8,128)(2,1)} %param.8, s32[]{:T(128)S(6)} %select_n.16), kind=kOutput, calls=%fused_computation.23 | convolution fusion | flops 1075314688 | bytes 6291460 | tf_op jit(solution)/shard_map/dot_general | solution.py:137
  43.1 1.1 %shard_map.74 = s32[4]{0:T(128)} custom-call(s32[4]{0:T(128)} %bitcast.42), custom_call_target="tpu_custom_call" | custom-call | flops 99999997952 | bytes 1 | tf_op jit(solution)/shard_map/pallas_call | solution.py:106
  44.2 0.9 %convert_reduce_fusion = s32[4]{0:T(128)S(1)} fusion(s32[4]{0:T(128)} %shard_map.74), kind=kLoop, calls=%fused_computation.34 | loop fusion | flops 76 | bytes 32 | tf_op jit(solution)/shard_map/reduce_sum | solution.py:120
  45.1 0.7 multiply_add_fusion.2
  45.8 7.6 %all-to-all-done = bf16[8,2,16,2560]{3,2,1,0:T(8,128)(2,1)S(1)} async-done(((bf16[8,2,16,2560]{3,2,1,0:T(8,128)(2,1)}), bf16[8,2,16,2560]{3,2,1,0:T(8,128)(2,1)S(1)}, u32[]{:S(2)}, u32[]{:S(2)}) %all-to-all-start) | async-done | bytes 1310752 | tf_op jit(solution)/shard_map/all_to_all | solution.py:100
  53.4 1.3 %gather_fusion = bf16[4,16,2560]{2,1,0:T(8,128)(2,1)} fusion(bf16[16,16,2560]{2,1,0:T(8,128)(2,1)S(1)} %bitcast.41, s32[1024]{0:T(1024)S(1)} %pad_clamp_fusion), kind=kCustom, calls=%fused_computation | custom fusion | bytes 655376 | tf_op jit(solution)/shard_map/jit(_take)/gather | solution.py:121
  54.7 0.0 copy-start.1
  54.7 1.7 %fusion.34 = f32[4,16,128]{2,1,0:T(8,128)S(1)} fusion(bf16[4,128,2048]{2,1,0:T(8,128)(2,1)S(1)} %bitcast.39, bf16[4,16,2560]{2,1,0:T(8,128)(2,1)} %gather_fusion), kind=kOutput, calls=%fused_computation.25 | convolution fusion | flops 33554432 | bytes 2392064 | tf_op jit(solution)/shard_map/nbd,nrd->nrb/dot_general | solution.py:123
  56.4 1.6 %collective-permute-start.10 = (f32[4,16,128]{2,1,0:T(8,128)S(1)}, f32[4,16,128]{2,1,0:T(8,128)S(1)}, u32[]{:S(2)}, u32[]{:S(2)}) collective-permute-start(f32[4,16,128]{2,1,0:T(8,128)S(1)} %fusion.34), channel_id=1, source_target_pairs={{0,3},{1,2},{2,1},{3,0},{4,7},{5,6},{6,5},{7,4},{8,11},{9,10},{10,... | collective-permute-start | bytes 98312 | tf_op jit(solution)/shard_map/ppermute | solution.py:171
  58.0 1.9 %collective-permute-start.9 = (f32[4,16,128]{2,1,0:T(8,128)S(1)}, f32[4,16,128]{2,1,0:T(8,128)S(1)}, u32[]{:S(2)}, u32[]{:S(2)}) collective-permute-start(f32[4,16,128]{2,1,0:T(8,128)S(1)} %fusion.34), channel_id=1, source_target_pairs={{0,2},{1,3},{2,0},{3,1},{4,6},{5,7},{6,4},{7,5},{8,10},{9,11},{10,... | collective-permute-start | bytes 98312 | tf_op jit(solution)/shard_map/ppermute | solution.py:171
  59.9 0.9 %collective-permute-start.8 = (f32[4,16,128]{2,1,0:T(8,128)S(1)}, f32[4,16,128]{2,1,0:T(8,128)S(1)}, u32[]{:S(2)}, u32[]{:S(2)}) collective-permute-start(f32[4,16,128]{2,1,0:T(8,128)S(1)} %fusion.34), channel_id=1, source_target_pairs={{0,1},{1,0},{2,3},{3,2},{4,5},{5,4},{6,7},{7,6},{8,9},{9,8},{10,11... | collective-permute-start | bytes 98312 | tf_op jit(solution)/shard_map/ppermute | solution.py:171
  60.8 0.0 collective-permute-done.4
  60.8 0.0 collective-permute-done.6
  60.8 0.0 copy-done.1
  60.8 1.5 %multiply_add_fusion = f32[512,512]{1,0:T(8,128)S(1)} fusion(f32[512,512]{1,0:T(8,128)S(1)} %copy-done.1, f16[512,512]{1,0:T(8,128)(2,1)} %collective-permute-done.6, f16[512,512]{1,0:T(8,128)(2,1)} %collective-permute-done.4), kind=kLoop, calls=%fused_computation.21 | loop fusion | flops 1310720 | bytes 3145728 | tf_op jit(solution)/shard_map/add | solution.py:164
  62.3 0.0 collective-permute-done.10
  62.3 0.5 collective-permute-done.9
  62.8 1.0 %collective-permute-done.8 = f32[4,16,128]{2,1,0:T(8,128)S(1)} collective-permute-done((f32[4,16,128]{2,1,0:T(8,128)S(1)}, f32[4,16,128]{2,1,0:T(8,128)S(1)}, u32[]{:S(2)}, u32[]{:S(2)}) %collective-permute-start.8) | collective-permute-done | bytes 32800 | tf_op jit(solution)/shard_map/ppermute | solution.py:171
  63.8 1.5 %convolution_multiply_fusion = f32[4,128,512]{2,1,0:T(8,128)S(1)} fusion(bf16[4,16,2560]{2,1,0:T(8,128)(2,1)} %gather_fusion, f32[4,16,128]{2,1,0:T(8,128)S(1)} %collective-permute-done.10, f32[4,16,128]{2,1,0:T(8,128)S(1)} %collective-permute-done.9, f32[4,16,128]{2,1,0:T(8,128)S(1)} %fusion.34, f32[4,16,128]{2,1,0:T(8,128)S(1)} %collective-permute-done.8), kind=kOutput, calls=%fused_computation.15 | convolution fusion | flops 50618368 | bytes 1245184 | tf_op jit(solution)/shard_map/nrb,nro->nbo/dot_general | solution.py:172
  65.3 1.0 %fusion.33 = bf16[512,512]{1,0:T(8,128)(2,1)} fusion(f32[512,512]{1,0:T(8,128)S(1)} %multiply_add_fusion, f32[4,128,512]{2,1,0:T(8,128)S(1)} %convolution_multiply_fusion, pred[512]{0:T(512)(128)(4,1)S(1)} %fusion.40), kind=kLoop, calls=%fused_computation.20 | loop fusion | flops 786432 | bytes 2621952 | tf_op jit(solution)/shard_map/convert_element_type | solution.py:176
  (4 shorter events, 0.0 us)
Async XLA Ops:
  0.0 1.6 %copy-start = (bf16[512,2048]{1,0:T(8,128)(2,1)S(1)}, bf16[512,2048]{1,0:T(8,128)(2,1)}, u32[]{:S(2)}) copy-start(bf16[512,2048]{1,0:T(8,128)(2,1)} %param.7) | copy-start | bytes 6291460
  1.6 12.9 %copy-start.2 = (s32[4]{0:T(128)S(1)}, s32[4]{0:T(128)}, u32[]{:S(2)}) copy-start(s32[4]{0:T(128)} %param.12) | copy-start | bytes 52
  1.6 12.9 %copy-start.4 = (s32[4,1]{0,1:T(1,128)S(1)}, s32[4,1]{0,1:T(1,128)}, u32[]{:S(2)}) copy-start(s32[4,1]{0,1:T(1,128)} %param.11) | copy-start | bytes 52
  1.6 13.0 %copy-start.3 = (s32[4]{0:T(128)S(1)}, s32[4]{0:T(128)}, u32[]{:S(2)}) copy-start(s32[4]{0:T(128)} %param.13) | copy-start | bytes 52
  5.3 33.7 %collective-permute-start = (f16[512,512]{1,0:T(8,128)(2,1)}, f16[512,512]{1,0:T(8,128)(2,1)}, u32[]{:S(2)}, u32[]{:S(2)}) collective-permute-start(f16[512,512]{1,0:T(8,128)(2,1)} %fusion.29), channel_id=1, source_target_pairs={{1,2},{2,1},{5,6},{6,5},{9,10},{10,9},{13,14},{14,13},{17,18},{18,... | collective-permute-start | bytes 1572872 | tf_op jit(solution)/shard_map/ppermute | solution.py:154
  6.8 28.5 %collective-permute-start.5 = (f16[512,512]{1,0:T(8,128)(2,1)}, f16[512,512]{1,0:T(8,128)(2,1)}, u32[]{:S(2)}, u32[]{:S(2)}) collective-permute-start(f16[512,512]{1,0:T(8,128)(2,1)} %fusion.29), channel_id=1, source_target_pairs={{0,1},{3,2},{4,5},{7,6},{8,9},{11,10},{12,13},{15,14},{16,17},{19,... | collective-permute-start | bytes 1572872 | tf_op jit(solution)/shard_map/ppermute | solution.py:153
  14.5 1.2 %collective-permute-start.1 = (s32[1,4]{1,0:T(1,128)S(1)}, s32[1,4]{1,0:T(1,128)S(1)}, u32[]{:S(2)}, u32[]{:S(2)}) collective-permute-start(s32[1,4]{1,0:T(1,128)S(1)} %add_bitcast_fusion), channel_id=1, source_target_pairs={{0,4},{4,0},{8,12},{12,8},{16,20},{20,16},{24,28},{28,24},{1,5},{5... | collective-permute-start | bytes 56 | tf_op jit(solution)/shard_map/ppermute | solution.py:74
  15.7 7.6 %collective-permute-start.3 = (s32[2,4]{1,0:T(2,128)S(1)}, s32[2,4]{1,0:T(2,128)S(1)}, u32[]{:S(2)}, u32[]{:S(2)}) collective-permute-start(s32[2,4]{1,0:T(2,128)S(1)} %pad_add_fusion.2), channel_id=1, source_target_pairs={{0,8},{4,12},{8,0},{12,4},{16,24},{20,28},{24,16},{28,20},{1,9},{5... | collective-permute-start | bytes 104 | tf_op jit(solution)/shard_map/ppermute | solution.py:74
  21.3 17.7 %collective-permute-start.2 = (f16[512,512]{1,0:T(8,128)(2,1)}, f16[512,512]{1,0:T(8,128)(2,1)}, u32[]{:S(2)}, u32[]{:S(2)}) collective-permute-start(f16[512,512]{1,0:T(8,128)(2,1)} %get-tuple-element.11), channel_id=1, source_target_pairs={{0,2},{3,1},{4,6},{7,5},{8,10},{11,9},{12,14},{15,13},{16,18},{19,... | collective-permute-start | bytes 1572872 | tf_op jit(solution)/shard_map/ppermute | solution.py:157
  23.4 5.2 %collective-permute-start.7 = (s32[4,4]{1,0:T(4,128)S(1)}, s32[4,4]{1,0:T(4,128)S(1)}, u32[]{:S(2)}, u32[]{:S(2)}) collective-permute-start(s32[4,4]{1,0:T(4,128)S(1)} %pad_add_fusion.1), channel_id=1, source_target_pairs={{0,16},{4,20},{8,24},{12,28},{16,0},{20,4},{24,8},{28,12},{1,17},{... | collective-permute-start | bytes 200 | tf_op jit(solution)/shard_map/ppermute | solution.py:74
  28.6 32.2 %collective-permute-start.4 = (f16[512,512]{1,0:T(8,128)(2,1)}, f16[512,512]{1,0:T(8,128)(2,1)}, u32[]{:S(2)}, u32[]{:S(2)}) collective-permute-start(f16[512,512]{1,0:T(8,128)(2,1)} %fusion.26), channel_id=1, source_target_pairs={{0,1},{1,0},{2,3},{3,2},{4,5},{5,4},{6,7},{7,6},{8,9},{9,8},{10,11... | collective-permute-start | bytes 1572872 | tf_op jit(solution)/shard_map/ppermute | solution.py:159
  31.7 21.7 %all-to-all-start = ((bf16[8,2,16,2560]{3,2,1,0:T(8,128)(2,1)}), bf16[8,2,16,2560]{3,2,1,0:T(8,128)(2,1)S(1)}, u32[]{:S(2)}, u32[]{:S(2)}) async-start(bf16[8,2,16,2560]{3,2,1,0:T(8,128)(2,1)} %shard_map.73), calls=%async_computation | async-start | bytes 2621440 | tf_op jit(solution)/shard_map/all_to_all | solution.py:100
  37.7 23.1 %collective-permute-start.6 = (f16[512,512]{1,0:T(8,128)(2,1)}, f16[512,512]{1,0:T(8,128)(2,1)}, u32[]{:S(2)}, u32[]{:S(2)}) collective-permute-start(f16[512,512]{1,0:T(8,128)(2,1)} %multiply_convert_fusion), channel_id=1, source_target_pairs={{1,3},{2,0},{5,7},{6,4},{9,11},{10,8},{13,15},{14,12},{17,19},{18,... | collective-permute-start | bytes 1572872 | tf_op jit(solution)/shard_map/ppermute | solution.py:161
  54.7 6.1 %copy-start.1 = (f32[512,512]{1,0:T(8,128)S(1)}, f32[512,512]{1,0:T(8,128)}, u32[]{:S(2)}) copy-start(f32[512,512]{1,0:T(8,128)} %multiply_add_fusion.1) | copy-start | bytes 3145732
  56.4 5.9 %collective-permute-start.10 = (f32[4,16,128]{2,1,0:T(8,128)S(1)}, f32[4,16,128]{2,1,0:T(8,128)S(1)}, u32[]{:S(2)}, u32[]{:S(2)}) collective-permute-start(f32[4,16,128]{2,1,0:T(8,128)S(1)} %fusion.34), channel_id=1, source_target_pairs={{0,3},{1,2},{2,1},{3,0},{4,7},{5,6},{6,5},{7,4},{8,11},{9,10},{10,... | collective-permute-start | bytes 98312 | tf_op jit(solution)/shard_map/ppermute | solution.py:171
  58.0 4.8 %collective-permute-start.9 = (f32[4,16,128]{2,1,0:T(8,128)S(1)}, f32[4,16,128]{2,1,0:T(8,128)S(1)}, u32[]{:S(2)}, u32[]{:S(2)}) collective-permute-start(f32[4,16,128]{2,1,0:T(8,128)S(1)} %fusion.34), channel_id=1, source_target_pairs={{0,2},{1,3},{2,0},{3,1},{4,6},{5,7},{6,4},{7,5},{8,10},{9,11},{10,... | collective-permute-start | bytes 98312 | tf_op jit(solution)/shard_map/ppermute | solution.py:171
  59.9 3.9 %collective-permute-start.8 = (f32[4,16,128]{2,1,0:T(8,128)S(1)}, f32[4,16,128]{2,1,0:T(8,128)S(1)}, u32[]{:S(2)}, u32[]{:S(2)}) collective-permute-start(f32[4,16,128]{2,1,0:T(8,128)S(1)} %fusion.34), channel_id=1, source_target_pairs={{0,1},{1,0},{2,3},{3,2},{4,5},{5,4},{6,7},{7,6},{8,9},{9,8},{10,11... | collective-permute-start | bytes 98312 | tf_op jit(solution)/shard_map/ppermute | solution.py:171

commit v3 on v2

--- a/solution.py
+++ b/solution.py
@@ -77,12 +77,12 @@
         step *= 2
 
 
-def fetch_adapters(ids, down_tables, up_tables):
+def pack_adapters(ids, down_tables, up_tables):
     group_count = lax.axis_size("grp")
     me = lax.axis_index("grp").astype(jnp.int32).reshape(1)
     _, cols, rank = down_tables.shape
     wide = cols + up_tables.shape[2]
-    packed = pl.pallas_call(
+    return pl.pallas_call(
         pack_kernel,
         out_shape=jax.ShapeDtypeStruct((group_count, CAP, rank, wide), jnp.bfloat16),
         grid_spec=pltpu.PrefetchScalarGridSpec(
@@ -97,8 +97,11 @@
         ),
         cost_estimate=CHEAP,
     )(ids, me, jnp.transpose(down_tables, (0, 2, 1)), up_tables)
+
+
+def exchange(packed):
     got = lax.all_to_all(packed, "grp", split_axis=0, concat_axis=0, tiled=True)
-    return got.reshape(group_count * CAP, rank, wide)
+    return got.reshape(got.shape[0] * CAP, *got.shape[2:])
 
 
 def later(value, *others):
@@ -113,15 +116,21 @@
     )(value)
 
 
-def reduce_tokens(tokens, got, owners):
-    blocks, cols = owners.shape[0], tokens.shape[1]
-    order = jnp.arange(blocks, dtype=jnp.int32)
+def slot_plan(owners):
+    order = jnp.arange(owners.shape[0], dtype=jnp.int32)
     earlier = (owners[None, :] == owners[:, None]) & (order[None, :] < order[:, None])
-    block_slot = owners * CAP + jnp.sum(earlier.astype(jnp.int32), axis=1)
+    return owners * CAP + jnp.sum(earlier.astype(jnp.int32), axis=1)
+
+
+def reduce_tokens(tokens, got, block_slot):
+    blocks, cols = block_slot.shape[0], tokens.shape[1]
     mine = jnp.take(got, block_slot, axis=0, mode="clip")
+    mine = lax.optimization_barrier(mine)
+    down_block = lax.optimization_barrier(mine[:, :, :cols])
     blocked = tokens.reshape(blocks, BLOCK, cols)
-    reduced = jnp.einsum("nbd,nrd->nrb", blocked, mine[:, :, :cols], preferred_element_type=jnp.float32)
-    return reduced, mine[:, :, cols:]
+    reduced = jnp.einsum("nbd,nrd->nrb", blocked, down_block, preferred_element_type=jnp.float32)
+    up_block, _ = lax.optimization_barrier((mine[:, :, cols:], reduced))
+    return reduced, up_block
 
 
 def body(tokens, base_weight, down_tables, up_tables, block_owner, block_local, block_count):
@@ -147,25 +156,31 @@
         return lax.optimization_barrier((value, *others))[0]
 
     id_steps = list(adapter_ids(block_owner, block_local, down_tables.shape[0]))
-    got = fetch_adapters(id_steps[-1], down_tables, up_tables)
     if tp_count == 4:
-        far = code(product(z ^ 3))
+        end = (z == 0) | (z == 3)
+        far = after(code(product(z ^ 3)), id_steps[0])
         to_inner = lax.ppermute(far, "tp", [(0, 1), (3, 2)])
         from_inner = lax.ppermute(far, "tp", [(1, 2), (2, 1)])
-        middle = product(after(z, id_steps[0]) ^ 2)
-        middle, middle_code = lax.optimization_barrier((middle, code(middle)))
-        from_middle = lax.ppermute(middle_code, "tp", [(0, 2), (3, 1)])
-        near = code(product(after(z, id_steps[1]) ^ 1))
-        from_near = lax.ppermute(near, "tp", [(0, 1), (1, 0), (2, 3), (3, 2)])
-        inner_sum = code(middle + plain(to_inner))
-        from_far = lax.ppermute(inner_sum, "tp", [(1, 3), (2, 0)])
-        base_projection = lax.optimization_barrier(product(z) + plain(from_inner) + plain(from_middle))
-        reduced, up_block = reduce_tokens(tokens, got, later(owners, base_projection))
-        base_projection = lax.optimization_barrier(base_projection + (plain(from_near) + plain(from_far)))
+        later_z = after(z, id_steps[1])
+        first = code(product(later_z ^ jnp.where(end, 2, 1)))
+        from_first = lax.ppermute(first, "tp", [(0, 2), (3, 1), (1, 0), (2, 3)])
+        packed = pack_adapters(after(id_steps[-1], first), down_tables, up_tables)
+        later_z, packed = lax.optimization_barrier((z, packed))
+        got = exchange(packed)
+        second = product(later_z ^ jnp.where(end, 1, 2))
+        second = code(second + plain(to_inner))
+        from_second = lax.ppermute(second, "tp", [(0, 1), (3, 2), (1, 3), (2, 0)])
+        own = lax.optimization_barrier(product(after(z, second)))
+        base_projection = lax.optimization_barrier(own + plain(from_inner) + plain(from_first))
+        block_slot = slot_plan(later(owners, base_projection))
+        reduced, up_block = reduce_tokens(tokens, got, block_slot)
+        from_second = after(from_second, reduced)
+        base_projection = lax.optimization_barrier(base_projection + plain(from_second))
     else:
         partial_value = jnp.dot(tokens, base_weight, preferred_element_type=jnp.float32)
         base_projection = lax.psum_scatter(partial_value, "tp", scatter_dimension=1, tiled=True)
-        reduced, up_block = reduce_tokens(tokens, got, owners)
+        got = exchange(pack_adapters(id_steps[-1], down_tables, up_tables))
+        reduced, up_block = reduce_tokens(tokens, got, slot_plan(owners))
     total = reduced
     for j in range(1, tp_count):
         total = total + lax.ppermute(reduced, "tp", [(i, i ^ j) for i in range(tp_count)])

time: 66.9 us -> 58.9 us (0.88)
  matrix products: 18.6 us -> 14.2 us
  starting transfers between devices: 23.8 us -> 19.7 us
  other arithmetic: 7.08 us -> 8.38 us
  waiting for transfers between devices: 10.2 us -> 9.51 us
    ppermute x1, starting transfers between devices: 7.75 us -> 3.5 us  [body(): to_inner = lax.ppermute(far, 'tp', [(0, 1), (3, 2)])]
    dot_general x4, matrix products: 15.4 us -> 13 us  [product(): value = jnp.dot(tokens, columns, preferred_element_type=jnp.float32)]
    all_to_all x1, waiting for transfers between devices: 7.63 us -> 5.6 us  [exchange(): got = lax.all_to_all(packed, 'grp', split_axis=0, concat_axis=0, tiled=True)]
    ppermute x3, waiting for transfers between devices: 1.52 us -> 3.1 us  [body(): lax.ppermute(reduced, 'tp', [(i, i ^ j) for i in range(tp_count)])]
    ppermute x3, starting transfers between devices: 3.19 us -> 4.65 us  [adapter_ids(): lax.ppermute(ids, 'grp', [(i, i ^ step) for i in range(group_count)])]
    convert_element_type x1, other arithmetic: 2.37 us -> 1.03 us  [code(): return (value * SEND_SCALE).astype(jnp.float16)]
    ppermute x3 -> x2, starting transfers between devices: 3.38 us -> 2.16 us  [the longest x1 2.03 us: body(): from_first = lax.ppermute(first, 'tp', [(0, 2), (3, 1), (1, 0), (2, 3)])]
    add x2 -> x3, other arithmetic: 2.12 us -> 3.3 us  [the longest x1 1.42 us: body(): own + plain(from_inner) + plain(from_first)]
  transfers between devices with their start and end apart: 12 -> 11, of which waited for: 4 -> 3; matrix products, arithmetic and copies ran while one was open for 31% -> 38% of each run, Pallas kernels for 5% -> 6%
where the time goes in v3:
time: 58.9 us; the launch traced here: 58.3 us
  starting transfers between devices  19.7 us (33%)
  matrix products  14.2 us (24%)
  waiting for transfers between devices  9.51 us (16%)
  other arithmetic  8.38 us (14%)
  Pallas kernels  3.6 us (6%)
  local copies, waits for them, and re-layouts  2.73 us (5%)
    dot_general x4, matrix products, product(): value = jnp.dot(tokens, columns, preferred_element_type=jnp.float32)  13 us
    all_to_all x1, waiting for transfers between devices, exchange(): got = lax.all_to_all(packed, 'grp', split_axis=0, concat_axis=0, tiled=True)  5.6 us
    ppermute x3, starting transfers between devices, adapter_ids(): lax.ppermute(ids, 'grp', [(i, i ^ step) for i in range(group_count)])  4.65 us
    ppermute x3, starting transfers between devices, body(): lax.ppermute(reduced, 'tp', [(i, i ^ j) for i in range(tp_count)])  4.4 us
    all_to_all x1, starting transfers between devices, exchange(): got = lax.all_to_all(packed, 'grp', split_axis=0, concat_axis=0, tiled=True)  4.26 us
    ppermute x1, starting transfers between devices, body(): to_inner = lax.ppermute(far, 'tp', [(0, 1), (3, 2)])  3.5 us
    ppermute x3, waiting for transfers between devices, body(): lax.ppermute(reduced, 'tp', [(i, i ^ j) for i in range(tp_count)])  3.1 us
    pallas_call x1, Pallas kernels, pack_adapters(): pl.pallas_call(pack_kernel, out_shape=jax.ShapeDtypeStruct((group_count,...  2.47 us
  transfers between devices with their start and end apart: 11, of which 3 were waited for; matrix products, arithmetic and copies ran while one was open for 38% of the time, Pallas kernels for 6%

profile of v3, /device:TPU:0, one launch (start us, length us, event | category | flops | bytes accessed | tf_op | source)
XLA Modules:
  0.0 58.3 jit_solution(14115704371305826480)
XLA Ops:
  0.0 0.0 copy-start
  0.0 0.8 %add_bitcast_fusion = s32[1,4]{1,0:T(1,128)S(1)} fusion(s32[4]{0:T(128)} %param.12, s32[4,1]{0,1:T(1,128)} %param.11), kind=kLoop, calls=%fused_computation.41 | loop fusion | flops 8 | bytes 48 | tf_op jit(solution)/shard_map/reshape | solution.py:71
  0.8 0.5 collective-permute-start
  1.3 0.7 %fusion.37 = pred[512]{0:T(512)(128)(4,1)S(1)} fusion(s32[4]{0:T(128)} %param.13), kind=kLoop, calls=%fused_computation.33 | loop fusion | flops 512 | bytes 528 | tf_op jit(solution)/shard_map/lt | solution.py:142
  2.0 0.0 copy-done
  2.0 3.7 %fusion.26 = f16[512,512]{1,0:T(8,128)(2,1)} fusion(bf16[512,2048]{1,0:T(8,128)(2,1)S(1)} %copy-done, bf16[2048,2048]{1,0:T(8,128)(2,1)} %param.8, s32[]{:T(128)S(6)} %select_n.27), kind=kOutput, calls=%fused_computation.16 | convolution fusion | flops 1074266112 | bytes 4718596 | tf_op jit(solution)/shard_map/dot_general | solution.py:146
  5.7 0.0 collective-permute-done
  5.7 2.6 %collective-permute-start.1 = (s32[2,4]{1,0:T(2,128)S(1)}, s32[2,4]{1,0:T(2,128)S(1)}, u32[]{:S(2)}, u32[]{:S(2)}) collective-permute-start(s32[2,4]{1,0:T(2,128)S(1)} %pad_add_fusion.2), channel_id=1, source_target_pairs={{0,8},{4,12},{8,0},{12,4},{16,24},{20,28},{24,16},{28,20},{1,9},{5... | collective-permute-start | bytes 104 | tf_op jit(solution)/shard_map/ppermute | solution.py:74
  8.3 3.5 %collective-permute-start.3 = (f16[512,512]{1,0:T(8,128)(2,1)}, f16[512,512]{1,0:T(8,128)(2,1)S(1)}, u32[]{:S(2)}, u32[]{:S(2)}) collective-permute-start(f16[512,512]{1,0:T(8,128)(2,1)} %fusion.26), channel_id=1, source_target_pairs={{0,1},{3,2},{4,5},{7,6},{8,9},{11,10},{12,13},{15,14},{16,17},{19,... | collective-permute-start | bytes 1572872 | tf_op jit(solution)/shard_map/ppermute | solution.py:162
  11.8 0.7 %collective-permute-start.4 = (f16[512,512]{1,0:T(8,128)(2,1)}, f16[512,512]{1,0:T(8,128)(2,1)S(1)}, u32[]{:S(2)}, u32[]{:S(2)}) collective-permute-start(f16[512,512]{1,0:T(8,128)(2,1)} %fusion.26), channel_id=1, source_target_pairs={{1,2},{2,1},{5,6},{6,5},{9,10},{10,9},{13,14},{14,13},{17,18},{18,... | collective-permute-start | bytes 1572872 | tf_op jit(solution)/shard_map/ppermute | solution.py:163
  12.5 0.0 collective-permute-done.1
  12.5 1.6 %collective-permute-start.2 = (s32[4,4]{1,0:T(4,128)S(1)}, s32[4,4]{1,0:T(4,128)S(1)}, u32[]{:S(2)}, u32[]{:S(2)}) collective-permute-start(s32[4,4]{1,0:T(4,128)S(1)} %pad_add_fusion.1), channel_id=1, source_target_pairs={{0,16},{4,20},{8,24},{12,28},{16,0},{20,4},{24,8},{28,12},{1,17},{... | collective-permute-start | bytes 200 | tf_op jit(solution)/shard_map/ppermute | solution.py:74
  14.1 3.6 %fusion.29 = f16[512,512]{1,0:T(8,128)(2,1)} fusion(bf16[512,2048]{1,0:T(8,128)(2,1)S(1)} %copy-done, bf16[2048,2048]{1,0:T(8,128)(2,1)} %param.8, s32[]{:T(128)S(6)} %select_n.24), kind=kOutput, calls=%fused_computation.17 | convolution fusion | flops 1074266112 | bytes 4718596 | tf_op jit(solution)/shard_map/dot_general | solution.py:146
  17.8 2.0 %collective-permute-start.5 = (f16[512,512]{1,0:T(8,128)(2,1)}, f16[512,512]{1,0:T(8,128)(2,1)}, u32[]{:S(2)}, u32[]{:S(2)}) collective-permute-start(f16[512,512]{1,0:T(8,128)(2,1)} %fusion.29), channel_id=1, source_target_pairs={{0,2},{3,1},{1,0},{2,3},{4,6},{7,5},{5,4},{6,7},{8,10},{11,9},{9,8... | collective-permute-start | bytes 1572872 | tf_op jit(solution)/shard_map/ppermute | solution.py:166
  19.8 0.0 collective-permute-done.2
  19.8 0.6 %pad_add_fusion.ids_ref = s32[8,4]{1,0:T(8,128)} fusion(s32[4,4]{1,0:T(4,128)S(1)} %collective-permute-done.2, s32[2,4]{1,0:T(2,128)S(1)} %collective-permute-done.1, s32[1,4]{1,0:T(1,128)S(1)} %collective-permute-done, s32[1,4]{1,0:T(1,128)S(1)} %add_bitcast_fusion), kind=kLoop, calls=%fused_computation.28 | loop fusion | flops 96 | bytes 256 | tf_op jit(solution)/shard_map/concatenate | solution.py:75
  20.4 2.5 %shard_map.73 = bf16[8,2,16,2560]{3,2,1,0:T(8,128)(2,1)} custom-call(s32[8,4]{1,0:T(8,128)} %pad_add_fusion.ids_ref, s32[1]{0:T(128)} %bitcast.4.me_ref, bf16[128,16,2048]{2,1,0:T(8,128)(2,1)} %bitcast.40, bf16[128,16,512]{2,1,0:T(8,128)(2,1)} %up_ref.1), custom_call_target="tpu_custom_call" | custom-call | flops 1 | bytes 1 | tf_op jit(solution)/shard_map/pallas_call | solution.py:85
  22.9 4.3 %all-to-all-start = ((bf16[8,2,16,2560]{3,2,1,0:T(8,128)(2,1)}), bf16[8,2,16,2560]{3,2,1,0:T(8,128)(2,1)}, u32[]{:S(2)}, u32[]{:S(2)}) async-start(bf16[8,2,16,2560]{3,2,1,0:T(8,128)(2,1)} %shard_map.73), calls=%async_computation | async-start | bytes 2621440 | tf_op jit(solution)/shard_map/all_to_all | solution.py:103
  27.2 2.8 %fusion.14 = f32[512,512]{1,0:T(8,128)S(1)} fusion(bf16[512,2048]{1,0:T(8,128)(2,1)S(1)} %copy-done, bf16[2048,2048]{1,0:T(8,128)(2,1)} %param.8, s32[]{:T(128)S(6)} %select_n.26), kind=kOutput, calls=%fused_computation.11 | convolution fusion | flops 1073741824 | bytes 5242884 | tf_op jit(solution)/shard_map/dot_general | solution.py:146
  30.0 0.0 collective-permute-done.3
  30.0 1.0 %multiply_convert_fusion = f16[512,512]{1,0:T(8,128)(2,1)} fusion(f32[512,512]{1,0:T(8,128)S(1)} %fusion.14, f16[512,512]{1,0:T(8,128)(2,1)S(1)} %collective-permute-done.3), kind=kLoop, calls=%fused_computation.23 | loop fusion | flops 1310720 | bytes 2097152 | tf_op jit(solution)/shard_map/convert_element_type | solution.py:150
  31.0 0.1 collective-permute-start.6
  31.2 2.8 %fusion.23 = f32[512,512]{1,0:T(8,128)S(1)} fusion(bf16[512,2048]{1,0:T(8,128)(2,1)S(1)} %copy-done, bf16[2048,2048]{1,0:T(8,128)(2,1)} %param.8, s32[]{:T(128)S(6)} %select_n.28), kind=kOutput, calls=%fused_computation.14 | convolution fusion | flops 1073741824 | bytes 5242884 | tf_op jit(solution)/shard_map/dot_general | solution.py:146
  34.0 0.0 collective-permute-done.4
  34.0 0.0 copy-start.1
  34.0 0.8 %copy-done.1 = f16[512,512]{1,0:T(8,128)(2,1)} copy-done((f16[512,512]{1,0:T(8,128)(2,1)}, f16[512,512]{1,0:T(8,128)(2,1)S(1)}, u32[]{:S(2)}) %copy-start.1) | copy-done | bytes 524312
  34.8 0.8 %collective-permute-done.5 = f16[512,512]{1,0:T(8,128)(2,1)} collective-permute-done((f16[512,512]{1,0:T(8,128)(2,1)}, f16[512,512]{1,0:T(8,128)(2,1)}, u32[]{:S(2)}, u32[]{:S(2)}) %collective-permute-start.5) | collective-permute-done | bytes 524320 | tf_op jit(solution)/shard_map/ppermute | solution.py:166
  35.6 1.4 %multiply_add_fusion.1 = f32[512,512]{1,0:T(8,128)S(1)} fusion(f16[512,512]{1,0:T(8,128)(2,1)} %collective-permute-done.5, f32[512,512]{1,0:T(8,128)S(1)} %fusion.23, f16[512,512]{1,0:T(8,128)(2,1)} %copy-done.1), kind=kLoop, calls=%fused_computation.22 | loop fusion | flops 1572864 | bytes 3145728 | tf_op jit(solution)/shard_map/add | solution.py:174
  37.1 1.1 %shard_map.74 = s32[4]{0:T(128)} custom-call(s32[4]{0:T(128)} %bitcast.41), custom_call_target="tpu_custom_call" | custom-call | flops 99999997952 | bytes 1 | tf_op jit(solution)/shard_map/pallas_call | solution.py:109
  38.2 0.9 %convert_reduce_fusion = s32[4]{0:T(128)S(1)} fusion(s32[4]{0:T(128)} %shard_map.74), kind=kLoop, calls=%fused_computation.30 | loop fusion | flops 76 | bytes 32 | tf_op jit(solution)/shard_map/reduce_sum | solution.py:122
  39.1 0.7 %multiply_add_fusion.2 = s32[4]{0:T(128)S(1)} fusion(s32[4]{0:T(128)S(1)} %convert_reduce_fusion, s32[4]{0:T(128)} %shard_map.74), kind=kLoop, calls=%fused_computation.40 | loop fusion | flops 8 | bytes 48 | tf_op jit(solution)/shard_map/add | solution.py:122
  39.8 5.6 %all-to-all-done = bf16[8,2,16,2560]{3,2,1,0:T(8,128)(2,1)} async-done(((bf16[8,2,16,2560]{3,2,1,0:T(8,128)(2,1)}), bf16[8,2,16,2560]{3,2,1,0:T(8,128)(2,1)}, u32[]{:S(2)}, u32[]{:S(2)}) %all-to-all-start) | async-done | bytes 1310752 | tf_op jit(solution)/shard_map/all_to_all | solution.py:103
  45.4 1.9 %gather_fusion = bf16[4,16,2560]{2,1,0:T(8,128)(2,1)S(1)} fusion(bf16[16,16,2560]{2,1,0:T(8,128)(2,1)} %bitcast.9, s32[1024]{0:T(1024)S(1)} %pad_clamp_fusion), kind=kCustom, calls=%fused_computation | custom fusion | bytes 655376 | tf_op jit(solution)/shard_map/jit(_take)/gather | solution.py:127
  47.3 0.6 %fusion.43 = f32[4,16,128]{2,1,0:T(8,128)S(1)} fusion(bf16[4,16,2048]{2,1,0:T(8,128)(2,1)S(1)} %slice.10, bf16[4,128,2048]{2,1,0:T(8,128)(2,1)S(1)} %bitcast.39), kind=kOutput, calls=%fused_computation.42 | convolution fusion | flops 33554432 | bytes 2392064 | tf_op jit(solution)/shard_map/nbd,nrd->nrb/dot_general | solution.py:131
  47.9 0.1 collective-permute-start.7
  48.1 2.9 %collective-permute-start.8 = (f32[4,16,128]{2,1,0:T(8,128)S(1)}, f32[4,16,128]{2,1,0:T(8,128)S(1)}, u32[]{:S(2)}, u32[]{:S(2)}) collective-permute-start(f32[4,16,128]{2,1,0:T(8,128)S(1)} %fusion.43), channel_id=1, source_target_pairs={{0,2},{1,3},{2,0},{3,1},{4,6},{5,7},{6,4},{7,5},{8,10},{9,11},{10,... | collective-permute-start | bytes 98312 | tf_op jit(solution)/shard_map/ppermute | solution.py:186
  51.0 1.3 %collective-permute-start.9 = (f32[4,16,128]{2,1,0:T(8,128)S(1)}, f32[4,16,128]{2,1,0:T(8,128)S(1)}, u32[]{:S(2)}, u32[]{:S(2)}) collective-permute-start(f32[4,16,128]{2,1,0:T(8,128)S(1)} %fusion.43), channel_id=1, source_target_pairs={{0,3},{1,2},{2,1},{3,0},{4,7},{5,6},{6,5},{7,4},{8,11},{9,10},{10,... | collective-permute-start | bytes 98312 | tf_op jit(solution)/shard_map/ppermute | solution.py:186
  52.4 0.0 collective-permute-done.6
  52.4 1.2 %multiply_add_fusion = f32[512,512]{1,0:T(8,128)S(1)} fusion(f32[512,512]{1,0:T(8,128)S(1)} %multiply_add_fusion.1, f16[512,512]{1,0:T(8,128)(2,1)} %collective-permute-done.6), kind=kLoop, calls=%fused_computation.21 | loop fusion | flops 786432 | bytes 2621440 | tf_op jit(solution)/shard_map/add | solution.py:178
  53.6 0.0 collective-permute-done.7
  53.6 0.0 collective-permute-done.8
  53.6 3.1 %collective-permute-done.9 = f32[4,16,128]{2,1,0:T(8,128)S(1)} collective-permute-done((f32[4,16,128]{2,1,0:T(8,128)S(1)}, f32[4,16,128]{2,1,0:T(8,128)S(1)}, u32[]{:S(2)}, u32[]{:S(2)}) %collective-permute-start.9) | collective-permute-done | bytes 32800 | tf_op jit(solution)/shard_map/ppermute | solution.py:186
  56.7 0.6 %convolution_multiply_fusion = f32[4,128,512]{2,1,0:T(8,128)S(1)} fusion(bf16[4,16,512]{2,1,0:T(8,128)(2,1)S(1)} %slice.11, f32[4,16,128]{2,1,0:T(8,128)S(1)} %collective-permute-done.9, f32[4,16,128]{2,1,0:T(8,128)S(1)} %collective-permute-done.8, f32[4,16,128]{2,1,0:T(8,128)S(1)} %fusion.43, f32[4,16,128]{2,1,0:T(8,128)S(1)} %collective-permute-done.7), kind=kOutput, calls=%fused_computation.15 | convolution fusion | flops 50618368 | bytes 1245184 | tf_op jit(solution)/shard_map/nrb,nro->nbo/dot_general | solution.py:187
  57.4 1.0 %fusion.33 = bf16[512,512]{1,0:T(8,128)(2,1)} fusion(f32[512,512]{1,0:T(8,128)S(1)} %multiply_add_fusion, f32[4,128,512]{2,1,0:T(8,128)S(1)} %convolution_multiply_fusion, pred[512]{0:T(512)(128)(4,1)S(1)} %fusion.37), kind=kLoop, calls=%fused_computation.20 | loop fusion | flops 786432 | bytes 2621952 | tf_op jit(solution)/shard_map/convert_element_type | solution.py:191
  (5 shorter events, 0.1 us)
Async XLA Ops:
  0.0 2.0 %copy-start = (bf16[512,2048]{1,0:T(8,128)(2,1)S(1)}, bf16[512,2048]{1,0:T(8,128)(2,1)}, u32[]{:S(2)}) copy-start(bf16[512,2048]{1,0:T(8,128)(2,1)} %param.7) | copy-start | bytes 6291460
  0.8 4.8 %collective-permute-start = (s32[1,4]{1,0:T(1,128)S(1)}, s32[1,4]{1,0:T(1,128)S(1)}, u32[]{:S(2)}, u32[]{:S(2)}) collective-permute-start(s32[1,4]{1,0:T(1,128)S(1)} %add_bitcast_fusion), channel_id=1, source_target_pairs={{0,4},{4,0},{8,12},{12,8},{16,20},{20,16},{24,28},{28,24},{1,5},{5... | collective-permute-start | bytes 56 | tf_op jit(solution)/shard_map/ppermute | solution.py:74
  5.7 6.8 %collective-permute-start.1 = (s32[2,4]{1,0:T(2,128)S(1)}, s32[2,4]{1,0:T(2,128)S(1)}, u32[]{:S(2)}, u32[]{:S(2)}) collective-permute-start(s32[2,4]{1,0:T(2,128)S(1)} %pad_add_fusion.2), channel_id=1, source_target_pairs={{0,8},{4,12},{8,0},{12,4},{16,24},{20,28},{24,16},{28,20},{1,9},{5... | collective-permute-start | bytes 104 | tf_op jit(solution)/shard_map/ppermute | solution.py:74
  8.3 21.7 %collective-permute-start.3 = (f16[512,512]{1,0:T(8,128)(2,1)}, f16[512,512]{1,0:T(8,128)(2,1)S(1)}, u32[]{:S(2)}, u32[]{:S(2)}) collective-permute-start(f16[512,512]{1,0:T(8,128)(2,1)} %fusion.26), channel_id=1, source_target_pairs={{0,1},{3,2},{4,5},{7,6},{8,9},{11,10},{12,13},{15,14},{16,17},{19,... | collective-permute-start | bytes 1572872 | tf_op jit(solution)/shard_map/ppermute | solution.py:162
  11.8 22.2 %collective-permute-start.4 = (f16[512,512]{1,0:T(8,128)(2,1)}, f16[512,512]{1,0:T(8,128)(2,1)S(1)}, u32[]{:S(2)}, u32[]{:S(2)}) collective-permute-start(f16[512,512]{1,0:T(8,128)(2,1)} %fusion.26), channel_id=1, source_target_pairs={{1,2},{2,1},{5,6},{6,5},{9,10},{10,9},{13,14},{14,13},{17,18},{18,... | collective-permute-start | bytes 1572872 | tf_op jit(solution)/shard_map/ppermute | solution.py:163
  12.5 7.3 %collective-permute-start.2 = (s32[4,4]{1,0:T(4,128)S(1)}, s32[4,4]{1,0:T(4,128)S(1)}, u32[]{:S(2)}, u32[]{:S(2)}) collective-permute-start(s32[4,4]{1,0:T(4,128)S(1)} %pad_add_fusion.1), channel_id=1, source_target_pairs={{0,16},{4,20},{8,24},{12,28},{16,0},{20,4},{24,8},{28,12},{1,17},{... | collective-permute-start | bytes 200 | tf_op jit(solution)/shard_map/ppermute | solution.py:74
  17.8 17.9 %collective-permute-start.5 = (f16[512,512]{1,0:T(8,128)(2,1)}, f16[512,512]{1,0:T(8,128)(2,1)}, u32[]{:S(2)}, u32[]{:S(2)}) collective-permute-start(f16[512,512]{1,0:T(8,128)(2,1)} %fusion.29), channel_id=1, source_target_pairs={{0,2},{3,1},{1,0},{2,3},{4,6},{7,5},{5,4},{6,7},{8,10},{11,9},{9,8... | collective-permute-start | bytes 1572872 | tf_op jit(solution)/shard_map/ppermute | solution.py:166
  22.9 22.5 %all-to-all-start = ((bf16[8,2,16,2560]{3,2,1,0:T(8,128)(2,1)}), bf16[8,2,16,2560]{3,2,1,0:T(8,128)(2,1)}, u32[]{:S(2)}, u32[]{:S(2)}) async-start(bf16[8,2,16,2560]{3,2,1,0:T(8,128)(2,1)} %shard_map.73), calls=%async_computation | async-start | bytes 2621440 | tf_op jit(solution)/shard_map/all_to_all | solution.py:103
  31.0 21.3 %collective-permute-start.6 = (f16[512,512]{1,0:T(8,128)(2,1)}, f16[512,512]{1,0:T(8,128)(2,1)}, u32[]{:S(2)}, u32[]{:S(2)}) collective-permute-start(f16[512,512]{1,0:T(8,128)(2,1)} %multiply_convert_fusion), channel_id=1, source_target_pairs={{0,1},{3,2},{1,3},{2,0},{4,5},{7,6},{5,7},{6,4},{8,9},{11,10},{9,1... | collective-permute-start | bytes 1572872 | tf_op jit(solution)/shard_map/ppermute | solution.py:172
  34.0 0.8 %copy-start.1 = (f16[512,512]{1,0:T(8,128)(2,1)}, f16[512,512]{1,0:T(8,128)(2,1)S(1)}, u32[]{:S(2)}) copy-start(f16[512,512]{1,0:T(8,128)(2,1)S(1)} %collective-permute-done.4) | copy-start | bytes 1572868
  47.9 5.7 %collective-permute-start.7 = (f32[4,16,128]{2,1,0:T(8,128)S(1)}, f32[4,16,128]{2,1,0:T(8,128)S(1)}, u32[]{:S(2)}, u32[]{:S(2)}) collective-permute-start(f32[4,16,128]{2,1,0:T(8,128)S(1)} %fusion.43), channel_id=1, source_target_pairs={{0,1},{1,0},{2,3},{3,2},{4,5},{5,4},{6,7},{7,6},{8,9},{9,8},{10,11... | collective-permute-start | bytes 98312 | tf_op jit(solution)/shard_map/ppermute | solution.py:186
  48.1 5.5 %collective-permute-start.8 = (f32[4,16,128]{2,1,0:T(8,128)S(1)}, f32[4,16,128]{2,1,0:T(8,128)S(1)}, u32[]{:S(2)}, u32[]{:S(2)}) collective-permute-start(f32[4,16,128]{2,1,0:T(8,128)S(1)} %fusion.43), channel_id=1, source_target_pairs={{0,2},{1,3},{2,0},{3,1},{4,6},{5,7},{6,4},{7,5},{8,10},{9,11},{10,... | collective-permute-start | bytes 98312 | tf_op jit(solution)/shard_map/ppermute | solution.py:186
  51.0 5.7 %collective-permute-start.9 = (f32[4,16,128]{2,1,0:T(8,128)S(1)}, f32[4,16,128]{2,1,0:T(8,128)S(1)}, u32[]{:S(2)}, u32[]{:S(2)}) collective-permute-start(f32[4,16,128]{2,1,0:T(8,128)S(1)} %fusion.43), channel_id=1, source_target_pairs={{0,3},{1,2},{2,1},{3,0},{4,7},{5,6},{6,5},{7,4},{8,11},{9,10},{10,... | collective-permute-start | bytes 98312 | tf_op jit(solution)/shard_map/ppermute | solution.py:186

commit v4 on v3

--- a/solution.py
+++ b/solution.py
@@ -138,8 +138,6 @@
     z = lax.axis_index("tp")
     width = base_weight.shape[1] // tp_count
     owners = block_owner[:, 0]
-    offsets = jnp.arange(BLOCK, dtype=jnp.int32)
-    live_rows = (offsets[None, :] < block_count[:, None]).reshape(tokens.shape[0], 1)
 
     def product(block):
         columns = lax.dynamic_slice_in_dim(base_weight, block * width, width, 1)
@@ -156,6 +154,7 @@
         return lax.optimization_barrier((value, *others))[0]
 
     id_steps = list(adapter_ids(block_owner, block_local, down_tables.shape[0]))
+    live_counts = block_count
     if tp_count == 4:
         end = (z == 0) | (z == 3)
         far = after(code(product(z ^ 3)), id_steps[0])
@@ -171,6 +170,7 @@
         second = code(second + plain(to_inner))
         from_second = lax.ppermute(second, "tp", [(0, 1), (3, 2), (1, 3), (2, 0)])
         own = lax.optimization_barrier(product(after(z, second)))
+        live_counts = after(block_count, own)
         base_projection = lax.optimization_barrier(own + plain(from_inner) + plain(from_first))
         block_slot = slot_plan(later(owners, base_projection))
         reduced, up_block = reduce_tokens(tokens, got, block_slot)
@@ -187,8 +187,11 @@
     lowrank = jnp.einsum(
         "nrb,nro->nbo", total, up_block.astype(jnp.float32), precision=lax.Precision.HIGHEST
     )
-    combined_output = base_projection + adapter_scale * lowrank.reshape(base_projection.shape)
-    return jnp.where(live_rows, combined_output, jnp.float32(0.0)).astype(jnp.bfloat16)
+    offsets = jnp.arange(BLOCK, dtype=jnp.int32)
+    live_rows = offsets[None, :, None] < live_counts[:, None, None]
+    combined_output = base_projection.reshape(lowrank.shape) + adapter_scale * lowrank
+    projected = jnp.where(live_rows, combined_output, jnp.float32(0.0)).astype(jnp.bfloat16)
+    return projected.reshape(base_projection.shape)
 
 
 def solution(mesh):

time: 58.9 us -> 58.4 us (level)
  waiting for transfers between devices: 9.51 us -> 6.16 us
  starting transfers between devices: 19.7 us -> 22.7 us
  other arithmetic: 8.38 us -> 6.79 us
  matrix products: 14.2 us -> 15.1 us
    ppermute x1, starting transfers between devices: 3.5 us -> 6.3 us  [body(): to_inner = lax.ppermute(far, 'tp', [(0, 1), (3, 2)])]
    all_to_all x1, waiting for transfers between devices: 5.6 us -> 3.03 us  [exchange(): got = lax.all_to_all(packed, 'grp', split_axis=0, concat_axis=0, tiled=True)]
    ppermute x1, starting transfers between devices: 2.03 us -> 0.01 us  [body(): from_first = lax.ppermute(first, 'tp', [(0, 2), (3, 1), (1, 0), (2, 3)])]
    ppermute x1, starting transfers between devices: 0.13 us -> 2.04 us  [body(): from_second = lax.ppermute(second, 'tp', [(0, 1), (3, 2), (1, 3), (2, 0)])]
    ppermute x3, waiting for transfers between devices: 3.1 us -> 1.78 us  [body(): lax.ppermute(reduced, 'tp', [(i, i ^ j) for i in range(tp_count)])]
    convert_element_type x1 -> x0, other arithmetic: 0.95 us -> none  [body(): jnp.where(live_rows, combined_output, jnp.float32(0.0)).astype(jnp.bfloat16)]
    dot_general x1, matrix products: 0.63 us -> 1.46 us  [body(): jnp.einsum('nrb,nro->nbo', total, up_block.astype(jnp.float32), precision...]
    lt x1, other arithmetic: 0.73 us -> 0.07 us  [body(): live_rows = offsets[None, :, None] < live_counts[:, None, None]]
  transfers between devices with their start and end apart: 11 -> 11, of which waited for: 3 -> 5; matrix products, arithmetic and copies ran while one was open for 38% -> 37% of each run, Pallas kernels for 6% -> 7%
where the time goes in v4:
time: 58.4 us; the launch traced here: 57.9 us
  starting transfers between devices  22.7 us (39%)
  matrix products  15.1 us (26%)
  other arithmetic  6.79 us (12%)
  waiting for transfers between devices  6.16 us (11%)
  Pallas kernels  3.88 us (7%)
  local copies, waits for them, and re-layouts  3.07 us (5%)
    dot_general x4, matrix products, product(): value = jnp.dot(tokens, columns, preferred_element_type=jnp.float32)  13 us
    ppermute x1, starting transfers between devices, body(): to_inner = lax.ppermute(far, 'tp', [(0, 1), (3, 2)])  6.3 us
    ppermute x3, starting transfers between devices, adapter_ids(): lax.ppermute(ids, 'grp', [(i, i ^ step) for i in range(group_count)])  5.04 us
    ppermute x3, starting transfers between devices, body(): lax.ppermute(reduced, 'tp', [(i, i ^ j) for i in range(tp_count)])  4.4 us
    all_to_all x1, starting transfers between devices, exchange(): got = lax.all_to_all(packed, 'grp', split_axis=0, concat_axis=0, tiled=True)  4.27 us
    all_to_all x1, waiting for transfers between devices, exchange(): got = lax.all_to_all(packed, 'grp', split_axis=0, concat_axis=0, tiled=True)  3.03 us
    pallas_call x1, Pallas kernels, pack_adapters(): pl.pallas_call(pack_kernel, out_shape=jax.ShapeDtypeStruct((group_count,...  2.75 us
    ppermute x1, starting transfers between devices, body(): from_second = lax.ppermute(second, 'tp', [(0, 1), (3, 2), (1, 3), (2, 0)])  2.04 us
  transfers between devices with their start and end apart: 11, of which 5 were waited for; matrix products, arithmetic and copies ran while one was open for 37% of the time, Pallas kernels for 7%

profile of v4, /device:TPU:0, one launch (start us, length us, event | category | flops | bytes accessed | tf_op | source)
XLA Modules:
  0.0 57.9 jit_solution(10076294580901989390)
XLA Ops:
  0.0 0.0 copy-start
  0.0 0.8 %add_bitcast_fusion = s32[1,4]{1,0:T(1,128)S(1)} fusion(s32[4]{0:T(128)} %param.12, s32[4,1]{0,1:T(1,128)} %param.11), kind=kLoop, calls=%fused_computation.40 | loop fusion | flops 8 | bytes 48 | tf_op jit(solution)/shard_map/reshape | solution.py:71
  0.8 0.5 collective-permute-start
  1.3 0.3 copy-done
  1.6 3.7 %fusion.29 = f16[512,512]{1,0:T(8,128)(2,1)} fusion(bf16[512,2048]{1,0:T(8,128)(2,1)S(1)} %copy-done, bf16[2048,2048]{1,0:T(8,128)(2,1)} %param.8, s32[]{:T(128)S(6)} %select_n.27), kind=kOutput, calls=%fused_computation.19 | convolution fusion | flops 1074266112 | bytes 4718596 | tf_op jit(solution)/shard_map/dot_general | solution.py:144
  5.3 0.0 collective-permute-done
  5.3 3.0 %collective-permute-start.1 = (s32[2,4]{1,0:T(2,128)S(1)}, s32[2,4]{1,0:T(2,128)S(1)}, u32[]{:S(2)}, u32[]{:S(2)}) collective-permute-start(s32[2,4]{1,0:T(2,128)S(1)} %pad_add_fusion.2), channel_id=1, source_target_pairs={{0,8},{4,12},{8,0},{12,4},{16,24},{20,28},{24,16},{28,20},{1,9},{5... | collective-permute-start | bytes 104 | tf_op jit(solution)/shard_map/ppermute | solution.py:74
  8.3 0.7 %collective-permute-start.4 = (f16[512,512]{1,0:T(8,128)(2,1)}, f16[512,512]{1,0:T(8,128)(2,1)S(1)}, u32[]{:S(2)}, u32[]{:S(2)}) collective-permute-start(f16[512,512]{1,0:T(8,128)(2,1)} %fusion.29), channel_id=1, source_target_pairs={{1,2},{2,1},{5,6},{6,5},{9,10},{10,9},{13,14},{14,13},{17,18},{18,... | collective-permute-start | bytes 1572872 | tf_op jit(solution)/shard_map/ppermute | solution.py:162
  9.0 6.3 %collective-permute-start.3 = (f16[512,512]{1,0:T(8,128)(2,1)}, f16[512,512]{1,0:T(8,128)(2,1)S(1)}, u32[]{:S(2)}, u32[]{:S(2)}) collective-permute-start(f16[512,512]{1,0:T(8,128)(2,1)} %fusion.29), channel_id=1, source_target_pairs={{0,1},{3,2},{4,5},{7,6},{8,9},{11,10},{12,13},{15,14},{16,17},{19,... | collective-permute-start | bytes 1572872 | tf_op jit(solution)/shard_map/ppermute | solution.py:161
  15.3 0.0 collective-permute-done.1
  15.3 1.6 %collective-permute-start.2 = (s32[4,4]{1,0:T(4,128)S(1)}, s32[4,4]{1,0:T(4,128)S(1)}, u32[]{:S(2)}, u32[]{:S(2)}) collective-permute-start(s32[4,4]{1,0:T(4,128)S(1)} %pad_add_fusion.1), channel_id=1, source_target_pairs={{0,16},{4,20},{8,24},{12,28},{16,0},{20,4},{24,8},{28,12},{1,17},{... | collective-permute-start | bytes 200 | tf_op jit(solution)/shard_map/ppermute | solution.py:74
  16.9 3.6 %fusion.32 = f16[512,512]{1,0:T(8,128)(2,1)} fusion(bf16[512,2048]{1,0:T(8,128)(2,1)S(1)} %copy-done, bf16[2048,2048]{1,0:T(8,128)(2,1)} %param.8, s32[]{:T(128)S(6)} %select_n.24), kind=kOutput, calls=%fused_computation.20 | convolution fusion | flops 1074266112 | bytes 4718596 | tf_op jit(solution)/shard_map/dot_general | solution.py:144
  20.6 0.0 collective-permute-start.5
  20.6 0.0 collective-permute-done.2
  20.6 0.6 %pad_add_fusion.ids_ref = s32[8,4]{1,0:T(8,128)} fusion(s32[4,4]{1,0:T(4,128)S(1)} %collective-permute-done.2, s32[2,4]{1,0:T(2,128)S(1)} %collective-permute-done.1, s32[1,4]{1,0:T(1,128)S(1)} %collective-permute-done, s32[1,4]{1,0:T(1,128)S(1)} %add_bitcast_fusion), kind=kLoop, calls=%fused_computation.28 | loop fusion | flops 96 | bytes 256 | tf_op jit(solution)/shard_map/concatenate | solution.py:75
  21.2 2.8 %shard_map.73 = bf16[8,2,16,2560]{3,2,1,0:T(8,128)(2,1)} custom-call(s32[8,4]{1,0:T(8,128)} %pad_add_fusion.ids_ref, s32[1]{0:T(128)} %bitcast.3.me_ref, bf16[128,16,2048]{2,1,0:T(8,128)(2,1)} %bitcast.34, bf16[128,16,512]{2,1,0:T(8,128)(2,1)} %up_ref.1), custom_call_target="tpu_custom_call" | custom-call | flops 1 | bytes 1 | tf_op jit(solution)/shard_map/pallas_call | solution.py:85
  23.9 4.3 %all-to-all-start = ((bf16[8,2,16,2560]{3,2,1,0:T(8,128)(2,1)}), bf16[8,2,16,2560]{3,2,1,0:T(8,128)(2,1)}, u32[]{:S(2)}, u32[]{:S(2)}) async-start(bf16[8,2,16,2560]{3,2,1,0:T(8,128)(2,1)} %shard_map.73), calls=%async_computation | async-start | bytes 2621440 | tf_op jit(solution)/shard_map/all_to_all | solution.py:103
  28.2 2.8 %fusion.14 = f32[512,512]{1,0:T(8,128)S(1)} fusion(bf16[512,2048]{1,0:T(8,128)(2,1)S(1)} %copy-done, bf16[2048,2048]{1,0:T(8,128)(2,1)} %param.8, s32[]{:T(128)S(6)} %select_n.26), kind=kOutput, calls=%fused_computation.11 | convolution fusion | flops 1073741824 | bytes 5242884 | tf_op jit(solution)/shard_map/dot_general | solution.py:144
  31.1 0.0 collective-permute-done.3
  31.1 1.0 %multiply_convert_fusion = f16[512,512]{1,0:T(8,128)(2,1)} fusion(f32[512,512]{1,0:T(8,128)S(1)} %fusion.14, f16[512,512]{1,0:T(8,128)(2,1)S(1)} %collective-permute-done.3), kind=kLoop, calls=%fused_computation.23 | loop fusion | flops 1310720 | bytes 2097152 | tf_op jit(solution)/shard_map/convert_element_type | solution.py:148
  32.1 2.0 %collective-permute-start.6 = (f16[512,512]{1,0:T(8,128)(2,1)}, f16[512,512]{1,0:T(8,128)(2,1)}, u32[]{:S(2)}, u32[]{:S(2)}) collective-permute-start(f16[512,512]{1,0:T(8,128)(2,1)} %multiply_convert_fusion), channel_id=1, source_target_pairs={{0,1},{3,2},{1,3},{2,0},{4,5},{7,6},{5,7},{6,4},{8,9},{11,10},{9,1... | collective-permute-start | bytes 1572872 | tf_op jit(solution)/shard_map/ppermute | solution.py:171
  34.1 0.0 copy-start.2
  34.1 2.8 %fusion.23 = f32[512,512]{1,0:T(8,128)S(1)} fusion(bf16[512,2048]{1,0:T(8,128)(2,1)S(1)} %copy-done, bf16[2048,2048]{1,0:T(8,128)(2,1)} %param.8, s32[]{:T(128)S(6)} %select_n.28), kind=kOutput, calls=%fused_computation.14 | convolution fusion | flops 1073741824 | bytes 5242884 | tf_op jit(solution)/shard_map/dot_general | solution.py:144
  37.0 0.0 copy-done.2
  37.0 0.1 iota_compare_fusion.1
  37.1 0.0 collective-permute-done.4
  37.1 0.0 copy-start.1
  37.1 0.8 %copy-done.1 = f16[512,512]{1,0:T(8,128)(2,1)} copy-done((f16[512,512]{1,0:T(8,128)(2,1)}, f16[512,512]{1,0:T(8,128)(2,1)S(1)}, u32[]{:S(2)}) %copy-start.1) | copy-done | bytes 524312
  37.9 1.3 %collective-permute-done.5 = f16[512,512]{1,0:T(8,128)(2,1)} collective-permute-done((f16[512,512]{1,0:T(8,128)(2,1)}, f16[512,512]{1,0:T(8,128)(2,1)}, u32[]{:S(2)}, u32[]{:S(2)}) %collective-permute-start.5) | collective-permute-done | bytes 524320 | tf_op jit(solution)/shard_map/ppermute | solution.py:165
  39.2 1.5 %multiply_add_fusion.1 = f32[512,512]{1,0:T(8,128)S(1)} fusion(f16[512,512]{1,0:T(8,128)(2,1)} %collective-permute-done.5, f32[512,512]{1,0:T(8,128)S(1)} %fusion.23, f16[512,512]{1,0:T(8,128)(2,1)} %copy-done.1), kind=kLoop, calls=%fused_computation.22 | loop fusion | flops 1572864 | bytes 3145728 | tf_op jit(solution)/shard_map/add | solution.py:174
  40.7 1.1 %shard_map.74 = s32[4]{0:T(128)} custom-call(s32[4]{0:T(128)} %bitcast.36), custom_call_target="tpu_custom_call" | custom-call | flops 99999997952 | bytes 1 | tf_op jit(solution)/shard_map/pallas_call | solution.py:109
  41.8 0.9 %convert_reduce_fusion = s32[4]{0:T(128)S(1)} fusion(s32[4]{0:T(128)} %shard_map.74), kind=kLoop, calls=%fused_computation.30 | loop fusion | flops 76 | bytes 32 | tf_op jit(solution)/shard_map/reduce_sum | solution.py:122
  42.7 0.7 %multiply_add_fusion.2 = s32[4]{0:T(128)S(1)} fusion(s32[4]{0:T(128)S(1)} %convert_reduce_fusion, s32[4]{0:T(128)} %shard_map.74), kind=kLoop, calls=%fused_computation.39 | loop fusion | flops 8 | bytes 48 | tf_op jit(solution)/shard_map/add | solution.py:122
  43.4 3.0 %all-to-all-done = bf16[8,2,16,2560]{3,2,1,0:T(8,128)(2,1)} async-done(((bf16[8,2,16,2560]{3,2,1,0:T(8,128)(2,1)}), bf16[8,2,16,2560]{3,2,1,0:T(8,128)(2,1)}, u32[]{:S(2)}, u32[]{:S(2)}) %all-to-all-start) | async-done | bytes 1310752 | tf_op jit(solution)/shard_map/all_to_all | solution.py:103
  46.4 1.9 %gather_fusion = bf16[4,16,2560]{2,1,0:T(8,128)(2,1)S(1)} fusion(bf16[16,16,2560]{2,1,0:T(8,128)(2,1)} %bitcast.8, s32[1024]{0:T(1024)S(1)} %pad_clamp_fusion), kind=kCustom, calls=%fused_computation | custom fusion | bytes 655376 | tf_op jit(solution)/shard_map/jit(_take)/gather | solution.py:127
  48.4 0.6 %fusion.43 = f32[4,16,128]{2,1,0:T(8,128)S(1)} fusion(bf16[4,16,2048]{2,1,0:T(8,128)(2,1)S(1)} %slice.10, bf16[4,128,2048]{2,1,0:T(8,128)(2,1)S(1)} %bitcast.33), kind=kOutput, calls=%fused_computation.41 | convolution fusion | flops 33554432 | bytes 2392064 | tf_op jit(solution)/shard_map/nbd,nrd->nrb/dot_general | solution.py:131
  49.0 1.7 %collective-permute-start.9 = (f32[4,16,128]{2,1,0:T(8,128)S(1)}, f32[4,16,128]{2,1,0:T(8,128)S(1)}, u32[]{:S(2)}, u32[]{:S(2)}) collective-permute-start(f32[4,16,128]{2,1,0:T(8,128)S(1)} %fusion.43), channel_id=1, source_target_pairs={{0,3},{1,2},{2,1},{3,0},{4,7},{5,6},{6,5},{7,4},{8,11},{9,10},{10,... | collective-permute-start | bytes 98312 | tf_op jit(solution)/shard_map/ppermute | solution.py:186
  50.7 1.8 %collective-permute-start.8 = (f32[4,16,128]{2,1,0:T(8,128)S(1)}, f32[4,16,128]{2,1,0:T(8,128)S(1)}, u32[]{:S(2)}, u32[]{:S(2)}) collective-permute-start(f32[4,16,128]{2,1,0:T(8,128)S(1)} %fusion.43), channel_id=1, source_target_pairs={{0,2},{1,3},{2,0},{3,1},{4,6},{5,7},{6,4},{7,5},{8,10},{9,11},{10,... | collective-permute-start | bytes 98312 | tf_op jit(solution)/shard_map/ppermute | solution.py:186
  52.5 0.9 %collective-permute-start.7 = (f32[4,16,128]{2,1,0:T(8,128)S(1)}, f32[4,16,128]{2,1,0:T(8,128)S(1)}, u32[]{:S(2)}, u32[]{:S(2)}) collective-permute-start(f32[4,16,128]{2,1,0:T(8,128)S(1)} %fusion.43), channel_id=1, source_target_pairs={{0,1},{1,0},{2,3},{3,2},{4,5},{5,4},{6,7},{7,6},{8,9},{9,8},{10,11... | collective-permute-start | bytes 98312 | tf_op jit(solution)/shard_map/ppermute | solution.py:186
  53.4 0.0 collective-permute-done.6
  53.4 1.2 %multiply_add_fusion = f32[512,512]{1,0:T(8,128)S(1)} fusion(f32[512,512]{1,0:T(8,128)S(1)} %multiply_add_fusion.1, f16[512,512]{1,0:T(8,128)(2,1)} %collective-permute-done.6), kind=kLoop, calls=%fused_computation.21 | loop fusion | flops 786432 | bytes 2621440 | tf_op jit(solution)/shard_map/add | solution.py:178
  54.6 0.1 collective-permute-done.9
  54.7 1.2 %collective-permute-done.8 = f32[4,16,128]{2,1,0:T(8,128)S(1)} collective-permute-done((f32[4,16,128]{2,1,0:T(8,128)S(1)}, f32[4,16,128]{2,1,0:T(8,128)S(1)}, u32[]{:S(2)}, u32[]{:S(2)}) %collective-permute-start.8) | collective-permute-done | bytes 32800 | tf_op jit(solution)/shard_map/ppermute | solution.py:186
  55.9 0.5 collective-permute-done.7
  56.4 1.5 %fusion.28 = bf16[4,128,512]{2,1,0:T(8,128)(2,1)} fusion(f32[4,128,512]{2,1,0:T(8,128)S(1)} %bitcast.35, bf16[4,16,512]{2,1,0:T(8,128)(2,1)S(1)} %slice.11, pred[4,128]{1,0:T(4,128)(4,1)S(1)} %iota_compare_fusion.1, f32[4,16,128]{2,1,0:T(8,128)S(1)} %collective-permute-done.9, f32[4,16,128]{2,1,0:T(8,128)S(1)} %collective-permute-done.8, ...), kind=kOutput, calls=%fused_computation.18 | convolution fusion | flops 51404800 | bytes 1769984 | tf_op jit(solution)/shard_map/nrb,nro->nbo/dot_general | solution.py:187
  (5 shorter events, 0.1 us)
Async XLA Ops:
  0.0 1.6 %copy-start = (bf16[512,2048]{1,0:T(8,128)(2,1)S(1)}, bf16[512,2048]{1,0:T(8,128)(2,1)}, u32[]{:S(2)}) copy-start(bf16[512,2048]{1,0:T(8,128)(2,1)} %param.7) | copy-start | bytes 6291460
  0.8 4.5 %collective-permute-start = (s32[1,4]{1,0:T(1,128)S(1)}, s32[1,4]{1,0:T(1,128)S(1)}, u32[]{:S(2)}, u32[]{:S(2)}) collective-permute-start(s32[1,4]{1,0:T(1,128)S(1)} %add_bitcast_fusion), channel_id=1, source_target_pairs={{0,4},{4,0},{8,12},{12,8},{16,20},{20,16},{24,28},{28,24},{1,5},{5... | collective-permute-start | bytes 56 | tf_op jit(solution)/shard_map/ppermute | solution.py:74
  5.3 10.0 %collective-permute-start.1 = (s32[2,4]{1,0:T(2,128)S(1)}, s32[2,4]{1,0:T(2,128)S(1)}, u32[]{:S(2)}, u32[]{:S(2)}) collective-permute-start(s32[2,4]{1,0:T(2,128)S(1)} %pad_add_fusion.2), channel_id=1, source_target_pairs={{0,8},{4,12},{8,0},{12,4},{16,24},{20,28},{24,16},{28,20},{1,9},{5... | collective-permute-start | bytes 104 | tf_op jit(solution)/shard_map/ppermute | solution.py:74
  8.3 28.8 %collective-permute-start.4 = (f16[512,512]{1,0:T(8,128)(2,1)}, f16[512,512]{1,0:T(8,128)(2,1)S(1)}, u32[]{:S(2)}, u32[]{:S(2)}) collective-permute-start(f16[512,512]{1,0:T(8,128)(2,1)} %fusion.29), channel_id=1, source_target_pairs={{1,2},{2,1},{5,6},{6,5},{9,10},{10,9},{13,14},{14,13},{17,18},{18,... | collective-permute-start | bytes 1572872 | tf_op jit(solution)/shard_map/ppermute | solution.py:162
  9.0 22.1 %collective-permute-start.3 = (f16[512,512]{1,0:T(8,128)(2,1)}, f16[512,512]{1,0:T(8,128)(2,1)S(1)}, u32[]{:S(2)}, u32[]{:S(2)}) collective-permute-start(f16[512,512]{1,0:T(8,128)(2,1)} %fusion.29), channel_id=1, source_target_pairs={{0,1},{3,2},{4,5},{7,6},{8,9},{11,10},{12,13},{15,14},{16,17},{19,... | collective-permute-start | bytes 1572872 | tf_op jit(solution)/shard_map/ppermute | solution.py:161
  15.3 5.2 %collective-permute-start.2 = (s32[4,4]{1,0:T(4,128)S(1)}, s32[4,4]{1,0:T(4,128)S(1)}, u32[]{:S(2)}, u32[]{:S(2)}) collective-permute-start(s32[4,4]{1,0:T(4,128)S(1)} %pad_add_fusion.1), channel_id=1, source_target_pairs={{0,16},{4,20},{8,24},{12,28},{16,0},{20,4},{24,8},{28,12},{1,17},{... | collective-permute-start | bytes 200 | tf_op jit(solution)/shard_map/ppermute | solution.py:74
  20.6 18.7 %collective-permute-start.5 = (f16[512,512]{1,0:T(8,128)(2,1)}, f16[512,512]{1,0:T(8,128)(2,1)}, u32[]{:S(2)}, u32[]{:S(2)}) collective-permute-start(f16[512,512]{1,0:T(8,128)(2,1)} %fusion.32), channel_id=1, source_target_pairs={{0,2},{3,1},{1,0},{2,3},{4,6},{7,5},{5,4},{6,7},{8,10},{11,9},{9,8... | collective-permute-start | bytes 1572872 | tf_op jit(solution)/shard_map/ppermute | solution.py:165
  23.9 22.5 %all-to-all-start = ((bf16[8,2,16,2560]{3,2,1,0:T(8,128)(2,1)}), bf16[8,2,16,2560]{3,2,1,0:T(8,128)(2,1)}, u32[]{:S(2)}, u32[]{:S(2)}) async-start(bf16[8,2,16,2560]{3,2,1,0:T(8,128)(2,1)} %shard_map.73), calls=%async_computation | async-start | bytes 2621440 | tf_op jit(solution)/shard_map/all_to_all | solution.py:103
  32.1 21.3 %collective-permute-start.6 = (f16[512,512]{1,0:T(8,128)(2,1)}, f16[512,512]{1,0:T(8,128)(2,1)}, u32[]{:S(2)}, u32[]{:S(2)}) collective-permute-start(f16[512,512]{1,0:T(8,128)(2,1)} %multiply_convert_fusion), channel_id=1, source_target_pairs={{0,1},{3,2},{1,3},{2,0},{4,5},{7,6},{5,7},{6,4},{8,9},{11,10},{9,1... | collective-permute-start | bytes 1572872 | tf_op jit(solution)/shard_map/ppermute | solution.py:171
  34.1 2.9 %copy-start.2 = (s32[4]{0:T(128)S(1)}, s32[4]{0:T(128)}, u32[]{:S(2)}) copy-start(s32[4]{0:T(128)} %param.13) | copy-start | bytes 52
  37.1 0.8 %copy-start.1 = (f16[512,512]{1,0:T(8,128)(2,1)}, f16[512,512]{1,0:T(8,128)(2,1)S(1)}, u32[]{:S(2)}) copy-start(f16[512,512]{1,0:T(8,128)(2,1)S(1)} %collective-permute-done.4) | copy-start | bytes 1572868
  49.0 5.7 %collective-permute-start.9 = (f32[4,16,128]{2,1,0:T(8,128)S(1)}, f32[4,16,128]{2,1,0:T(8,128)S(1)}, u32[]{:S(2)}, u32[]{:S(2)}) collective-permute-start(f32[4,16,128]{2,1,0:T(8,128)S(1)} %fusion.43), channel_id=1, source_target_pairs={{0,3},{1,2},{2,1},{3,0},{4,7},{5,6},{6,5},{7,4},{8,11},{9,10},{10,... | collective-permute-start | bytes 98312 | tf_op jit(solution)/shard_map/ppermute | solution.py:186
  50.7 5.2 %collective-permute-start.8 = (f32[4,16,128]{2,1,0:T(8,128)S(1)}, f32[4,16,128]{2,1,0:T(8,128)S(1)}, u32[]{:S(2)}, u32[]{:S(2)}) collective-permute-start(f32[4,16,128]{2,1,0:T(8,128)S(1)} %fusion.43), channel_id=1, source_target_pairs={{0,2},{1,3},{2,0},{3,1},{4,6},{5,7},{6,4},{7,5},{8,10},{9,11},{10,... | collective-permute-start | bytes 98312 | tf_op jit(solution)/shard_map/ppermute | solution.py:186
  52.5 3.9 %collective-permute-start.7 = (f32[4,16,128]{2,1,0:T(8,128)S(1)}, f32[4,16,128]{2,1,0:T(8,128)S(1)}, u32[]{:S(2)}, u32[]{:S(2)}) collective-permute-start(f32[4,16,128]{2,1,0:T(8,128)S(1)} %fusion.43), channel_id=1, source_target_pairs={{0,1},{1,0},{2,3},{3,2},{4,5},{5,4},{6,7},{7,6},{8,9},{9,8},{10,11... | collective-permute-start | bytes 98312 | tf_op jit(solution)/shard_map/ppermute | solution.py:186

commit v5 on v4

--- a/solution.py
+++ b/solution.py
@@ -171,11 +171,11 @@
         from_second = lax.ppermute(second, "tp", [(0, 1), (3, 2), (1, 3), (2, 0)])
         own = lax.optimization_barrier(product(after(z, second)))
         live_counts = after(block_count, own)
-        base_projection = lax.optimization_barrier(own + plain(from_inner) + plain(from_first))
+        base_projection = lax.optimization_barrier(own + plain(from_first))
         block_slot = slot_plan(later(owners, base_projection))
         reduced, up_block = reduce_tokens(tokens, got, block_slot)
         from_second = after(from_second, reduced)
-        base_projection = lax.optimization_barrier(base_projection + plain(from_second))
+        base_projection = lax.optimization_barrier(base_projection + plain(from_inner) + plain(from_second))
     else:
         partial_value = jnp.dot(tokens, base_weight, preferred_element_type=jnp.float32)
         base_projection = lax.psum_scatter(partial_value, "tp", scatter_dimension=1, tiled=True)

time: 58.4 us -> 56.6 us (0.969)
  waiting for transfers between devices: 6.16 us -> 8.16 us
  starting transfers between devices: 22.7 us -> 20.8 us
  local copies, waits for them, and re-layouts: 3.07 us -> 2.26 us
  matrix products: 15.1 us -> 14.3 us
    ppermute x1, starting transfers between devices: 6.3 us -> 3.5 us  [body(): to_inner = lax.ppermute(far, 'tp', [(0, 1), (3, 2)])]
    all_to_all x1, waiting for transfers between devices: 3.03 us -> 5.23 us  [exchange(): got = lax.all_to_all(packed, 'grp', split_axis=0, concat_axis=0, tiled=True)]
    ppermute x1, starting transfers between devices: 0.01 us -> 1.33 us  [body(): from_first = lax.ppermute(first, 'tp', [(0, 2), (3, 1), (1, 0), (2, 3)])]
    ppermute x1, starting transfers between devices: 2.04 us -> 0.77 us  [body(): from_second = lax.ppermute(second, 'tp', [(0, 1), (3, 2), (1, 3), (2, 0)])]
    unnamed x6 -> x4, local copies, waits for them, and re-layouts: 1.16 us -> 0.35 us
    dot_general x4, matrix products: 13 us -> 12.2 us  [product(): value = jnp.dot(tokens, columns, preferred_element_type=jnp.float32)]
    ppermute x1, starting transfers between devices: 0.68 us -> 1.47 us  [body(): from_inner = lax.ppermute(far, 'tp', [(1, 2), (2, 1)])]
  transfers between devices with their start and end apart: 11 -> 11, of which waited for: 5 -> 3; matrix products, arithmetic and copies ran while one was open for 37% -> 37% of each run, Pallas kernels for 7% -> 7%
where the time goes in v5:
time: 56.6 us; the launch traced here: 56 us
  starting transfers between devices  20.8 us (37%)
  matrix products  14.3 us (25%)
  waiting for transfers between devices  8.16 us (14%)
  other arithmetic  6.76 us (12%)
  Pallas kernels  3.69 us (7%)
  local copies, waits for them, and re-layouts  2.26 us (4%)
    dot_general x4, matrix products, product(): value = jnp.dot(tokens, columns, preferred_element_type=jnp.float32)  12.2 us
    all_to_all x1, waiting for transfers between devices, exchange(): got = lax.all_to_all(packed, 'grp', split_axis=0, concat_axis=0, tiled=True)  5.23 us
    ppermute x3, starting transfers between devices, adapter_ids(): lax.ppermute(ids, 'grp', [(i, i ^ step) for i in range(group_count)])  5.04 us
    ppermute x3, starting transfers between devices, body(): lax.ppermute(reduced, 'tp', [(i, i ^ j) for i in range(tp_count)])  4.4 us
    all_to_all x1, starting transfers between devices, exchange(): got = lax.all_to_all(packed, 'grp', split_axis=0, concat_axis=0, tiled=True)  4.26 us
    ppermute x1, starting transfers between devices, body(): to_inner = lax.ppermute(far, 'tp', [(0, 1), (3, 2)])  3.5 us
    pallas_call x1, Pallas kernels, pack_adapters(): pl.pallas_call(pack_kernel, out_shape=jax.ShapeDtypeStruct((group_count,...  2.56 us
    gather x1, local copies, waits for them, and re-layouts, reduce_tokens(): mine = jnp.take(got, block_slot, axis=0, mode='clip')  1.88 us
  transfers between devices with their start and end apart: 11, of which 3 were waited for; matrix products, arithmetic and copies ran while one was open for 37% of the time, Pallas kernels for 7%

profile of v5, /device:TPU:0, one launch (start us, length us, event | category | flops | bytes accessed | tf_op | source)
XLA Modules:
  0.0 56.0 jit_solution(8461427429884585365)
XLA Ops:
  0.0 0.0 copy-start
  0.0 0.8 %add_bitcast_fusion = s32[1,4]{1,0:T(1,128)S(1)} fusion(s32[4]{0:T(128)} %param.12, s32[4,1]{0,1:T(1,128)} %param.11), kind=kLoop, calls=%fused_computation.40 | loop fusion | flops 8 | bytes 48 | tf_op jit(solution)/shard_map/reshape | solution.py:71
  0.8 0.5 collective-permute-start
  1.3 0.3 copy-done
  1.6 3.6 %fusion.29 = f16[512,512]{1,0:T(8,128)(2,1)} fusion(bf16[512,2048]{1,0:T(8,128)(2,1)S(1)} %copy-done, bf16[2048,2048]{1,0:T(8,128)(2,1)} %param.8, s32[]{:T(128)S(6)} %select_n.27), kind=kOutput, calls=%fused_computation.19 | convolution fusion | flops 1074266112 | bytes 4718596 | tf_op jit(solution)/shard_map/dot_general | solution.py:144
  5.3 0.0 collective-permute-done
  5.3 3.0 %collective-permute-start.1 = (s32[2,4]{1,0:T(2,128)S(1)}, s32[2,4]{1,0:T(2,128)S(1)}, u32[]{:S(2)}, u32[]{:S(2)}) collective-permute-start(s32[2,4]{1,0:T(2,128)S(1)} %pad_add_fusion.2), channel_id=1, source_target_pairs={{0,8},{4,12},{8,0},{12,4},{16,24},{20,28},{24,16},{28,20},{1,9},{5... | collective-permute-start | bytes 104 | tf_op jit(solution)/shard_map/ppermute | solution.py:74
  8.3 3.5 %collective-permute-start.3 = (f16[512,512]{1,0:T(8,128)(2,1)}, f16[512,512]{1,0:T(8,128)(2,1)S(1)}, u32[]{:S(2)}, u32[]{:S(2)}) collective-permute-start(f16[512,512]{1,0:T(8,128)(2,1)} %fusion.29), channel_id=1, source_target_pairs={{0,1},{3,2},{4,5},{7,6},{8,9},{11,10},{12,13},{15,14},{16,17},{19,... | collective-permute-start | bytes 1572872 | tf_op jit(solution)/shard_map/ppermute | solution.py:161
  11.8 1.5 %collective-permute-start.5 = (f16[512,512]{1,0:T(8,128)(2,1)}, f16[512,512]{1,0:T(8,128)(2,1)}, u32[]{:S(2)}, u32[]{:S(2)}) collective-permute-start(f16[512,512]{1,0:T(8,128)(2,1)} %fusion.29), channel_id=1, source_target_pairs={{1,2},{2,1},{5,6},{6,5},{9,10},{10,9},{13,14},{14,13},{17,18},{18,... | collective-permute-start | bytes 1572872 | tf_op jit(solution)/shard_map/ppermute | solution.py:162
  13.3 0.0 collective-permute-done.1
  13.3 1.6 %collective-permute-start.2 = (s32[4,4]{1,0:T(4,128)S(1)}, s32[4,4]{1,0:T(4,128)S(1)}, u32[]{:S(2)}, u32[]{:S(2)}) collective-permute-start(s32[4,4]{1,0:T(4,128)S(1)} %pad_add_fusion.1), channel_id=1, source_target_pairs={{0,16},{4,20},{8,24},{12,28},{16,0},{20,4},{24,8},{28,12},{1,17},{... | collective-permute-start | bytes 200 | tf_op jit(solution)/shard_map/ppermute | solution.py:74
  14.9 2.8 %fusion.32 = f16[512,512]{1,0:T(8,128)(2,1)S(1)} fusion(bf16[512,2048]{1,0:T(8,128)(2,1)S(1)} %copy-done, bf16[2048,2048]{1,0:T(8,128)(2,1)} %param.8, s32[]{:T(128)S(6)} %select_n.24), kind=kOutput, calls=%fused_computation.20 | convolution fusion | flops 1074266112 | bytes 4718596 | tf_op jit(solution)/shard_map/dot_general | solution.py:144
  17.7 1.3 %collective-permute-start.4 = (f16[512,512]{1,0:T(8,128)(2,1)S(1)}, f16[512,512]{1,0:T(8,128)(2,1)}, u32[]{:S(2)}, u32[]{:S(2)}) collective-permute-start(f16[512,512]{1,0:T(8,128)(2,1)S(1)} %fusion.32), channel_id=1, source_target_pairs={{0,2},{3,1},{1,0},{2,3},{4,6},{7,5},{5,4},{6,7},{8,10},{11,9},{9,8... | collective-permute-start | bytes 1572872 | tf_op jit(solution)/shard_map/ppermute | solution.py:165
  19.0 0.0 collective-permute-done.2
  19.0 0.6 %pad_add_fusion.ids_ref = s32[8,4]{1,0:T(8,128)} fusion(s32[4,4]{1,0:T(4,128)S(1)} %collective-permute-done.2, s32[2,4]{1,0:T(2,128)S(1)} %collective-permute-done.1, s32[1,4]{1,0:T(1,128)S(1)} %collective-permute-done, s32[1,4]{1,0:T(1,128)S(1)} %add_bitcast_fusion), kind=kLoop, calls=%fused_computation.28 | loop fusion | flops 96 | bytes 256 | tf_op jit(solution)/shard_map/concatenate | solution.py:75
  19.6 2.6 %shard_map.73 = bf16[8,2,16,2560]{3,2,1,0:T(8,128)(2,1)} custom-call(s32[8,4]{1,0:T(8,128)} %pad_add_fusion.ids_ref, s32[1]{0:T(128)} %bitcast.3.me_ref, bf16[128,16,2048]{2,1,0:T(8,128)(2,1)} %bitcast.34, bf16[128,16,512]{2,1,0:T(8,128)(2,1)} %up_ref.1), custom_call_target="tpu_custom_call" | custom-call | flops 1 | bytes 1 | tf_op jit(solution)/shard_map/pallas_call | solution.py:85
  22.2 4.3 %all-to-all-start = ((bf16[8,2,16,2560]{3,2,1,0:T(8,128)(2,1)}), bf16[8,2,16,2560]{3,2,1,0:T(8,128)(2,1)}, u32[]{:S(2)}, u32[]{:S(2)}) async-start(bf16[8,2,16,2560]{3,2,1,0:T(8,128)(2,1)} %shard_map.73), calls=%async_computation | async-start | bytes 2621440 | tf_op jit(solution)/shard_map/all_to_all | solution.py:103
  26.5 2.8 %fusion.14 = f32[512,512]{1,0:T(8,128)S(1)} fusion(bf16[512,2048]{1,0:T(8,128)(2,1)S(1)} %copy-done, bf16[2048,2048]{1,0:T(8,128)(2,1)} %param.8, s32[]{:T(128)S(6)} %select_n.26), kind=kOutput, calls=%fused_computation.11 | convolution fusion | flops 1073741824 | bytes 5242884 | tf_op jit(solution)/shard_map/dot_general | solution.py:144
  29.3 0.0 collective-permute-done.3
  29.3 1.0 %multiply_convert_fusion = f16[512,512]{1,0:T(8,128)(2,1)} fusion(f32[512,512]{1,0:T(8,128)S(1)} %fusion.14, f16[512,512]{1,0:T(8,128)(2,1)S(1)} %collective-permute-done.3), kind=kLoop, calls=%fused_computation.23 | loop fusion | flops 1310720 | bytes 2097152 | tf_op jit(solution)/shard_map/convert_element_type | solution.py:148
  30.4 0.8 %collective-permute-start.6 = (f16[512,512]{1,0:T(8,128)(2,1)}, f16[512,512]{1,0:T(8,128)(2,1)}, u32[]{:S(2)}, u32[]{:S(2)}) collective-permute-start(f16[512,512]{1,0:T(8,128)(2,1)} %multiply_convert_fusion), channel_id=1, source_target_pairs={{0,1},{3,2},{1,3},{2,0},{4,5},{7,6},{5,7},{6,4},{8,9},{11,10},{9,1... | collective-permute-start | bytes 1572872 | tf_op jit(solution)/shard_map/ppermute | solution.py:171
  31.1 0.0 copy-start.1
  31.1 2.9 %fusion.23 = f32[512,512]{1,0:T(8,128)S(1)} fusion(bf16[512,2048]{1,0:T(8,128)(2,1)S(1)} %copy-done, bf16[2048,2048]{1,0:T(8,128)(2,1)} %param.8, s32[]{:T(128)S(6)} %select_n.28), kind=kOutput, calls=%fused_computation.14 | convolution fusion | flops 1073741824 | bytes 5242884 | tf_op jit(solution)/shard_map/dot_general | solution.py:144
  34.0 0.0 copy-done.1
  34.0 0.1 iota_compare_fusion.1
  34.1 1.5 %collective-permute-done.4 = f16[512,512]{1,0:T(8,128)(2,1)} collective-permute-done((f16[512,512]{1,0:T(8,128)(2,1)S(1)}, f16[512,512]{1,0:T(8,128)(2,1)}, u32[]{:S(2)}, u32[]{:S(2)}) %collective-permute-start.4) | collective-permute-done | bytes 524320 | tf_op jit(solution)/shard_map/ppermute | solution.py:165
  35.6 1.2 %multiply_add_fusion.1 = f32[512,512]{1,0:T(8,128)S(1)} fusion(f32[512,512]{1,0:T(8,128)S(1)} %fusion.23, f16[512,512]{1,0:T(8,128)(2,1)} %collective-permute-done.4), kind=kLoop, calls=%fused_computation.22 | loop fusion | flops 786432 | bytes 2621440 | tf_op jit(solution)/shard_map/add | solution.py:174
  36.8 1.1 %shard_map.74 = s32[4]{0:T(128)} custom-call(s32[4]{0:T(128)} %bitcast.36), custom_call_target="tpu_custom_call" | custom-call | flops 99999997952 | bytes 1 | tf_op jit(solution)/shard_map/pallas_call | solution.py:109
  38.0 0.9 %convert_reduce_fusion = s32[4]{0:T(128)S(1)} fusion(s32[4]{0:T(128)} %shard_map.74), kind=kLoop, calls=%fused_computation.30 | loop fusion | flops 76 | bytes 32 | tf_op jit(solution)/shard_map/reduce_sum | solution.py:122
  38.8 0.6 %multiply_add_fusion.2 = s32[4]{0:T(128)S(1)} fusion(s32[4]{0:T(128)S(1)} %convert_reduce_fusion, s32[4]{0:T(128)} %shard_map.74), kind=kLoop, calls=%fused_computation.39 | loop fusion | flops 8 | bytes 48 | tf_op jit(solution)/shard_map/add | solution.py:122
  39.5 5.2 %all-to-all-done = bf16[8,2,16,2560]{3,2,1,0:T(8,128)(2,1)} async-done(((bf16[8,2,16,2560]{3,2,1,0:T(8,128)(2,1)}), bf16[8,2,16,2560]{3,2,1,0:T(8,128)(2,1)}, u32[]{:S(2)}, u32[]{:S(2)}) %all-to-all-start) | async-done | bytes 1310752 | tf_op jit(solution)/shard_map/all_to_all | solution.py:103
  44.7 1.9 %gather_fusion = bf16[4,16,2560]{2,1,0:T(8,128)(2,1)S(1)} fusion(bf16[16,16,2560]{2,1,0:T(8,128)(2,1)} %bitcast.8, s32[1024]{0:T(1024)S(1)} %pad_clamp_fusion), kind=kCustom, calls=%fused_computation | custom fusion | bytes 655376 | tf_op jit(solution)/shard_map/jit(_take)/gather | solution.py:127
  46.6 0.6 %fusion.43 = f32[4,16,128]{2,1,0:T(8,128)S(1)} fusion(bf16[4,16,2048]{2,1,0:T(8,128)(2,1)S(1)} %slice.10, bf16[4,128,2048]{2,1,0:T(8,128)(2,1)S(1)} %bitcast.33), kind=kOutput, calls=%fused_computation.41 | convolution fusion | flops 33554432 | bytes 2392064 | tf_op jit(solution)/shard_map/nbd,nrd->nrb/dot_general | solution.py:131
  47.3 2.5 %collective-permute-start.9 = (f32[4,16,128]{2,1,0:T(8,128)S(1)}, f32[4,16,128]{2,1,0:T(8,128)S(1)}, u32[]{:S(2)}, u32[]{:S(2)}) collective-permute-start(f32[4,16,128]{2,1,0:T(8,128)S(1)} %fusion.43), channel_id=1, source_target_pairs={{0,3},{1,2},{2,1},{3,0},{4,7},{5,6},{6,5},{7,4},{8,11},{9,10},{10,... | collective-permute-start | bytes 98312 | tf_op jit(solution)/shard_map/ppermute | solution.py:186
  49.8 0.0 collective-permute-start.8
  49.8 1.9 %collective-permute-start.7 = (f32[4,16,128]{2,1,0:T(8,128)S(1)}, f32[4,16,128]{2,1,0:T(8,128)S(1)}, u32[]{:S(2)}, u32[]{:S(2)}) collective-permute-start(f32[4,16,128]{2,1,0:T(8,128)S(1)} %fusion.43), channel_id=1, source_target_pairs={{0,1},{1,0},{2,3},{3,2},{4,5},{5,4},{6,7},{7,6},{8,9},{9,8},{10,11... | collective-permute-start | bytes 98312 | tf_op jit(solution)/shard_map/ppermute | solution.py:186
  51.7 0.0 collective-permute-done.6
  51.7 0.0 collective-permute-done.5
  51.7 1.5 %multiply_add_fusion = f32[512,512]{1,0:T(8,128)S(1)} fusion(f16[512,512]{1,0:T(8,128)(2,1)} %collective-permute-done.6, f32[512,512]{1,0:T(8,128)S(1)} %multiply_add_fusion.1, f16[512,512]{1,0:T(8,128)(2,1)} %collective-permute-done.5), kind=kLoop, calls=%fused_computation.21 | loop fusion | flops 1572864 | bytes 3145728 | tf_op jit(solution)/shard_map/add | solution.py:178
  53.2 0.0 collective-permute-done.9
  53.2 1.4 %collective-permute-done.8 = f32[4,16,128]{2,1,0:T(8,128)S(1)} collective-permute-done((f32[4,16,128]{2,1,0:T(8,128)S(1)}, f32[4,16,128]{2,1,0:T(8,128)S(1)}, u32[]{:S(2)}, u32[]{:S(2)}) %collective-permute-start.8) | collective-permute-done | bytes 32800 | tf_op jit(solution)/shard_map/ppermute | solution.py:186
  54.6 0.0 collective-permute-done.7
  54.6 1.5 %fusion.28 = bf16[4,128,512]{2,1,0:T(8,128)(2,1)} fusion(f32[4,128,512]{2,1,0:T(8,128)S(1)} %bitcast.35, bf16[4,16,512]{2,1,0:T(8,128)(2,1)S(1)} %slice.11, pred[4,128]{1,0:T(4,128)(4,1)S(1)} %iota_compare_fusion.1, f32[4,16,128]{2,1,0:T(8,128)S(1)} %collective-permute-done.9, f32[4,16,128]{2,1,0:T(8,128)S(1)} %collective-permute-done.8, ...), kind=kOutput, calls=%fused_computation.18 | convolution fusion | flops 51404800 | bytes 1769984 | tf_op jit(solution)/shard_map/nrb,nro->nbo/dot_general | solution.py:187
  (5 shorter events, 0.1 us)
Async XLA Ops:
  0.0 1.6 %copy-start = (bf16[512,2048]{1,0:T(8,128)(2,1)S(1)}, bf16[512,2048]{1,0:T(8,128)(2,1)}, u32[]{:S(2)}) copy-start(bf16[512,2048]{1,0:T(8,128)(2,1)} %param.7) | copy-start | bytes 6291460
  0.8 4.4 %collective-permute-start = (s32[1,4]{1,0:T(1,128)S(1)}, s32[1,4]{1,0:T(1,128)S(1)}, u32[]{:S(2)}, u32[]{:S(2)}) collective-permute-start(s32[1,4]{1,0:T(1,128)S(1)} %add_bitcast_fusion), channel_id=1, source_target_pairs={{0,4},{4,0},{8,12},{12,8},{16,20},{20,16},{24,28},{28,24},{1,5},{5... | collective-permute-start | bytes 56 | tf_op jit(solution)/shard_map/ppermute | solution.py:74
  5.3 8.0 %collective-permute-start.1 = (s32[2,4]{1,0:T(2,128)S(1)}, s32[2,4]{1,0:T(2,128)S(1)}, u32[]{:S(2)}, u32[]{:S(2)}) collective-permute-start(s32[2,4]{1,0:T(2,128)S(1)} %pad_add_fusion.2), channel_id=1, source_target_pairs={{0,8},{4,12},{8,0},{12,4},{16,24},{20,28},{24,16},{28,20},{1,9},{5... | collective-permute-start | bytes 104 | tf_op jit(solution)/shard_map/ppermute | solution.py:74
  8.3 21.1 %collective-permute-start.3 = (f16[512,512]{1,0:T(8,128)(2,1)}, f16[512,512]{1,0:T(8,128)(2,1)S(1)}, u32[]{:S(2)}, u32[]{:S(2)}) collective-permute-start(f16[512,512]{1,0:T(8,128)(2,1)} %fusion.29), channel_id=1, source_target_pairs={{0,1},{3,2},{4,5},{7,6},{8,9},{11,10},{12,13},{15,14},{16,17},{19,... | collective-permute-start | bytes 1572872 | tf_op jit(solution)/shard_map/ppermute | solution.py:161
  11.8 39.9 %collective-permute-start.5 = (f16[512,512]{1,0:T(8,128)(2,1)}, f16[512,512]{1,0:T(8,128)(2,1)}, u32[]{:S(2)}, u32[]{:S(2)}) collective-permute-start(f16[512,512]{1,0:T(8,128)(2,1)} %fusion.29), channel_id=1, source_target_pairs={{1,2},{2,1},{5,6},{6,5},{9,10},{10,9},{13,14},{14,13},{17,18},{18,... | collective-permute-start | bytes 1572872 | tf_op jit(solution)/shard_map/ppermute | solution.py:162
  13.3 5.8 %collective-permute-start.2 = (s32[4,4]{1,0:T(4,128)S(1)}, s32[4,4]{1,0:T(4,128)S(1)}, u32[]{:S(2)}, u32[]{:S(2)}) collective-permute-start(s32[4,4]{1,0:T(4,128)S(1)} %pad_add_fusion.1), channel_id=1, source_target_pairs={{0,16},{4,20},{8,24},{12,28},{16,0},{20,4},{24,8},{28,12},{1,17},{... | collective-permute-start | bytes 200 | tf_op jit(solution)/shard_map/ppermute | solution.py:74
  17.7 17.9 %collective-permute-start.4 = (f16[512,512]{1,0:T(8,128)(2,1)S(1)}, f16[512,512]{1,0:T(8,128)(2,1)}, u32[]{:S(2)}, u32[]{:S(2)}) collective-permute-start(f16[512,512]{1,0:T(8,128)(2,1)S(1)} %fusion.32), channel_id=1, source_target_pairs={{0,2},{3,1},{1,0},{2,3},{4,6},{7,5},{5,4},{6,7},{8,10},{11,9},{9,8... | collective-permute-start | bytes 1572872 | tf_op jit(solution)/shard_map/ppermute | solution.py:165
  22.2 22.5 %all-to-all-start = ((bf16[8,2,16,2560]{3,2,1,0:T(8,128)(2,1)}), bf16[8,2,16,2560]{3,2,1,0:T(8,128)(2,1)}, u32[]{:S(2)}, u32[]{:S(2)}) async-start(bf16[8,2,16,2560]{3,2,1,0:T(8,128)(2,1)} %shard_map.73), calls=%async_computation | async-start | bytes 2621440 | tf_op jit(solution)/shard_map/all_to_all | solution.py:103
  30.4 21.3 %collective-permute-start.6 = (f16[512,512]{1,0:T(8,128)(2,1)}, f16[512,512]{1,0:T(8,128)(2,1)}, u32[]{:S(2)}, u32[]{:S(2)}) collective-permute-start(f16[512,512]{1,0:T(8,128)(2,1)} %multiply_convert_fusion), channel_id=1, source_target_pairs={{0,1},{3,2},{1,3},{2,0},{4,5},{7,6},{5,7},{6,4},{8,9},{11,10},{9,1... | collective-permute-start | bytes 1572872 | tf_op jit(solution)/shard_map/ppermute | solution.py:171
  31.1 2.9 %copy-start.1 = (s32[4]{0:T(128)S(1)}, s32[4]{0:T(128)}, u32[]{:S(2)}) copy-start(s32[4]{0:T(128)} %param.13) | copy-start | bytes 52
  47.3 5.9 %collective-permute-start.9 = (f32[4,16,128]{2,1,0:T(8,128)S(1)}, f32[4,16,128]{2,1,0:T(8,128)S(1)}, u32[]{:S(2)}, u32[]{:S(2)}) collective-permute-start(f32[4,16,128]{2,1,0:T(8,128)S(1)} %fusion.43), channel_id=1, source_target_pairs={{0,3},{1,2},{2,1},{3,0},{4,7},{5,6},{6,5},{7,4},{8,11},{9,10},{10,... | collective-permute-start | bytes 98312 | tf_op jit(solution)/shard_map/ppermute | solution.py:186
  49.8 4.8 %collective-permute-start.8 = (f32[4,16,128]{2,1,0:T(8,128)S(1)}, f32[4,16,128]{2,1,0:T(8,128)S(1)}, u32[]{:S(2)}, u32[]{:S(2)}) collective-permute-start(f32[4,16,128]{2,1,0:T(8,128)S(1)} %fusion.43), channel_id=1, source_target_pairs={{0,2},{1,3},{2,0},{3,1},{4,6},{5,7},{6,4},{7,5},{8,10},{9,11},{10,... | collective-permute-start | bytes 98312 | tf_op jit(solution)/shard_map/ppermute | solution.py:186
  49.8 4.8 %collective-permute-start.7 = (f32[4,16,128]{2,1,0:T(8,128)S(1)}, f32[4,16,128]{2,1,0:T(8,128)S(1)}, u32[]{:S(2)}, u32[]{:S(2)}) collective-permute-start(f32[4,16,128]{2,1,0:T(8,128)S(1)} %fusion.43), channel_id=1, source_target_pairs={{0,1},{1,0},{2,3},{3,2},{4,5},{5,4},{6,7},{7,6},{8,9},{9,8},{10,11... | collective-permute-start | bytes 98312 | tf_op jit(solution)/shard_map/ppermute | solution.py:186

commit v6 on v5

--- a/solution.py
+++ b/solution.py
@@ -1,4 +1,4 @@
-import functools
+import math
 
 import jax
 import jax.numpy as jnp
@@ -11,7 +11,8 @@
 BLOCK = 128
 CAP = 2
 adapter_scale = 2.0
-SEND_SCALE = 16.0
+FLOAT16_MAX = 65504.0
+PRODUCT_MAX = 6.0 * 0.0625
 HBM = pl.BlockSpec(memory_space=pl.ANY)
 
 
@@ -133,6 +134,17 @@
     return reduced, up_block
 
 
+def expand_tokens(total, up_block):
+    parts, rest = [], total
+    for _ in range(3):
+        part = lax.reduce_precision(rest, exponent_bits=8, mantissa_bits=7)
+        parts.append(part.astype(jnp.bfloat16))
+        rest = rest - part
+    parts = jnp.concatenate(parts, axis=1)
+    up_parts = jnp.concatenate([up_block] * 3, axis=1)
+    return jnp.einsum("nrb,nro->nbo", parts, up_parts, preferred_element_type=jnp.float32)
+
+
 def body(tokens, base_weight, down_tables, up_tables, block_owner, block_local, block_count):
     tp_count = lax.axis_size("tp")
     z = lax.axis_index("tp")
@@ -144,11 +156,13 @@
         value = jnp.dot(tokens, columns, preferred_element_type=jnp.float32)
         return with_layout_constraint(value, Layout((0, 1)))
 
+    scale = 2.0 ** math.floor(math.log2(FLOAT16_MAX / (2 * tokens.shape[1] * PRODUCT_MAX)))
+
     def code(value):
-        return (value * SEND_SCALE).astype(jnp.float16)
+        return (value * scale).astype(jnp.float16)
 
     def plain(value):
-        return value.astype(jnp.float32) * (1.0 / SEND_SCALE)
+        return value.astype(jnp.float32) * (1.0 / scale)
 
     def after(value, *others):
         return lax.optimization_barrier((value, *others))[0]
@@ -184,9 +198,7 @@
     total = reduced
     for j in range(1, tp_count):
         total = total + lax.ppermute(reduced, "tp", [(i, i ^ j) for i in range(tp_count)])
-    lowrank = jnp.einsum(
-        "nrb,nro->nbo", total, up_block.astype(jnp.float32), precision=lax.Precision.HIGHEST
-    )
+    lowrank = expand_tokens(total, up_block)
     offsets = jnp.arange(BLOCK, dtype=jnp.int32)
     live_rows = offsets[None, :, None] < live_counts[:, None, None]
     combined_output = base_projection.reshape(lowrank.shape) + adapter_scale * lowrank

time: 56.6 us -> 56.3 us (level)
  no operation moved by 1% of the time
where the time goes in v6:
time: 56.3 us; the launch traced here: 55.8 us
  starting transfers between devices  20.8 us (37%)
  matrix products  14 us (25%)
  waiting for transfers between devices  8.12 us (14%)
  other arithmetic  6.81 us (12%)
  Pallas kernels  3.69 us (7%)
  local copies, waits for them, and re-layouts  2.26 us (4%)
    dot_general x4, matrix products, product(): value = jnp.dot(tokens, columns, preferred_element_type=jnp.float32)  12.2 us
    all_to_all x1, waiting for transfers between devices, exchange(): got = lax.all_to_all(packed, 'grp', split_axis=0, concat_axis=0, tiled=True)  5.14 us
    ppermute x3, starting transfers between devices, adapter_ids(): lax.ppermute(ids, 'grp', [(i, i ^ step) for i in range(group_count)])  5.04 us
    ppermute x3, starting transfers between devices, body(): lax.ppermute(reduced, 'tp', [(i, i ^ j) for i in range(tp_count)])  4.4 us
    all_to_all x1, starting transfers between devices, exchange(): got = lax.all_to_all(packed, 'grp', split_axis=0, concat_axis=0, tiled=True)  4.27 us
    ppermute x1, starting transfers between devices, body(): to_inner = lax.ppermute(far, 'tp', [(0, 1), (3, 2)])  3.5 us
    pallas_call x1, Pallas kernels, pack_adapters(): pl.pallas_call(pack_kernel, out_shape=jax.ShapeDtypeStruct((group_count,...  2.56 us
    gather x1, local copies, waits for them, and re-layouts, reduce_tokens(): mine = jnp.take(got, block_slot, axis=0, mode='clip')  1.88 us
  transfers between devices with their start and end apart: 11, of which 3 were waited for; matrix products, arithmetic and copies ran while one was open for 37% of the time, Pallas kernels for 7%

profile of v6, /device:TPU:0, one launch (start us, length us, event | category | flops | bytes accessed | tf_op | source)
XLA Modules:
  0.0 55.8 jit_solution(3249821218851205183)
XLA Ops:
  0.0 0.0 copy-start
  0.0 0.8 %add_bitcast_fusion = s32[1,4]{1,0:T(1,128)S(1)} fusion(s32[4]{0:T(128)} %param.12, s32[4,1]{0,1:T(1,128)} %param.11), kind=kLoop, calls=%fused_computation.54 | loop fusion | flops 8 | bytes 48 | tf_op jit(solution)/shard_map/reshape | solution.py:72
  0.8 0.5 collective-permute-start
  1.3 0.3 copy-done
  1.6 3.6 %fusion.29 = f16[512,512]{1,0:T(8,128)(2,1)} fusion(bf16[512,2048]{1,0:T(8,128)(2,1)S(1)} %copy-done, bf16[2048,2048]{1,0:T(8,128)(2,1)} %param.8, s32[]{:T(128)S(6)} %select_n.27), kind=kOutput, calls=%fused_computation.19 | convolution fusion | flops 1074266112 | bytes 4718596 | tf_op jit(solution)/shard_map/dot_general | solution.py:156
  5.3 0.0 collective-permute-done
  5.3 3.0 %collective-permute-start.1 = (s32[2,4]{1,0:T(2,128)S(1)}, s32[2,4]{1,0:T(2,128)S(1)}, u32[]{:S(2)}, u32[]{:S(2)}) collective-permute-start(s32[2,4]{1,0:T(2,128)S(1)} %pad_add_fusion.2), channel_id=1, source_target_pairs={{0,8},{4,12},{8,0},{12,4},{16,24},{20,28},{24,16},{28,20},{1,9},{5... | collective-permute-start | bytes 104 | tf_op jit(solution)/shard_map/ppermute | solution.py:75
  8.3 3.5 %collective-permute-start.3 = (f16[512,512]{1,0:T(8,128)(2,1)}, f16[512,512]{1,0:T(8,128)(2,1)S(1)}, u32[]{:S(2)}, u32[]{:S(2)}) collective-permute-start(f16[512,512]{1,0:T(8,128)(2,1)} %fusion.29), channel_id=1, source_target_pairs={{0,1},{3,2},{4,5},{7,6},{8,9},{11,10},{12,13},{15,14},{16,17},{19,... | collective-permute-start | bytes 1572872 | tf_op jit(solution)/shard_map/ppermute | solution.py:175
  11.8 1.5 %collective-permute-start.5 = (f16[512,512]{1,0:T(8,128)(2,1)}, f16[512,512]{1,0:T(8,128)(2,1)}, u32[]{:S(2)}, u32[]{:S(2)}) collective-permute-start(f16[512,512]{1,0:T(8,128)(2,1)} %fusion.29), channel_id=1, source_target_pairs={{1,2},{2,1},{5,6},{6,5},{9,10},{10,9},{13,14},{14,13},{17,18},{18,... | collective-permute-start | bytes 1572872 | tf_op jit(solution)/shard_map/ppermute | solution.py:176
  13.3 0.0 collective-permute-done.1
  13.3 1.6 %collective-permute-start.2 = (s32[4,4]{1,0:T(4,128)S(1)}, s32[4,4]{1,0:T(4,128)S(1)}, u32[]{:S(2)}, u32[]{:S(2)}) collective-permute-start(s32[4,4]{1,0:T(4,128)S(1)} %pad_add_fusion.1), channel_id=1, source_target_pairs={{0,16},{4,20},{8,24},{12,28},{16,0},{20,4},{24,8},{28,12},{1,17},{... | collective-permute-start | bytes 200 | tf_op jit(solution)/shard_map/ppermute | solution.py:75
  14.9 2.8 %fusion.32 = f16[512,512]{1,0:T(8,128)(2,1)S(1)} fusion(bf16[512,2048]{1,0:T(8,128)(2,1)S(1)} %copy-done, bf16[2048,2048]{1,0:T(8,128)(2,1)} %param.8, s32[]{:T(128)S(6)} %select_n.24), kind=kOutput, calls=%fused_computation.20 | convolution fusion | flops 1074266112 | bytes 4718596 | tf_op jit(solution)/shard_map/dot_general | solution.py:156
  17.7 1.3 %collective-permute-start.4 = (f16[512,512]{1,0:T(8,128)(2,1)S(1)}, f16[512,512]{1,0:T(8,128)(2,1)}, u32[]{:S(2)}, u32[]{:S(2)}) collective-permute-start(f16[512,512]{1,0:T(8,128)(2,1)S(1)} %fusion.32), channel_id=1, source_target_pairs={{0,2},{3,1},{1,0},{2,3},{4,6},{7,5},{5,4},{6,7},{8,10},{11,9},{9,8... | collective-permute-start | bytes 1572872 | tf_op jit(solution)/shard_map/ppermute | solution.py:179
  19.0 0.0 collective-permute-done.2
  19.0 0.6 %pad_add_fusion.ids_ref = s32[8,4]{1,0:T(8,128)} fusion(s32[4,4]{1,0:T(4,128)S(1)} %collective-permute-done.2, s32[2,4]{1,0:T(2,128)S(1)} %collective-permute-done.1, s32[1,4]{1,0:T(1,128)S(1)} %collective-permute-done, s32[1,4]{1,0:T(1,128)S(1)} %add_bitcast_fusion), kind=kLoop, calls=%fused_computation.42 | loop fusion | flops 96 | bytes 256 | tf_op jit(solution)/shard_map/concatenate | solution.py:76
  19.6 2.6 %shard_map.73 = bf16[8,2,16,2560]{3,2,1,0:T(8,128)(2,1)} custom-call(s32[8,4]{1,0:T(8,128)} %pad_add_fusion.ids_ref, s32[1]{0:T(128)} %bitcast.3.me_ref, bf16[128,16,2048]{2,1,0:T(8,128)(2,1)} %bitcast.33, bf16[128,16,512]{2,1,0:T(8,128)(2,1)} %up_ref.1), custom_call_target="tpu_custom_call" | custom-call | flops 1 | bytes 1 | tf_op jit(solution)/shard_map/pallas_call | solution.py:86
  22.2 4.3 %all-to-all-start = ((bf16[8,2,16,2560]{3,2,1,0:T(8,128)(2,1)}), bf16[8,2,16,2560]{3,2,1,0:T(8,128)(2,1)}, u32[]{:S(2)}, u32[]{:S(2)}) async-start(bf16[8,2,16,2560]{3,2,1,0:T(8,128)(2,1)} %shard_map.73), calls=%async_computation | async-start | bytes 2621440 | tf_op jit(solution)/shard_map/all_to_all | solution.py:104
  26.5 2.8 %fusion.14 = f32[512,512]{1,0:T(8,128)S(1)} fusion(bf16[512,2048]{1,0:T(8,128)(2,1)S(1)} %copy-done, bf16[2048,2048]{1,0:T(8,128)(2,1)} %param.8, s32[]{:T(128)S(6)} %select_n.26), kind=kOutput, calls=%fused_computation.11 | convolution fusion | flops 1073741824 | bytes 5242884 | tf_op jit(solution)/shard_map/dot_general | solution.py:156
  29.3 0.0 collective-permute-done.3
  29.3 1.0 %multiply_convert_fusion = f16[512,512]{1,0:T(8,128)(2,1)} fusion(f32[512,512]{1,0:T(8,128)S(1)} %fusion.14, f16[512,512]{1,0:T(8,128)(2,1)S(1)} %collective-permute-done.3), kind=kLoop, calls=%fused_computation.23 | loop fusion | flops 1310720 | bytes 2097152 | tf_op jit(solution)/shard_map/convert_element_type | solution.py:162
  30.4 0.8 %collective-permute-start.6 = (f16[512,512]{1,0:T(8,128)(2,1)}, f16[512,512]{1,0:T(8,128)(2,1)}, u32[]{:S(2)}, u32[]{:S(2)}) collective-permute-start(f16[512,512]{1,0:T(8,128)(2,1)} %multiply_convert_fusion), channel_id=1, source_target_pairs={{0,1},{3,2},{1,3},{2,0},{4,5},{7,6},{5,7},{6,4},{8,9},{11,10},{9,1... | collective-permute-start | bytes 1572872 | tf_op jit(solution)/shard_map/ppermute | solution.py:185
  31.1 0.0 copy-start.1
  31.1 2.8 %fusion.23 = f32[512,512]{1,0:T(8,128)S(1)} fusion(bf16[512,2048]{1,0:T(8,128)(2,1)S(1)} %copy-done, bf16[2048,2048]{1,0:T(8,128)(2,1)} %param.8, s32[]{:T(128)S(6)} %select_n.28), kind=kOutput, calls=%fused_computation.14 | convolution fusion | flops 1073741824 | bytes 5242884 | tf_op jit(solution)/shard_map/dot_general | solution.py:156
  34.0 0.0 copy-done.1
  34.0 0.1 iota_compare_fusion.1
  34.1 1.5 %collective-permute-done.4 = f16[512,512]{1,0:T(8,128)(2,1)} collective-permute-done((f16[512,512]{1,0:T(8,128)(2,1)S(1)}, f16[512,512]{1,0:T(8,128)(2,1)}, u32[]{:S(2)}, u32[]{:S(2)}) %collective-permute-start.4) | collective-permute-done | bytes 524320 | tf_op jit(solution)/shard_map/ppermute | solution.py:179
  35.6 1.2 %multiply_add_fusion.1 = f32[512,512]{1,0:T(8,128)S(1)} fusion(f32[512,512]{1,0:T(8,128)S(1)} %fusion.23, f16[512,512]{1,0:T(8,128)(2,1)} %collective-permute-done.4), kind=kLoop, calls=%fused_computation.22 | loop fusion | flops 786432 | bytes 2621440 | tf_op jit(solution)/shard_map/add | solution.py:188
  36.8 1.1 %shard_map.74 = s32[4]{0:T(128)} custom-call(s32[4]{0:T(128)} %bitcast.35), custom_call_target="tpu_custom_call" | custom-call | flops 99999997952 | bytes 1 | tf_op jit(solution)/shard_map/pallas_call | solution.py:110
  38.0 0.9 %convert_reduce_fusion = s32[4]{0:T(128)S(1)} fusion(s32[4]{0:T(128)} %shard_map.74), kind=kLoop, calls=%fused_computation.44 | loop fusion | flops 76 | bytes 32 | tf_op jit(solution)/shard_map/reduce_sum | solution.py:123
  38.9 0.7 %multiply_add_fusion.2 = s32[4]{0:T(128)S(1)} fusion(s32[4]{0:T(128)S(1)} %convert_reduce_fusion, s32[4]{0:T(128)} %shard_map.74), kind=kLoop, calls=%fused_computation.53 | loop fusion | flops 8 | bytes 48 | tf_op jit(solution)/shard_map/add | solution.py:123
  39.6 5.1 %all-to-all-done = bf16[8,2,16,2560]{3,2,1,0:T(8,128)(2,1)} async-done(((bf16[8,2,16,2560]{3,2,1,0:T(8,128)(2,1)}), bf16[8,2,16,2560]{3,2,1,0:T(8,128)(2,1)}, u32[]{:S(2)}, u32[]{:S(2)}) %all-to-all-start) | async-done | bytes 1310752 | tf_op jit(solution)/shard_map/all_to_all | solution.py:104
  44.7 1.9 %gather_fusion = bf16[4,16,2560]{2,1,0:T(8,128)(2,1)S(1)} fusion(bf16[16,16,2560]{2,1,0:T(8,128)(2,1)} %bitcast.8, s32[1024]{0:T(1024)S(1)} %pad_clamp_fusion), kind=kCustom, calls=%fused_computation | custom fusion | bytes 655376 | tf_op jit(solution)/shard_map/jit(_take)/gather | solution.py:128
  46.6 0.6 %fusion.53 = f32[4,16,128]{2,1,0:T(8,128)S(1)} fusion(bf16[4,16,2048]{2,1,0:T(8,128)(2,1)S(1)} %slice.10, bf16[4,128,2048]{2,1,0:T(8,128)(2,1)S(1)} %bitcast.32), kind=kOutput, calls=%fused_computation.56 | convolution fusion | flops 33554432 | bytes 2392064 | tf_op jit(solution)/shard_map/nbd,nrd->nrb/dot_general | solution.py:132
  47.3 2.5 %collective-permute-start.9 = (f32[4,16,128]{2,1,0:T(8,128)S(1)}, f32[4,16,128]{2,1,0:T(8,128)S(1)}, u32[]{:S(2)}, u32[]{:S(2)}) collective-permute-start(f32[4,16,128]{2,1,0:T(8,128)S(1)} %fusion.53), channel_id=1, source_target_pairs={{0,3},{1,2},{2,1},{3,0},{4,7},{5,6},{6,5},{7,4},{8,11},{9,10},{10,... | collective-permute-start | bytes 98312 | tf_op jit(solution)/shard_map/ppermute | solution.py:200
  49.8 0.0 collective-permute-start.8
  49.8 1.9 %collective-permute-start.7 = (f32[4,16,128]{2,1,0:T(8,128)S(1)}, f32[4,16,128]{2,1,0:T(8,128)S(1)}, u32[]{:S(2)}, u32[]{:S(2)}) collective-permute-start(f32[4,16,128]{2,1,0:T(8,128)S(1)} %fusion.53), channel_id=1, source_target_pairs={{0,1},{1,0},{2,3},{3,2},{4,5},{5,4},{6,7},{7,6},{8,9},{9,8},{10,11... | collective-permute-start | bytes 98312 | tf_op jit(solution)/shard_map/ppermute | solution.py:200
  51.7 0.0 collective-permute-done.6
  51.7 0.0 collective-permute-done.5
  51.7 1.4 %multiply_add_fusion = f32[512,512]{1,0:T(8,128)S(1)} fusion(f16[512,512]{1,0:T(8,128)(2,1)} %collective-permute-done.6, f32[512,512]{1,0:T(8,128)S(1)} %multiply_add_fusion.1, f16[512,512]{1,0:T(8,128)(2,1)} %collective-permute-done.5), kind=kLoop, calls=%fused_computation.21 | loop fusion | flops 1572864 | bytes 3145728 | tf_op jit(solution)/shard_map/add | solution.py:192
  53.1 0.0 collective-permute-done.9
  53.1 1.4 %collective-permute-done.8 = f32[4,16,128]{2,1,0:T(8,128)S(1)} collective-permute-done((f32[4,16,128]{2,1,0:T(8,128)S(1)}, f32[4,16,128]{2,1,0:T(8,128)S(1)}, u32[]{:S(2)}, u32[]{:S(2)}) %collective-permute-start.8) | collective-permute-done | bytes 32800 | tf_op jit(solution)/shard_map/ppermute | solution.py:200
  54.6 0.0 collective-permute-done.7
  54.6 1.2 %fusion.28 = bf16[4,128,512]{2,1,0:T(8,128)(2,1)} fusion(f32[4,128,512]{2,1,0:T(8,128)S(1)} %bitcast.34, pred[4,128]{1,0:T(4,128)(4,1)S(1)} %iota_compare_fusion.1, bf16[4,16,512]{2,1,0:T(8,128)(2,1)S(1)} %slice.11, bf16[4,16,128]{2,1,0:T(8,128)(2,1)S(1)} %get-tuple-element.28, bf16[4,16,128]{2,1,0:T(8,128)(2,1)S(1)} %get-tuple-element.27, ...), kind=kOutput, calls=%fused_computation.18 | convolution fusion | flops 26951680 | bytes 1688064 | tf_op jit(solution)/shard_map/nrb,nro->nbo/dot_general | solution.py:145
  (7 shorter events, 0.1 us)
Async XLA Ops:
  0.0 1.6 %copy-start = (bf16[512,2048]{1,0:T(8,128)(2,1)S(1)}, bf16[512,2048]{1,0:T(8,128)(2,1)}, u32[]{:S(2)}) copy-start(bf16[512,2048]{1,0:T(8,128)(2,1)} %param.7) | copy-start | bytes 6291460
  0.8 4.4 %collective-permute-start = (s32[1,4]{1,0:T(1,128)S(1)}, s32[1,4]{1,0:T(1,128)S(1)}, u32[]{:S(2)}, u32[]{:S(2)}) collective-permute-start(s32[1,4]{1,0:T(1,128)S(1)} %add_bitcast_fusion), channel_id=1, source_target_pairs={{0,4},{4,0},{8,12},{12,8},{16,20},{20,16},{24,28},{28,24},{1,5},{5... | collective-permute-start | bytes 56 | tf_op jit(solution)/shard_map/ppermute | solution.py:75
  5.3 8.0 %collective-permute-start.1 = (s32[2,4]{1,0:T(2,128)S(1)}, s32[2,4]{1,0:T(2,128)S(1)}, u32[]{:S(2)}, u32[]{:S(2)}) collective-permute-start(s32[2,4]{1,0:T(2,128)S(1)} %pad_add_fusion.2), channel_id=1, source_target_pairs={{0,8},{4,12},{8,0},{12,4},{16,24},{20,28},{24,16},{28,20},{1,9},{5... | collective-permute-start | bytes 104 | tf_op jit(solution)/shard_map/ppermute | solution.py:75
  8.3 21.0 %collective-permute-start.3 = (f16[512,512]{1,0:T(8,128)(2,1)}, f16[512,512]{1,0:T(8,128)(2,1)S(1)}, u32[]{:S(2)}, u32[]{:S(2)}) collective-permute-start(f16[512,512]{1,0:T(8,128)(2,1)} %fusion.29), channel_id=1, source_target_pairs={{0,1},{3,2},{4,5},{7,6},{8,9},{11,10},{12,13},{15,14},{16,17},{19,... | collective-permute-start | bytes 1572872 | tf_op jit(solution)/shard_map/ppermute | solution.py:175
  11.8 39.9 %collective-permute-start.5 = (f16[512,512]{1,0:T(8,128)(2,1)}, f16[512,512]{1,0:T(8,128)(2,1)}, u32[]{:S(2)}, u32[]{:S(2)}) collective-permute-start(f16[512,512]{1,0:T(8,128)(2,1)} %fusion.29), channel_id=1, source_target_pairs={{1,2},{2,1},{5,6},{6,5},{9,10},{10,9},{13,14},{14,13},{17,18},{18,... | collective-permute-start | bytes 1572872 | tf_op jit(solution)/shard_map/ppermute | solution.py:176
  13.3 5.8 %collective-permute-start.2 = (s32[4,4]{1,0:T(4,128)S(1)}, s32[4,4]{1,0:T(4,128)S(1)}, u32[]{:S(2)}, u32[]{:S(2)}) collective-permute-start(s32[4,4]{1,0:T(4,128)S(1)} %pad_add_fusion.1), channel_id=1, source_target_pairs={{0,16},{4,20},{8,24},{12,28},{16,0},{20,4},{24,8},{28,12},{1,17},{... | collective-permute-start | bytes 200 | tf_op jit(solution)/shard_map/ppermute | solution.py:75
  17.7 17.9 %collective-permute-start.4 = (f16[512,512]{1,0:T(8,128)(2,1)S(1)}, f16[512,512]{1,0:T(8,128)(2,1)}, u32[]{:S(2)}, u32[]{:S(2)}) collective-permute-start(f16[512,512]{1,0:T(8,128)(2,1)S(1)} %fusion.32), channel_id=1, source_target_pairs={{0,2},{3,1},{1,0},{2,3},{4,6},{7,5},{5,4},{6,7},{8,10},{11,9},{9,8... | collective-permute-start | bytes 1572872 | tf_op jit(solution)/shard_map/ppermute | solution.py:179
  22.2 22.5 %all-to-all-start = ((bf16[8,2,16,2560]{3,2,1,0:T(8,128)(2,1)}), bf16[8,2,16,2560]{3,2,1,0:T(8,128)(2,1)}, u32[]{:S(2)}, u32[]{:S(2)}) async-start(bf16[8,2,16,2560]{3,2,1,0:T(8,128)(2,1)} %shard_map.73), calls=%async_computation | async-start | bytes 2621440 | tf_op jit(solution)/shard_map/all_to_all | solution.py:104
  30.4 21.3 %collective-permute-start.6 = (f16[512,512]{1,0:T(8,128)(2,1)}, f16[512,512]{1,0:T(8,128)(2,1)}, u32[]{:S(2)}, u32[]{:S(2)}) collective-permute-start(f16[512,512]{1,0:T(8,128)(2,1)} %multiply_convert_fusion), channel_id=1, source_target_pairs={{0,1},{3,2},{1,3},{2,0},{4,5},{7,6},{5,7},{6,4},{8,9},{11,10},{9,1... | collective-permute-start | bytes 1572872 | tf_op jit(solution)/shard_map/ppermute | solution.py:185
  31.1 2.9 %copy-start.1 = (s32[4]{0:T(128)S(1)}, s32[4]{0:T(128)}, u32[]{:S(2)}) copy-start(s32[4]{0:T(128)} %param.13) | copy-start | bytes 52
  47.3 5.9 %collective-permute-start.9 = (f32[4,16,128]{2,1,0:T(8,128)S(1)}, f32[4,16,128]{2,1,0:T(8,128)S(1)}, u32[]{:S(2)}, u32[]{:S(2)}) collective-permute-start(f32[4,16,128]{2,1,0:T(8,128)S(1)} %fusion.53), channel_id=1, source_target_pairs={{0,3},{1,2},{2,1},{3,0},{4,7},{5,6},{6,5},{7,4},{8,11},{9,10},{10,... | collective-permute-start | bytes 98312 | tf_op jit(solution)/shard_map/ppermute | solution.py:200
  49.8 4.8 %collective-permute-start.8 = (f32[4,16,128]{2,1,0:T(8,128)S(1)}, f32[4,16,128]{2,1,0:T(8,128)S(1)}, u32[]{:S(2)}, u32[]{:S(2)}) collective-permute-start(f32[4,16,128]{2,1,0:T(8,128)S(1)} %fusion.53), channel_id=1, source_target_pairs={{0,2},{1,3},{2,0},{3,1},{4,6},{5,7},{6,4},{7,5},{8,10},{9,11},{10,... | collective-permute-start | bytes 98312 | tf_op jit(solution)/shard_map/ppermute | solution.py:200
  49.8 4.8 %collective-permute-start.7 = (f32[4,16,128]{2,1,0:T(8,128)S(1)}, f32[4,16,128]{2,1,0:T(8,128)S(1)}, u32[]{:S(2)}, u32[]{:S(2)}) collective-permute-start(f32[4,16,128]{2,1,0:T(8,128)S(1)} %fusion.53), channel_id=1, source_target_pairs={{0,1},{1,0},{2,3},{3,2},{4,5},{5,4},{6,7},{7,6},{8,9},{9,8},{10,11... | collective-permute-start | bytes 98312 | tf_op jit(solution)/shard_map/ppermute | solution.py:200

commit v7 on v6

--- a/solution.py
+++ b/solution.py
@@ -125,7 +125,8 @@
 
 def reduce_tokens(tokens, got, block_slot):
     blocks, cols = block_slot.shape[0], tokens.shape[1]
-    mine = jnp.take(got, block_slot, axis=0, mode="clip")
+    match = block_slot[:, None] == jnp.arange(got.shape[0], dtype=jnp.int32)[None, :]
+    mine = jnp.sum(jnp.where(match[:, :, None, None], got[None], jnp.bfloat16(0.0)).astype(jnp.float32), axis=1).astype(jnp.bfloat16)
     mine = lax.optimization_barrier(mine)
     down_block = lax.optimization_barrier(mine[:, :, :cols])
     blocked = tokens.reshape(blocks, BLOCK, cols)
@@ -173,7 +174,8 @@
         end = (z == 0) | (z == 3)
         far = after(code(product(z ^ 3)), id_steps[0])
         to_inner = lax.ppermute(far, "tp", [(0, 1), (3, 2)])
-        from_inner = lax.ppermute(far, "tp", [(1, 2), (2, 1)])
+        direct, z = lax.optimization_barrier((far, z))
+        from_inner = lax.ppermute(direct, "tp", [(1, 2), (2, 1)])
         later_z = after(z, id_steps[1])
         first = code(product(later_z ^ jnp.where(end, 2, 1)))
         from_first = lax.ppermute(first, "tp", [(0, 2), (3, 1), (1, 0), (2, 3)])

time: 56.3 us -> 55.4 us (0.984)
  other arithmetic: 6.81 us -> 9.42 us
  waiting for transfers between devices: 8.12 us -> 5.69 us
  local copies, waits for them, and re-layouts: 2.26 us -> 0.38 us
  matrix products: 14 us -> 14.8 us
    gather x1 -> x0, local copies, waits for them, and re-layouts: 1.88 us -> none  [reduce_tokens(): mine = jnp.take(got, block_slot, axis=0, mode='clip')]
    ppermute x1, waiting for transfers between devices: 1.52 us -> 0.01 us  [body(): from_first = lax.ppermute(first, 'tp', [(0, 2), (3, 1), (1, 0), (2, 3)])]
    all_to_all x1, waiting for transfers between devices: 5.14 us -> 3.89 us  [exchange(): got = lax.all_to_all(packed, 'grp', split_axis=0, concat_axis=0, tiled=True)]
    convert_element_type x1, other arithmetic: 1.02 us -> 2.06 us  [code(): return (value * scale).astype(jnp.float16)]
    add x1, other arithmetic: 1.23 us -> 2.18 us  [body(): base_projection = lax.optimization_barrier(own + plain(from_first))]
    dot_general x4, matrix products: 12.2 us -> 13 us  [product(): value = jnp.dot(tokens, columns, preferred_element_type=jnp.float32)]
    ppermute x1, starting transfers between devices: 1.32 us -> 0.53 us  [body(): from_first = lax.ppermute(first, 'tp', [(0, 2), (3, 1), (1, 0), (2, 3)])]
    ppermute x1, starting transfers between devices: 3.5 us -> 4.27 us  [body(): to_inner = lax.ppermute(far, 'tp', [(0, 1), (3, 2)])]
  transfers between devices with their start and end apart: 11 -> 11, of which waited for: 3 -> 2; matrix products, arithmetic and copies ran while one was open for 37% -> 41% of each run, Pallas kernels for 7% -> 6%
where the time goes in v7:
time: 55.4 us; the launch traced here: 54.7 us
  starting transfers between devices  20.8 us (38%)
  matrix products  14.8 us (27%)
  other arithmetic  9.42 us (17%)
  waiting for transfers between devices  5.69 us (10%)
  Pallas kernels  3.55 us (6%)
    dot_general x4, matrix products, product(): value = jnp.dot(tokens, columns, preferred_element_type=jnp.float32)  13 us
    ppermute x3, starting transfers between devices, adapter_ids(): lax.ppermute(ids, 'grp', [(i, i ^ step) for i in range(group_count)])  5.04 us
    ppermute x3, starting transfers between devices, body(): lax.ppermute(reduced, 'tp', [(i, i ^ j) for i in range(tp_count)])  4.4 us
    ppermute x1, starting transfers between devices, body(): to_inner = lax.ppermute(far, 'tp', [(0, 1), (3, 2)])  4.27 us
    all_to_all x1, waiting for transfers between devices, exchange(): got = lax.all_to_all(packed, 'grp', split_axis=0, concat_axis=0, tiled=True)  3.89 us
    all_to_all x1, starting transfers between devices, exchange(): got = lax.all_to_all(packed, 'grp', split_axis=0, concat_axis=0, tiled=True)  3.58 us
    pallas_call x1, Pallas kernels, pack_adapters(): pl.pallas_call(pack_kernel, out_shape=jax.ShapeDtypeStruct((group_count,...  2.43 us
    add x1, other arithmetic, body(): base_projection = lax.optimization_barrier(own + plain(from_first))  2.18 us
  transfers between devices with their start and end apart: 11, of which 2 were waited for; matrix products, arithmetic and copies ran while one was open for 41% of the time, Pallas kernels for 6%

profile of v7, /device:TPU:0, one launch (start us, length us, event | category | flops | bytes accessed | tf_op | source)
XLA Modules:
  0.0 54.7 jit_solution(12644260854472473588)
XLA Ops:
  0.0 0.0 copy-start
  0.0 0.8 %add_bitcast_fusion = s32[1,4]{1,0:T(1,128)S(1)} fusion(s32[4]{0:T(128)} %param.12, s32[4,1]{0,1:T(1,128)} %param.11), kind=kLoop, calls=%fused_computation.54 | loop fusion | flops 8 | bytes 48 | tf_op jit(solution)/shard_map/reshape | solution.py:72
  0.8 0.5 collective-permute-start
  1.3 0.3 copy-done
  1.6 3.6 %fusion.32 = f16[512,512]{1,0:T(8,128)(2,1)} fusion(bf16[512,2048]{1,0:T(8,128)(2,1)S(1)} %copy-done, bf16[2048,2048]{1,0:T(8,128)(2,1)} %param.8, s32[]{:T(128)S(6)} %select_n.27), kind=kOutput, calls=%fused_computation.20 | convolution fusion | flops 1074266112 | bytes 4718596 | tf_op jit(solution)/shard_map/dot_general | solution.py:157
  5.3 0.0 collective-permute-done
  5.3 3.0 %collective-permute-start.1 = (s32[2,4]{1,0:T(2,128)S(1)}, s32[2,4]{1,0:T(2,128)S(1)}, u32[]{:S(2)}, u32[]{:S(2)}) collective-permute-start(s32[2,4]{1,0:T(2,128)S(1)} %pad_add_fusion.2), channel_id=1, source_target_pairs={{0,8},{4,12},{8,0},{12,4},{16,24},{20,28},{24,16},{28,20},{1,9},{5... | collective-permute-start | bytes 104 | tf_op jit(solution)/shard_map/ppermute | solution.py:75
  8.3 4.3 %collective-permute-start.3 = (f16[512,512]{1,0:T(8,128)(2,1)}, f16[512,512]{1,0:T(8,128)(2,1)}, u32[]{:S(2)}, u32[]{:S(2)}) collective-permute-start(f16[512,512]{1,0:T(8,128)(2,1)} %fusion.32), channel_id=1, source_target_pairs={{0,1},{3,2},{4,5},{7,6},{8,9},{11,10},{12,13},{15,14},{16,17},{19,... | collective-permute-start | bytes 1572872 | tf_op jit(solution)/shard_map/ppermute | solution.py:176
  12.5 1.5 %collective-permute-start.5 = (f16[512,512]{1,0:T(8,128)(2,1)}, f16[512,512]{1,0:T(8,128)(2,1)}, u32[]{:S(2)}, u32[]{:S(2)}) collective-permute-start(f16[512,512]{1,0:T(8,128)(2,1)} %fusion.32), channel_id=1, source_target_pairs={{1,2},{2,1},{5,6},{6,5},{9,10},{10,9},{13,14},{14,13},{17,18},{18,... | collective-permute-start | bytes 1572872 | tf_op jit(solution)/shard_map/ppermute | solution.py:178
  14.0 0.0 collective-permute-done.1
  14.0 1.6 %collective-permute-start.2 = (s32[4,4]{1,0:T(4,128)S(1)}, s32[4,4]{1,0:T(4,128)S(1)}, u32[]{:S(2)}, u32[]{:S(2)}) collective-permute-start(s32[4,4]{1,0:T(4,128)S(1)} %pad_add_fusion.1), channel_id=1, source_target_pairs={{0,16},{4,20},{8,24},{12,28},{16,0},{20,4},{24,8},{28,12},{1,17},{... | collective-permute-start | bytes 200 | tf_op jit(solution)/shard_map/ppermute | solution.py:75
  15.6 3.6 %fusion.29 = f16[512,512]{1,0:T(8,128)(2,1)} fusion(bf16[512,2048]{1,0:T(8,128)(2,1)S(1)} %copy-done, bf16[2048,2048]{1,0:T(8,128)(2,1)} %param.8, s32[]{:T(128)S(6)} %select_n.29), kind=kOutput, calls=%fused_computation.19 | convolution fusion | flops 1074266112 | bytes 4718596 | tf_op jit(solution)/shard_map/dot_general | solution.py:157
  19.2 0.5 collective-permute-start.4
  19.8 0.0 collective-permute-done.2
  19.8 0.6 %pad_add_fusion.ids_ref = s32[8,4]{1,0:T(8,128)} fusion(s32[4,4]{1,0:T(4,128)S(1)} %collective-permute-done.2, s32[2,4]{1,0:T(2,128)S(1)} %collective-permute-done.1, s32[1,4]{1,0:T(1,128)S(1)} %collective-permute-done, s32[1,4]{1,0:T(1,128)S(1)} %add_bitcast_fusion), kind=kLoop, calls=%fused_computation.41 | loop fusion | flops 96 | bytes 256 | tf_op jit(solution)/shard_map/concatenate | solution.py:76
  20.4 2.4 %shard_map.73 = bf16[8,2,16,2560]{3,2,1,0:T(8,128)(2,1)} custom-call(s32[8,4]{1,0:T(8,128)} %pad_add_fusion.ids_ref, s32[1]{0:T(128)} %bitcast.4.me_ref, bf16[128,16,2048]{2,1,0:T(8,128)(2,1)} %bitcast.33, bf16[128,16,512]{2,1,0:T(8,128)(2,1)} %up_ref.1), custom_call_target="tpu_custom_call" | custom-call | flops 1 | bytes 1 | tf_op jit(solution)/shard_map/pallas_call | solution.py:86
  22.8 3.6 %all-to-all-start = ((bf16[8,2,16,2560]{3,2,1,0:T(8,128)(2,1)}), bf16[8,2,16,2560]{3,2,1,0:T(8,128)(2,1)S(1)}, u32[]{:S(2)}, u32[]{:S(2)}) async-start(bf16[8,2,16,2560]{3,2,1,0:T(8,128)(2,1)} %shard_map.73), calls=%async_computation | async-start | bytes 2621440 | tf_op jit(solution)/shard_map/all_to_all | solution.py:104
  26.4 2.8 %fusion.20 = f32[512,512]{1,0:T(8,128)S(1)} fusion(bf16[512,2048]{1,0:T(8,128)(2,1)S(1)} %copy-done, bf16[2048,2048]{1,0:T(8,128)(2,1)} %param.8, s32[]{:T(128)S(6)} %select_n.31), kind=kOutput, calls=%fused_computation.13 | convolution fusion | flops 1073741824 | bytes 5242884 | tf_op jit(solution)/shard_map/dot_general | solution.py:157
  29.3 0.0 collective-permute-done.3
  29.3 2.1 %multiply_convert_fusion = f16[512,512]{1,0:T(8,128)(2,1)} fusion(f32[512,512]{1,0:T(8,128)S(1)} %fusion.20, f16[512,512]{1,0:T(8,128)(2,1)} %collective-permute-done.3), kind=kLoop, calls=%fused_computation.23 | loop fusion | flops 1310720 | bytes 2097152 | tf_op jit(solution)/shard_map/convert_element_type | solution.py:163
  31.3 1.5 %collective-permute-start.6 = (f16[512,512]{1,0:T(8,128)(2,1)}, f16[512,512]{1,0:T(8,128)(2,1)}, u32[]{:S(2)}, u32[]{:S(2)}) collective-permute-start(f16[512,512]{1,0:T(8,128)(2,1)} %multiply_convert_fusion), channel_id=1, source_target_pairs={{0,1},{3,2},{1,3},{2,0},{4,5},{7,6},{5,7},{6,4},{8,9},{11,10},{9,1... | collective-permute-start | bytes 1572872 | tf_op jit(solution)/shard_map/ppermute | solution.py:187
  32.9 0.0 copy-start.2
  32.9 2.8 %fusion.23 = f32[512,512]{1,0:T(8,128)S(1)} fusion(bf16[512,2048]{1,0:T(8,128)(2,1)S(1)} %copy-done, bf16[2048,2048]{1,0:T(8,128)(2,1)} %param.8, s32[]{:T(128)S(6)} %select_n.32), kind=kOutput, calls=%fused_computation.14 | convolution fusion | flops 1073741824 | bytes 5242884 | tf_op jit(solution)/shard_map/dot_general | solution.py:157
  35.7 0.0 copy-done.2
  35.7 0.1 iota_compare_fusion.2
  35.8 0.0 collective-permute-done.4
  35.8 2.2 %multiply_add_fusion.1 = f32[512,512]{1,0:T(8,128)} fusion(f32[512,512]{1,0:T(8,128)S(1)} %fusion.23, f16[512,512]{1,0:T(8,128)(2,1)} %collective-permute-done.4), kind=kLoop, calls=%fused_computation.22 | loop fusion | flops 786432 | bytes 2621440 | tf_op jit(solution)/shard_map/add | solution.py:190
  38.0 1.1 %shard_map.74 = s32[4]{0:T(128)} custom-call(s32[4]{0:T(128)} %bitcast.36), custom_call_target="tpu_custom_call" | custom-call | flops 99999997952 | bytes 1 | tf_op jit(solution)/shard_map/pallas_call | solution.py:110
  39.1 0.9 %convert_reduce_fusion = s32[4]{0:T(128)S(1)} fusion(s32[4]{0:T(128)} %shard_map.74), kind=kLoop, calls=%fused_computation.44 | loop fusion | flops 76 | bytes 32 | tf_op jit(solution)/shard_map/reduce_sum | solution.py:123
  40.0 0.6 %multiply_add_fusion.2 = s32[4]{0:T(128)S(1)} fusion(s32[4]{0:T(128)S(1)} %convert_reduce_fusion, s32[4]{0:T(128)} %shard_map.74), kind=kLoop, calls=%fused_computation.53 | loop fusion | flops 8 | bytes 48 | tf_op jit(solution)/shard_map/add | solution.py:123
  40.6 0.1 iota_compare_fusion
  40.7 3.9 %all-to-all-done = bf16[8,2,16,2560]{3,2,1,0:T(8,128)(2,1)S(1)} async-done(((bf16[8,2,16,2560]{3,2,1,0:T(8,128)(2,1)}), bf16[8,2,16,2560]{3,2,1,0:T(8,128)(2,1)S(1)}, u32[]{:S(2)}, u32[]{:S(2)}) %all-to-all-start) | async-done | bytes 1310752 | tf_op jit(solution)/shard_map/all_to_all | solution.py:104
  44.6 0.0 copy-start.1
  44.6 0.7 %select_reduce_fusion = bf16[4,16,2560]{2,1,0:T(8,128)(2,1)S(1)} fusion(pred[4,16]{1,0:T(4,128)(4,1)S(1)} %iota_compare_fusion, bf16[16,16,2560]{2,1,0:T(8,128)(2,1)S(1)} %bitcast.34), kind=kLoop, calls=%fused_computation | loop fusion | flops 5079040 | bytes 1638464 | tf_op jit(solution)/shard_map/reduce_sum | solution.py:129
  45.2 0.6 %fusion.53 = f32[4,16,128]{2,1,0:T(8,128)S(1)} fusion(bf16[4,16,2048]{2,1,0:T(8,128)(2,1)S(1)} %slice.8, bf16[4,128,2048]{2,1,0:T(8,128)(2,1)S(1)} %bitcast.32), kind=kOutput, calls=%fused_computation.56 | convolution fusion | flops 33554432 | bytes 2392064 | tf_op jit(solution)/shard_map/nbd,nrd->nrb/dot_general | solution.py:133
  45.9 2.5 %collective-permute-start.9 = (f32[4,16,128]{2,1,0:T(8,128)S(1)}, f32[4,16,128]{2,1,0:T(8,128)S(1)}, u32[]{:S(2)}, u32[]{:S(2)}) collective-permute-start(f32[4,16,128]{2,1,0:T(8,128)S(1)} %fusion.53), channel_id=1, source_target_pairs={{0,3},{1,2},{2,1},{3,0},{4,7},{5,6},{6,5},{7,4},{8,11},{9,10},{10,... | collective-permute-start | bytes 98312 | tf_op jit(solution)/shard_map/ppermute | solution.py:202
  48.4 0.5 collective-permute-start.8
  48.9 1.4 %collective-permute-start.7 = (f32[4,16,128]{2,1,0:T(8,128)S(1)}, f32[4,16,128]{2,1,0:T(8,128)S(1)}, u32[]{:S(2)}, u32[]{:S(2)}) collective-permute-start(f32[4,16,128]{2,1,0:T(8,128)S(1)} %fusion.53), channel_id=1, source_target_pairs={{0,1},{1,0},{2,3},{3,2},{4,5},{5,4},{6,7},{7,6},{8,9},{9,8},{10,11... | collective-permute-start | bytes 98312 | tf_op jit(solution)/shard_map/ppermute | solution.py:202
  50.3 0.0 collective-permute-done.6
  50.3 0.0 collective-permute-done.5
  50.3 0.0 copy-done.1
  50.3 1.4 %multiply_add_fusion = f32[512,512]{1,0:T(8,128)S(1)} fusion(f16[512,512]{1,0:T(8,128)(2,1)} %collective-permute-done.6, f32[512,512]{1,0:T(8,128)S(1)} %copy-done.1, f16[512,512]{1,0:T(8,128)(2,1)} %collective-permute-done.5), kind=kLoop, calls=%fused_computation.21 | loop fusion | flops 1572864 | bytes 3145728 | tf_op jit(solution)/shard_map/add | solution.py:194
  51.8 0.0 collective-permute-done.9
  51.8 1.8 %collective-permute-done.8 = f32[4,16,128]{2,1,0:T(8,128)S(1)} collective-permute-done((f32[4,16,128]{2,1,0:T(8,128)S(1)}, f32[4,16,128]{2,1,0:T(8,128)S(1)}, u32[]{:S(2)}, u32[]{:S(2)}) %collective-permute-start.8) | collective-permute-done | bytes 32800 | tf_op jit(solution)/shard_map/ppermute | solution.py:202
  53.5 0.0 collective-permute-done.7
  53.6 1.2 %fusion.28 = bf16[4,128,512]{2,1,0:T(8,128)(2,1)} fusion(f32[4,128,512]{2,1,0:T(8,128)S(1)} %bitcast.35, pred[4,128]{1,0:T(4,128)(4,1)S(1)} %iota_compare_fusion.2, bf16[4,16,512]{2,1,0:T(8,128)(2,1)S(1)} %slice.9, bf16[4,16,128]{2,1,0:T(8,128)(2,1)S(1)} %get-tuple-element.32, bf16[4,16,128]{2,1,0:T(8,128)(2,1)S(1)} %get-tuple-element.31, ...), kind=kOutput, calls=%fused_computation.18 | convolution fusion | flops 26951680 | bytes 1688064 | tf_op jit(solution)/shard_map/nrb,nro->nbo/dot_general | solution.py:146
  (6 shorter events, 0.1 us)
Async XLA Ops:
  0.0 1.6 %copy-start = (bf16[512,2048]{1,0:T(8,128)(2,1)S(1)}, bf16[512,2048]{1,0:T(8,128)(2,1)}, u32[]{:S(2)}) copy-start(bf16[512,2048]{1,0:T(8,128)(2,1)} %param.7) | copy-start | bytes 6291460
  0.8 4.4 %collective-permute-start = (s32[1,4]{1,0:T(1,128)S(1)}, s32[1,4]{1,0:T(1,128)S(1)}, u32[]{:S(2)}, u32[]{:S(2)}) collective-permute-start(s32[1,4]{1,0:T(1,128)S(1)} %add_bitcast_fusion), channel_id=1, source_target_pairs={{0,4},{4,0},{8,12},{12,8},{16,20},{20,16},{24,28},{28,24},{1,5},{5... | collective-permute-start | bytes 56 | tf_op jit(solution)/shard_map/ppermute | solution.py:75
  5.3 8.7 %collective-permute-start.1 = (s32[2,4]{1,0:T(2,128)S(1)}, s32[2,4]{1,0:T(2,128)S(1)}, u32[]{:S(2)}, u32[]{:S(2)}) collective-permute-start(s32[2,4]{1,0:T(2,128)S(1)} %pad_add_fusion.2), channel_id=1, source_target_pairs={{0,8},{4,12},{8,0},{12,4},{16,24},{20,28},{24,16},{28,20},{1,9},{5... | collective-permute-start | bytes 104 | tf_op jit(solution)/shard_map/ppermute | solution.py:75
  8.3 21.0 %collective-permute-start.3 = (f16[512,512]{1,0:T(8,128)(2,1)}, f16[512,512]{1,0:T(8,128)(2,1)}, u32[]{:S(2)}, u32[]{:S(2)}) collective-permute-start(f16[512,512]{1,0:T(8,128)(2,1)} %fusion.32), channel_id=1, source_target_pairs={{0,1},{3,2},{4,5},{7,6},{8,9},{11,10},{12,13},{15,14},{16,17},{19,... | collective-permute-start | bytes 1572872 | tf_op jit(solution)/shard_map/ppermute | solution.py:176
  12.5 37.8 %collective-permute-start.5 = (f16[512,512]{1,0:T(8,128)(2,1)}, f16[512,512]{1,0:T(8,128)(2,1)}, u32[]{:S(2)}, u32[]{:S(2)}) collective-permute-start(f16[512,512]{1,0:T(8,128)(2,1)} %fusion.32), channel_id=1, source_target_pairs={{1,2},{2,1},{5,6},{6,5},{9,10},{10,9},{13,14},{14,13},{17,18},{18,... | collective-permute-start | bytes 1572872 | tf_op jit(solution)/shard_map/ppermute | solution.py:178
  14.0 5.8 %collective-permute-start.2 = (s32[4,4]{1,0:T(4,128)S(1)}, s32[4,4]{1,0:T(4,128)S(1)}, u32[]{:S(2)}, u32[]{:S(2)}) collective-permute-start(s32[4,4]{1,0:T(4,128)S(1)} %pad_add_fusion.1), channel_id=1, source_target_pairs={{0,16},{4,20},{8,24},{12,28},{16,0},{20,4},{24,8},{28,12},{1,17},{... | collective-permute-start | bytes 200 | tf_op jit(solution)/shard_map/ppermute | solution.py:75
  19.2 16.6 %collective-permute-start.4 = (f16[512,512]{1,0:T(8,128)(2,1)}, f16[512,512]{1,0:T(8,128)(2,1)}, u32[]{:S(2)}, u32[]{:S(2)}) collective-permute-start(f16[512,512]{1,0:T(8,128)(2,1)} %fusion.29), channel_id=1, source_target_pairs={{0,2},{3,1},{1,0},{2,3},{4,6},{7,5},{5,4},{6,7},{8,10},{11,9},{9,8... | collective-permute-start | bytes 1572872 | tf_op jit(solution)/shard_map/ppermute | solution.py:181
  22.8 21.7 %all-to-all-start = ((bf16[8,2,16,2560]{3,2,1,0:T(8,128)(2,1)}), bf16[8,2,16,2560]{3,2,1,0:T(8,128)(2,1)S(1)}, u32[]{:S(2)}, u32[]{:S(2)}) async-start(bf16[8,2,16,2560]{3,2,1,0:T(8,128)(2,1)} %shard_map.73), calls=%async_computation | async-start | bytes 2621440 | tf_op jit(solution)/shard_map/all_to_all | solution.py:104
  31.3 19.0 %collective-permute-start.6 = (f16[512,512]{1,0:T(8,128)(2,1)}, f16[512,512]{1,0:T(8,128)(2,1)}, u32[]{:S(2)}, u32[]{:S(2)}) collective-permute-start(f16[512,512]{1,0:T(8,128)(2,1)} %multiply_convert_fusion), channel_id=1, source_target_pairs={{0,1},{3,2},{1,3},{2,0},{4,5},{7,6},{5,7},{6,4},{8,9},{11,10},{9,1... | collective-permute-start | bytes 1572872 | tf_op jit(solution)/shard_map/ppermute | solution.py:187
  32.9 2.9 %copy-start.2 = (s32[4]{0:T(128)S(1)}, s32[4]{0:T(128)}, u32[]{:S(2)}) copy-start(s32[4]{0:T(128)} %param.13) | copy-start | bytes 52
  44.6 5.7 %copy-start.1 = (f32[512,512]{1,0:T(8,128)S(1)}, f32[512,512]{1,0:T(8,128)}, u32[]{:S(2)}) copy-start(f32[512,512]{1,0:T(8,128)} %multiply_add_fusion.1) | copy-start | bytes 3145732
  45.9 5.9 %collective-permute-start.9 = (f32[4,16,128]{2,1,0:T(8,128)S(1)}, f32[4,16,128]{2,1,0:T(8,128)S(1)}, u32[]{:S(2)}, u32[]{:S(2)}) collective-permute-start(f32[4,16,128]{2,1,0:T(8,128)S(1)} %fusion.53), channel_id=1, source_target_pairs={{0,3},{1,2},{2,1},{3,0},{4,7},{5,6},{6,5},{7,4},{8,11},{9,10},{10,... | collective-permute-start | bytes 98312 | tf_op jit(solution)/shard_map/ppermute | solution.py:202
  48.4 5.2 %collective-permute-start.8 = (f32[4,16,128]{2,1,0:T(8,128)S(1)}, f32[4,16,128]{2,1,0:T(8,128)S(1)}, u32[]{:S(2)}, u32[]{:S(2)}) collective-permute-start(f32[4,16,128]{2,1,0:T(8,128)S(1)} %fusion.53), channel_id=1, source_target_pairs={{0,2},{1,3},{2,0},{3,1},{4,6},{5,7},{6,4},{7,5},{8,10},{9,11},{10,... | collective-permute-start | bytes 98312 | tf_op jit(solution)/shard_map/ppermute | solution.py:202
  48.9 4.7 %collective-permute-start.7 = (f32[4,16,128]{2,1,0:T(8,128)S(1)}, f32[4,16,128]{2,1,0:T(8,128)S(1)}, u32[]{:S(2)}, u32[]{:S(2)}) collective-permute-start(f32[4,16,128]{2,1,0:T(8,128)S(1)} %fusion.53), channel_id=1, source_target_pairs={{0,1},{1,0},{2,3},{3,2},{4,5},{5,4},{6,7},{7,6},{8,9},{9,8},{10,11... | collective-permute-start | bytes 98312 | tf_op jit(solution)/shard_map/ppermute | solution.py:202

commit v8 on v7

--- a/solution.py
+++ b/solution.py
@@ -188,7 +188,7 @@
         own = lax.optimization_barrier(product(after(z, second)))
         live_counts = after(block_count, own)
         base_projection = lax.optimization_barrier(own + plain(from_first))
-        block_slot = slot_plan(later(owners, base_projection))
+        block_slot = slot_plan(later(owners, own))
         reduced, up_block = reduce_tokens(tokens, got, block_slot)
         from_second = after(from_second, reduced)
         base_projection = lax.optimization_barrier(base_projection + plain(from_inner) + plain(from_second))

time: 55.4 us -> 55.3 us (level)
  waiting for transfers between devices: 5.69 us -> 4.42 us
  matrix products: 14.8 us -> 15.7 us
    all_to_all x1, waiting for transfers between devices: 3.89 us -> 2.62 us  [exchange(): got = lax.all_to_all(packed, 'grp', split_axis=0, concat_axis=0, tiled=True)]
    dot_general x4, matrix products: 13 us -> 13.9 us  [product(): value = jnp.dot(tokens, columns, preferred_element_type=jnp.float32)]
  transfers between devices with their start and end apart: 11 -> 11, of which waited for: 2 -> 2; matrix products, arithmetic and copies ran while one was open for 41% -> 43% of each run, Pallas kernels for 6% -> 7%
where the time goes in v8:
time: 55.3 us; the launch traced here: 54.8 us
  starting transfers between devices  20.8 us (38%)
  matrix products  15.7 us (28%)
  other arithmetic  9.76 us (18%)
  waiting for transfers between devices  4.42 us (8%)
  Pallas kernels  3.66 us (7%)
    dot_general x4, matrix products, product(): value = jnp.dot(tokens, columns, preferred_element_type=jnp.float32)  13.9 us
    ppermute x3, starting transfers between devices, adapter_ids(): lax.ppermute(ids, 'grp', [(i, i ^ step) for i in range(group_count)])  5.04 us
    ppermute x3, starting transfers between devices, body(): lax.ppermute(reduced, 'tp', [(i, i ^ j) for i in range(tp_count)])  4.4 us
    ppermute x1, starting transfers between devices, body(): to_inner = lax.ppermute(far, 'tp', [(0, 1), (3, 2)])  4.27 us
    all_to_all x1, starting transfers between devices, exchange(): got = lax.all_to_all(packed, 'grp', split_axis=0, concat_axis=0, tiled=True)  3.58 us
    all_to_all x1, waiting for transfers between devices, exchange(): got = lax.all_to_all(packed, 'grp', split_axis=0, concat_axis=0, tiled=True)  2.62 us
    pallas_call x1, Pallas kernels, pack_adapters(): pl.pallas_call(pack_kernel, out_shape=jax.ShapeDtypeStruct((group_count,...  2.54 us
    add x1, other arithmetic, body(): base_projection = lax.optimization_barrier(own + plain(from_first))  2.47 us
  transfers between devices with their start and end apart: 11, of which 2 were waited for; matrix products, arithmetic and copies ran while one was open for 43% of the time, Pallas kernels for 7%

profile of v8, /device:TPU:0, one launch (start us, length us, event | category | flops | bytes accessed | tf_op | source)
XLA Modules:
  0.0 54.8 jit_solution(4143042363569525477)
XLA Ops:
  0.0 0.0 copy-start
  0.0 0.8 %add_bitcast_fusion = s32[1,4]{1,0:T(1,128)S(1)} fusion(s32[4]{0:T(128)} %param.12, s32[4,1]{0,1:T(1,128)} %param.11), kind=kLoop, calls=%fused_computation.54 | loop fusion | flops 8 | bytes 48 | tf_op jit(solution)/shard_map/reshape | solution.py:72
  0.8 0.5 collective-permute-start
  1.3 0.3 copy-done
  1.6 3.6 %fusion.32 = f16[512,512]{1,0:T(8,128)(2,1)} fusion(bf16[512,2048]{1,0:T(8,128)(2,1)S(1)} %copy-done, bf16[2048,2048]{1,0:T(8,128)(2,1)} %param.8, s32[]{:T(128)S(6)} %select_n.27), kind=kOutput, calls=%fused_computation.20 | convolution fusion | flops 1074266112 | bytes 4718596 | tf_op jit(solution)/shard_map/dot_general | solution.py:157
  5.3 0.0 collective-permute-done
  5.3 3.0 %collective-permute-start.1 = (s32[2,4]{1,0:T(2,128)S(1)}, s32[2,4]{1,0:T(2,128)S(1)}, u32[]{:S(2)}, u32[]{:S(2)}) collective-permute-start(s32[2,4]{1,0:T(2,128)S(1)} %pad_add_fusion.2), channel_id=1, source_target_pairs={{0,8},{4,12},{8,0},{12,4},{16,24},{20,28},{24,16},{28,20},{1,9},{5... | collective-permute-start | bytes 104 | tf_op jit(solution)/shard_map/ppermute | solution.py:75
  8.3 4.3 %collective-permute-start.3 = (f16[512,512]{1,0:T(8,128)(2,1)}, f16[512,512]{1,0:T(8,128)(2,1)}, u32[]{:S(2)}, u32[]{:S(2)}) collective-permute-start(f16[512,512]{1,0:T(8,128)(2,1)} %fusion.32), channel_id=1, source_target_pairs={{0,1},{3,2},{4,5},{7,6},{8,9},{11,10},{12,13},{15,14},{16,17},{19,... | collective-permute-start | bytes 1572872 | tf_op jit(solution)/shard_map/ppermute | solution.py:176
  12.5 1.5 %collective-permute-start.5 = (f16[512,512]{1,0:T(8,128)(2,1)}, f16[512,512]{1,0:T(8,128)(2,1)}, u32[]{:S(2)}, u32[]{:S(2)}) collective-permute-start(f16[512,512]{1,0:T(8,128)(2,1)} %fusion.32), channel_id=1, source_target_pairs={{1,2},{2,1},{5,6},{6,5},{9,10},{10,9},{13,14},{14,13},{17,18},{18,... | collective-permute-start | bytes 1572872 | tf_op jit(solution)/shard_map/ppermute | solution.py:178
  14.0 0.0 collective-permute-done.1
  14.0 1.6 %collective-permute-start.2 = (s32[4,4]{1,0:T(4,128)S(1)}, s32[4,4]{1,0:T(4,128)S(1)}, u32[]{:S(2)}, u32[]{:S(2)}) collective-permute-start(s32[4,4]{1,0:T(4,128)S(1)} %pad_add_fusion.1), channel_id=1, source_target_pairs={{0,16},{4,20},{8,24},{12,28},{16,0},{20,4},{24,8},{28,12},{1,17},{... | collective-permute-start | bytes 200 | tf_op jit(solution)/shard_map/ppermute | solution.py:75
  15.6 3.6 %fusion.29 = f16[512,512]{1,0:T(8,128)(2,1)} fusion(bf16[512,2048]{1,0:T(8,128)(2,1)S(1)} %copy-done, bf16[2048,2048]{1,0:T(8,128)(2,1)} %param.8, s32[]{:T(128)S(6)} %select_n.29), kind=kOutput, calls=%fused_computation.19 | convolution fusion | flops 1074266112 | bytes 4718596 | tf_op jit(solution)/shard_map/dot_general | solution.py:157
  19.2 0.5 collective-permute-start.4
  19.8 0.0 collective-permute-done.2
  19.8 0.6 %pad_add_fusion.ids_ref = s32[8,4]{1,0:T(8,128)} fusion(s32[4,4]{1,0:T(4,128)S(1)} %collective-permute-done.2, s32[2,4]{1,0:T(2,128)S(1)} %collective-permute-done.1, s32[1,4]{1,0:T(1,128)S(1)} %collective-permute-done, s32[1,4]{1,0:T(1,128)S(1)} %add_bitcast_fusion), kind=kLoop, calls=%fused_computation.41 | loop fusion | flops 96 | bytes 256 | tf_op jit(solution)/shard_map/concatenate | solution.py:76
  20.4 2.5 %shard_map.73 = bf16[8,2,16,2560]{3,2,1,0:T(8,128)(2,1)} custom-call(s32[8,4]{1,0:T(8,128)} %pad_add_fusion.ids_ref, s32[1]{0:T(128)} %bitcast.4.me_ref, bf16[128,16,2048]{2,1,0:T(8,128)(2,1)} %bitcast.33, bf16[128,16,512]{2,1,0:T(8,128)(2,1)} %up_ref.1), custom_call_target="tpu_custom_call" | custom-call | flops 1 | bytes 1 | tf_op jit(solution)/shard_map/pallas_call | solution.py:86
  22.9 3.6 %all-to-all-start = ((bf16[8,2,16,2560]{3,2,1,0:T(8,128)(2,1)}), bf16[8,2,16,2560]{3,2,1,0:T(8,128)(2,1)S(1)}, u32[]{:S(2)}, u32[]{:S(2)}) async-start(bf16[8,2,16,2560]{3,2,1,0:T(8,128)(2,1)} %shard_map.73), calls=%async_computation | async-start | bytes 2621440 | tf_op jit(solution)/shard_map/all_to_all | solution.py:104
  26.5 2.8 %fusion.20 = f32[512,512]{1,0:T(8,128)S(1)} fusion(bf16[512,2048]{1,0:T(8,128)(2,1)S(1)} %copy-done, bf16[2048,2048]{1,0:T(8,128)(2,1)} %param.8, s32[]{:T(128)S(6)} %select_n.31), kind=kOutput, calls=%fused_computation.13 | convolution fusion | flops 1073741824 | bytes 5242884 | tf_op jit(solution)/shard_map/dot_general | solution.py:157
  29.4 0.0 collective-permute-done.3
  29.4 2.1 %multiply_convert_fusion = f16[512,512]{1,0:T(8,128)(2,1)} fusion(f32[512,512]{1,0:T(8,128)S(1)} %fusion.20, f16[512,512]{1,0:T(8,128)(2,1)} %collective-permute-done.3), kind=kLoop, calls=%fused_computation.23 | loop fusion | flops 1310720 | bytes 2097152 | tf_op jit(solution)/shard_map/convert_element_type | solution.py:163
  31.4 1.5 %collective-permute-start.6 = (f16[512,512]{1,0:T(8,128)(2,1)}, f16[512,512]{1,0:T(8,128)(2,1)}, u32[]{:S(2)}, u32[]{:S(2)}) collective-permute-start(f16[512,512]{1,0:T(8,128)(2,1)} %multiply_convert_fusion), channel_id=1, source_target_pairs={{0,1},{3,2},{1,3},{2,0},{4,5},{7,6},{5,7},{6,4},{8,9},{11,10},{9,1... | collective-permute-start | bytes 1572872 | tf_op jit(solution)/shard_map/ppermute | solution.py:187
  33.0 3.8 %fusion.23 = f32[512,512]{1,0:T(8,128)} fusion(bf16[512,2048]{1,0:T(8,128)(2,1)S(1)} %copy-done, bf16[2048,2048]{1,0:T(8,128)(2,1)} %param.8, s32[]{:T(128)S(6)} %select_n.32), kind=kOutput, calls=%fused_computation.14 | convolution fusion | flops 1073741824 | bytes 5242884 | tf_op jit(solution)/shard_map/dot_general | solution.py:157
  36.8 0.0 copy-start.2
  36.8 1.1 %shard_map.74 = s32[4]{0:T(128)} custom-call(s32[4]{0:T(128)} %bitcast.36), custom_call_target="tpu_custom_call" | custom-call | flops 99999997952 | bytes 1 | tf_op jit(solution)/shard_map/pallas_call | solution.py:110
  37.9 0.9 %convert_reduce_fusion = s32[4]{0:T(128)S(1)} fusion(s32[4]{0:T(128)} %shard_map.74), kind=kLoop, calls=%fused_computation.44 | loop fusion | flops 76 | bytes 32 | tf_op jit(solution)/shard_map/reduce_sum | solution.py:123
  38.8 0.6 %multiply_add_fusion.2 = s32[4]{0:T(128)S(1)} fusion(s32[4]{0:T(128)S(1)} %convert_reduce_fusion, s32[4]{0:T(128)} %shard_map.74), kind=kLoop, calls=%fused_computation.53 | loop fusion | flops 8 | bytes 48 | tf_op jit(solution)/shard_map/add | solution.py:123
  39.4 0.1 iota_compare_fusion
  39.5 0.0 copy-done.2
  39.5 0.1 iota_compare_fusion.2
  39.6 0.0 collective-permute-done.4
  39.6 2.5 %multiply_add_fusion.1 = f32[512,512]{1,0:T(8,128)} fusion(f32[512,512]{1,0:T(8,128)} %fusion.23, f16[512,512]{1,0:T(8,128)(2,1)} %collective-permute-done.4), kind=kLoop, calls=%fused_computation.22 | loop fusion | flops 786432 | bytes 2621440 | tf_op jit(solution)/shard_map/add | solution.py:190
  42.0 2.6 %all-to-all-done = bf16[8,2,16,2560]{3,2,1,0:T(8,128)(2,1)S(1)} async-done(((bf16[8,2,16,2560]{3,2,1,0:T(8,128)(2,1)}), bf16[8,2,16,2560]{3,2,1,0:T(8,128)(2,1)S(1)}, u32[]{:S(2)}, u32[]{:S(2)}) %all-to-all-start) | async-done | bytes 1310752 | tf_op jit(solution)/shard_map/all_to_all | solution.py:104
  44.7 0.0 copy-start.1
  44.7 0.7 %select_reduce_fusion = bf16[4,16,2560]{2,1,0:T(8,128)(2,1)S(1)} fusion(pred[4,16]{1,0:T(4,128)(4,1)S(1)} %iota_compare_fusion, bf16[16,16,2560]{2,1,0:T(8,128)(2,1)S(1)} %bitcast.34), kind=kLoop, calls=%fused_computation | loop fusion | flops 5079040 | bytes 1638464 | tf_op jit(solution)/shard_map/reduce_sum | solution.py:129
  45.3 0.6 %fusion.53 = f32[4,16,128]{2,1,0:T(8,128)S(1)} fusion(bf16[4,16,2048]{2,1,0:T(8,128)(2,1)S(1)} %slice.8, bf16[4,128,2048]{2,1,0:T(8,128)(2,1)S(1)} %bitcast.32), kind=kOutput, calls=%fused_computation.56 | convolution fusion | flops 33554432 | bytes 2392064 | tf_op jit(solution)/shard_map/nbd,nrd->nrb/dot_general | solution.py:133
  46.0 2.5 %collective-permute-start.9 = (f32[4,16,128]{2,1,0:T(8,128)S(1)}, f32[4,16,128]{2,1,0:T(8,128)S(1)}, u32[]{:S(2)}, u32[]{:S(2)}) collective-permute-start(f32[4,16,128]{2,1,0:T(8,128)S(1)} %fusion.53), channel_id=1, source_target_pairs={{0,3},{1,2},{2,1},{3,0},{4,7},{5,6},{6,5},{7,4},{8,11},{9,10},{10,... | collective-permute-start | bytes 98312 | tf_op jit(solution)/shard_map/ppermute | solution.py:202
  48.5 0.5 collective-permute-start.8
  49.0 1.4 %collective-permute-start.7 = (f32[4,16,128]{2,1,0:T(8,128)S(1)}, f32[4,16,128]{2,1,0:T(8,128)S(1)}, u32[]{:S(2)}, u32[]{:S(2)}) collective-permute-start(f32[4,16,128]{2,1,0:T(8,128)S(1)} %fusion.53), channel_id=1, source_target_pairs={{0,1},{1,0},{2,3},{3,2},{4,5},{5,4},{6,7},{7,6},{8,9},{9,8},{10,11... | collective-permute-start | bytes 98312 | tf_op jit(solution)/shard_map/ppermute | solution.py:202
  50.4 0.0 collective-permute-done.6
  50.4 0.0 collective-permute-done.5
  50.4 0.0 copy-done.1
  50.4 1.4 %multiply_add_fusion = f32[512,512]{1,0:T(8,128)S(1)} fusion(f16[512,512]{1,0:T(8,128)(2,1)} %collective-permute-done.6, f32[512,512]{1,0:T(8,128)S(1)} %copy-done.1, f16[512,512]{1,0:T(8,128)(2,1)} %collective-permute-done.5), kind=kLoop, calls=%fused_computation.21 | loop fusion | flops 1572864 | bytes 3145728 | tf_op jit(solution)/shard_map/add | solution.py:194
  51.9 0.0 collective-permute-done.9
  51.9 1.8 %collective-permute-done.8 = f32[4,16,128]{2,1,0:T(8,128)S(1)} collective-permute-done((f32[4,16,128]{2,1,0:T(8,128)S(1)}, f32[4,16,128]{2,1,0:T(8,128)S(1)}, u32[]{:S(2)}, u32[]{:S(2)}) %collective-permute-start.8) | collective-permute-done | bytes 32800 | tf_op jit(solution)/shard_map/ppermute | solution.py:202
  53.6 0.0 collective-permute-done.7
  53.7 1.2 %fusion.28 = bf16[4,128,512]{2,1,0:T(8,128)(2,1)} fusion(f32[4,128,512]{2,1,0:T(8,128)S(1)} %bitcast.35, pred[4,128]{1,0:T(4,128)(4,1)S(1)} %iota_compare_fusion.2, bf16[4,16,512]{2,1,0:T(8,128)(2,1)S(1)} %slice.9, bf16[4,16,128]{2,1,0:T(8,128)(2,1)S(1)} %get-tuple-element.32, bf16[4,16,128]{2,1,0:T(8,128)(2,1)S(1)} %get-tuple-element.31, ...), kind=kOutput, calls=%fused_computation.18 | convolution fusion | flops 26951680 | bytes 1688064 | tf_op jit(solution)/shard_map/nrb,nro->nbo/dot_general | solution.py:146
  (6 shorter events, 0.1 us)
Async XLA Ops:
  0.0 1.6 %copy-start = (bf16[512,2048]{1,0:T(8,128)(2,1)S(1)}, bf16[512,2048]{1,0:T(8,128)(2,1)}, u32[]{:S(2)}) copy-start(bf16[512,2048]{1,0:T(8,128)(2,1)} %param.7) | copy-start | bytes 6291460
  0.8 4.4 %collective-permute-start = (s32[1,4]{1,0:T(1,128)S(1)}, s32[1,4]{1,0:T(1,128)S(1)}, u32[]{:S(2)}, u32[]{:S(2)}) collective-permute-start(s32[1,4]{1,0:T(1,128)S(1)} %add_bitcast_fusion), channel_id=1, source_target_pairs={{0,4},{4,0},{8,12},{12,8},{16,20},{20,16},{24,28},{28,24},{1,5},{5... | collective-permute-start | bytes 56 | tf_op jit(solution)/shard_map/ppermute | solution.py:75
  5.3 8.7 %collective-permute-start.1 = (s32[2,4]{1,0:T(2,128)S(1)}, s32[2,4]{1,0:T(2,128)S(1)}, u32[]{:S(2)}, u32[]{:S(2)}) collective-permute-start(s32[2,4]{1,0:T(2,128)S(1)} %pad_add_fusion.2), channel_id=1, source_target_pairs={{0,8},{4,12},{8,0},{12,4},{16,24},{20,28},{24,16},{28,20},{1,9},{5... | collective-permute-start | bytes 104 | tf_op jit(solution)/shard_map/ppermute | solution.py:75
  8.3 21.1 %collective-permute-start.3 = (f16[512,512]{1,0:T(8,128)(2,1)}, f16[512,512]{1,0:T(8,128)(2,1)}, u32[]{:S(2)}, u32[]{:S(2)}) collective-permute-start(f16[512,512]{1,0:T(8,128)(2,1)} %fusion.32), channel_id=1, source_target_pairs={{0,1},{3,2},{4,5},{7,6},{8,9},{11,10},{12,13},{15,14},{16,17},{19,... | collective-permute-start | bytes 1572872 | tf_op jit(solution)/shard_map/ppermute | solution.py:176
  12.5 37.9 %collective-permute-start.5 = (f16[512,512]{1,0:T(8,128)(2,1)}, f16[512,512]{1,0:T(8,128)(2,1)}, u32[]{:S(2)}, u32[]{:S(2)}) collective-permute-start(f16[512,512]{1,0:T(8,128)(2,1)} %fusion.32), channel_id=1, source_target_pairs={{1,2},{2,1},{5,6},{6,5},{9,10},{10,9},{13,14},{14,13},{17,18},{18,... | collective-permute-start | bytes 1572872 | tf_op jit(solution)/shard_map/ppermute | solution.py:178
  14.0 5.7 %collective-permute-start.2 = (s32[4,4]{1,0:T(4,128)S(1)}, s32[4,4]{1,0:T(4,128)S(1)}, u32[]{:S(2)}, u32[]{:S(2)}) collective-permute-start(s32[4,4]{1,0:T(4,128)S(1)} %pad_add_fusion.1), channel_id=1, source_target_pairs={{0,16},{4,20},{8,24},{12,28},{16,0},{20,4},{24,8},{28,12},{1,17},{... | collective-permute-start | bytes 200 | tf_op jit(solution)/shard_map/ppermute | solution.py:75
  19.2 20.3 %collective-permute-start.4 = (f16[512,512]{1,0:T(8,128)(2,1)}, f16[512,512]{1,0:T(8,128)(2,1)}, u32[]{:S(2)}, u32[]{:S(2)}) collective-permute-start(f16[512,512]{1,0:T(8,128)(2,1)} %fusion.29), channel_id=1, source_target_pairs={{0,2},{3,1},{1,0},{2,3},{4,6},{7,5},{5,4},{6,7},{8,10},{11,9},{9,8... | collective-permute-start | bytes 1572872 | tf_op jit(solution)/shard_map/ppermute | solution.py:181
  22.9 21.7 %all-to-all-start = ((bf16[8,2,16,2560]{3,2,1,0:T(8,128)(2,1)}), bf16[8,2,16,2560]{3,2,1,0:T(8,128)(2,1)S(1)}, u32[]{:S(2)}, u32[]{:S(2)}) async-start(bf16[8,2,16,2560]{3,2,1,0:T(8,128)(2,1)} %shard_map.73), calls=%async_computation | async-start | bytes 2621440 | tf_op jit(solution)/shard_map/all_to_all | solution.py:104
  31.4 19.0 %collective-permute-start.6 = (f16[512,512]{1,0:T(8,128)(2,1)}, f16[512,512]{1,0:T(8,128)(2,1)}, u32[]{:S(2)}, u32[]{:S(2)}) collective-permute-start(f16[512,512]{1,0:T(8,128)(2,1)} %multiply_convert_fusion), channel_id=1, source_target_pairs={{0,1},{3,2},{1,3},{2,0},{4,5},{7,6},{5,7},{6,4},{8,9},{11,10},{9,1... | collective-permute-start | bytes 1572872 | tf_op jit(solution)/shard_map/ppermute | solution.py:187
  36.8 2.7 %copy-start.2 = (s32[4]{0:T(128)S(1)}, s32[4]{0:T(128)}, u32[]{:S(2)}) copy-start(s32[4]{0:T(128)} %param.13) | copy-start | bytes 52
  44.7 5.7 %copy-start.1 = (f32[512,512]{1,0:T(8,128)S(1)}, f32[512,512]{1,0:T(8,128)}, u32[]{:S(2)}) copy-start(f32[512,512]{1,0:T(8,128)} %multiply_add_fusion.1) | copy-start | bytes 3145732
  46.0 5.9 %collective-permute-start.9 = (f32[4,16,128]{2,1,0:T(8,128)S(1)}, f32[4,16,128]{2,1,0:T(8,128)S(1)}, u32[]{:S(2)}, u32[]{:S(2)}) collective-permute-start(f32[4,16,128]{2,1,0:T(8,128)S(1)} %fusion.53), channel_id=1, source_target_pairs={{0,3},{1,2},{2,1},{3,0},{4,7},{5,6},{6,5},{7,4},{8,11},{9,10},{10,... | collective-permute-start | bytes 98312 | tf_op jit(solution)/shard_map/ppermute | solution.py:202
  48.5 5.2 %collective-permute-start.8 = (f32[4,16,128]{2,1,0:T(8,128)S(1)}, f32[4,16,128]{2,1,0:T(8,128)S(1)}, u32[]{:S(2)}, u32[]{:S(2)}) collective-permute-start(f32[4,16,128]{2,1,0:T(8,128)S(1)} %fusion.53), channel_id=1, source_target_pairs={{0,2},{1,3},{2,0},{3,1},{4,6},{5,7},{6,4},{7,5},{8,10},{9,11},{10,... | collective-permute-start | bytes 98312 | tf_op jit(solution)/shard_map/ppermute | solution.py:202
  49.0 4.7 %collective-permute-start.7 = (f32[4,16,128]{2,1,0:T(8,128)S(1)}, f32[4,16,128]{2,1,0:T(8,128)S(1)}, u32[]{:S(2)}, u32[]{:S(2)}) collective-permute-start(f32[4,16,128]{2,1,0:T(8,128)S(1)} %fusion.53), channel_id=1, source_target_pairs={{0,1},{1,0},{2,3},{3,2},{4,5},{5,4},{6,7},{7,6},{8,9},{9,8},{10,11... | collective-permute-start | bytes 98312 | tf_op jit(solution)/shard_map/ppermute | solution.py:202

commit v9 on v7

--- a/solution.py
+++ b/solution.py
@@ -127,8 +127,7 @@
     blocks, cols = block_slot.shape[0], tokens.shape[1]
     match = block_slot[:, None] == jnp.arange(got.shape[0], dtype=jnp.int32)[None, :]
     mine = jnp.sum(jnp.where(match[:, :, None, None], got[None], jnp.bfloat16(0.0)).astype(jnp.float32), axis=1).astype(jnp.bfloat16)
-    mine = lax.optimization_barrier(mine)
-    down_block = lax.optimization_barrier(mine[:, :, :cols])
+    down_block = mine[:, :, :cols]
     blocked = tokens.reshape(blocks, BLOCK, cols)
     reduced = jnp.einsum("nbd,nrd->nrb", blocked, down_block, preferred_element_type=jnp.float32)
     up_block, _ = lax.optimization_barrier((mine[:, :, cols:], reduced))

time: 55.4 us -> 55.5 us (level)
  transfers between devices with their start and end apart: 11 -> 11, of which waited for: 2 -> 2; matrix products, arithmetic and copies ran while one was open for 41% -> 41% of each run, Pallas kernels for 6% -> 7%
where the time goes in v9:
time: 55.5 us; the launch traced here: 54.7 us
  starting transfers between devices  20.8 us (37%)
  matrix products  14.8 us (27%)
  other arithmetic  9.42 us (17%)
  waiting for transfers between devices  5.69 us (10%)
  Pallas kernels  3.57 us (6%)
    dot_general x4, matrix products, product(): value = jnp.dot(tokens, columns, preferred_element_type=jnp.float32)  13 us
    ppermute x3, starting transfers between devices, adapter_ids(): lax.ppermute(ids, 'grp', [(i, i ^ step) for i in range(group_count)])  5.04 us
    ppermute x3, starting transfers between devices, body(): lax.ppermute(reduced, 'tp', [(i, i ^ j) for i in range(tp_count)])  4.4 us
    ppermute x1, starting transfers between devices, body(): to_inner = lax.ppermute(far, 'tp', [(0, 1), (3, 2)])  4.27 us
    all_to_all x1, waiting for transfers between devices, exchange(): got = lax.all_to_all(packed, 'grp', split_axis=0, concat_axis=0, tiled=True)  3.89 us
    all_to_all x1, starting transfers between devices, exchange(): got = lax.all_to_all(packed, 'grp', split_axis=0, concat_axis=0, tiled=True)  3.58 us
    pallas_call x1, Pallas kernels, pack_adapters(): pl.pallas_call(pack_kernel, out_shape=jax.ShapeDtypeStruct((group_count,...  2.45 us
    add x1, other arithmetic, body(): base_projection = lax.optimization_barrier(own + plain(from_first))  2.18 us
  transfers between devices with their start and end apart: 11, of which 2 were waited for; matrix products, arithmetic and copies ran while one was open for 41% of the time, Pallas kernels for 7%

profile of v9, /device:TPU:0, one launch (start us, length us, event | category | flops | bytes accessed | tf_op | source)
XLA Modules:
  0.0 54.7 jit_solution(9779171979302629145)
XLA Ops:
  0.0 0.0 copy-start
  0.0 0.8 %add_bitcast_fusion = s32[1,4]{1,0:T(1,128)S(1)} fusion(s32[4]{0:T(128)} %param.12, s32[4,1]{0,1:T(1,128)} %param.11), kind=kLoop, calls=%fused_computation.56 | loop fusion | flops 8 | bytes 48 | tf_op jit(solution)/shard_map/reshape | solution.py:72
  0.8 0.5 collective-permute-start
  1.3 0.3 copy-done
  1.6 3.6 %fusion.32 = f16[512,512]{1,0:T(8,128)(2,1)} fusion(bf16[512,2048]{1,0:T(8,128)(2,1)S(1)} %copy-done, bf16[2048,2048]{1,0:T(8,128)(2,1)} %param.8, s32[]{:T(128)S(6)} %select_n.27), kind=kOutput, calls=%fused_computation.20 | convolution fusion | flops 1074266112 | bytes 4718596 | tf_op jit(solution)/shard_map/dot_general | solution.py:156
  5.3 0.0 collective-permute-done
  5.3 3.0 %collective-permute-start.1 = (s32[2,4]{1,0:T(2,128)S(1)}, s32[2,4]{1,0:T(2,128)S(1)}, u32[]{:S(2)}, u32[]{:S(2)}) collective-permute-start(s32[2,4]{1,0:T(2,128)S(1)} %pad_add_fusion.2), channel_id=1, source_target_pairs={{0,8},{4,12},{8,0},{12,4},{16,24},{20,28},{24,16},{28,20},{1,9},{5... | collective-permute-start | bytes 104 | tf_op jit(solution)/shard_map/ppermute | solution.py:75
  8.3 4.3 %collective-permute-start.3 = (f16[512,512]{1,0:T(8,128)(2,1)}, f16[512,512]{1,0:T(8,128)(2,1)}, u32[]{:S(2)}, u32[]{:S(2)}) collective-permute-start(f16[512,512]{1,0:T(8,128)(2,1)} %fusion.32), channel_id=1, source_target_pairs={{0,1},{3,2},{4,5},{7,6},{8,9},{11,10},{12,13},{15,14},{16,17},{19,... | collective-permute-start | bytes 1572872 | tf_op jit(solution)/shard_map/ppermute | solution.py:175
  12.5 1.5 %collective-permute-start.5 = (f16[512,512]{1,0:T(8,128)(2,1)}, f16[512,512]{1,0:T(8,128)(2,1)}, u32[]{:S(2)}, u32[]{:S(2)}) collective-permute-start(f16[512,512]{1,0:T(8,128)(2,1)} %fusion.32), channel_id=1, source_target_pairs={{1,2},{2,1},{5,6},{6,5},{9,10},{10,9},{13,14},{14,13},{17,18},{18,... | collective-permute-start | bytes 1572872 | tf_op jit(solution)/shard_map/ppermute | solution.py:177
  14.0 0.0 collective-permute-done.1
  14.0 1.6 %collective-permute-start.2 = (s32[4,4]{1,0:T(4,128)S(1)}, s32[4,4]{1,0:T(4,128)S(1)}, u32[]{:S(2)}, u32[]{:S(2)}) collective-permute-start(s32[4,4]{1,0:T(4,128)S(1)} %pad_add_fusion.1), channel_id=1, source_target_pairs={{0,16},{4,20},{8,24},{12,28},{16,0},{20,4},{24,8},{28,12},{1,17},{... | collective-permute-start | bytes 200 | tf_op jit(solution)/shard_map/ppermute | solution.py:75
  15.6 3.6 %fusion.29 = f16[512,512]{1,0:T(8,128)(2,1)} fusion(bf16[512,2048]{1,0:T(8,128)(2,1)S(1)} %copy-done, bf16[2048,2048]{1,0:T(8,128)(2,1)} %param.8, s32[]{:T(128)S(6)} %select_n.29), kind=kOutput, calls=%fused_computation.19 | convolution fusion | flops 1074266112 | bytes 4718596 | tf_op jit(solution)/shard_map/dot_general | solution.py:156
  19.2 0.5 collective-permute-start.4
  19.8 0.0 collective-permute-done.2
  19.8 0.6 %pad_add_fusion.ids_ref = s32[8,4]{1,0:T(8,128)} fusion(s32[4,4]{1,0:T(4,128)S(1)} %collective-permute-done.2, s32[2,4]{1,0:T(2,128)S(1)} %collective-permute-done.1, s32[1,4]{1,0:T(1,128)S(1)} %collective-permute-done, s32[1,4]{1,0:T(1,128)S(1)} %add_bitcast_fusion), kind=kLoop, calls=%fused_computation.43 | loop fusion | flops 96 | bytes 256 | tf_op jit(solution)/shard_map/concatenate | solution.py:76
  20.4 2.4 %shard_map.73 = bf16[8,2,16,2560]{3,2,1,0:T(8,128)(2,1)} custom-call(s32[8,4]{1,0:T(8,128)} %pad_add_fusion.ids_ref, s32[1]{0:T(128)} %bitcast.4.me_ref, bf16[128,16,2048]{2,1,0:T(8,128)(2,1)} %bitcast.32, bf16[128,16,512]{2,1,0:T(8,128)(2,1)} %up_ref.1), custom_call_target="tpu_custom_call" | custom-call | flops 1 | bytes 1 | tf_op jit(solution)/shard_map/pallas_call | solution.py:86
  22.8 3.6 %all-to-all-start = ((bf16[8,2,16,2560]{3,2,1,0:T(8,128)(2,1)}), bf16[8,2,16,2560]{3,2,1,0:T(8,128)(2,1)S(1)}, u32[]{:S(2)}, u32[]{:S(2)}) async-start(bf16[8,2,16,2560]{3,2,1,0:T(8,128)(2,1)} %shard_map.73), calls=%async_computation | async-start | bytes 2621440 | tf_op jit(solution)/shard_map/all_to_all | solution.py:104
  26.4 2.8 %fusion.20 = f32[512,512]{1,0:T(8,128)S(1)} fusion(bf16[512,2048]{1,0:T(8,128)(2,1)S(1)} %copy-done, bf16[2048,2048]{1,0:T(8,128)(2,1)} %param.8, s32[]{:T(128)S(6)} %select_n.31), kind=kOutput, calls=%fused_computation.13 | convolution fusion | flops 1073741824 | bytes 5242884 | tf_op jit(solution)/shard_map/dot_general | solution.py:156
  29.3 0.0 collective-permute-done.3
  29.3 2.1 %multiply_convert_fusion = f16[512,512]{1,0:T(8,128)(2,1)} fusion(f32[512,512]{1,0:T(8,128)S(1)} %fusion.20, f16[512,512]{1,0:T(8,128)(2,1)} %collective-permute-done.3), kind=kLoop, calls=%fused_computation.23 | loop fusion | flops 1310720 | bytes 2097152 | tf_op jit(solution)/shard_map/convert_element_type | solution.py:162
  31.3 1.5 %collective-permute-start.6 = (f16[512,512]{1,0:T(8,128)(2,1)}, f16[512,512]{1,0:T(8,128)(2,1)}, u32[]{:S(2)}, u32[]{:S(2)}) collective-permute-start(f16[512,512]{1,0:T(8,128)(2,1)} %multiply_convert_fusion), channel_id=1, source_target_pairs={{0,1},{3,2},{1,3},{2,0},{4,5},{7,6},{5,7},{6,4},{8,9},{11,10},{9,1... | collective-permute-start | bytes 1572872 | tf_op jit(solution)/shard_map/ppermute | solution.py:186
  32.9 0.0 copy-start.2
  32.9 2.8 %fusion.23 = f32[512,512]{1,0:T(8,128)S(1)} fusion(bf16[512,2048]{1,0:T(8,128)(2,1)S(1)} %copy-done, bf16[2048,2048]{1,0:T(8,128)(2,1)} %param.8, s32[]{:T(128)S(6)} %select_n.32), kind=kOutput, calls=%fused_computation.14 | convolution fusion | flops 1073741824 | bytes 5242884 | tf_op jit(solution)/shard_map/dot_general | solution.py:156
  35.7 0.0 copy-done.2
  35.7 0.1 iota_compare_fusion.2
  35.8 0.0 collective-permute-done.4
  35.8 2.2 %multiply_add_fusion.1 = f32[512,512]{1,0:T(8,128)} fusion(f32[512,512]{1,0:T(8,128)S(1)} %fusion.23, f16[512,512]{1,0:T(8,128)(2,1)} %collective-permute-done.4), kind=kLoop, calls=%fused_computation.22 | loop fusion | flops 786432 | bytes 2621440 | tf_op jit(solution)/shard_map/add | solution.py:189
  38.0 1.1 %shard_map.74 = s32[4]{0:T(128)} custom-call(s32[4]{0:T(128)} %bitcast.35), custom_call_target="tpu_custom_call" | custom-call | flops 99999997952 | bytes 1 | tf_op jit(solution)/shard_map/pallas_call | solution.py:110
  39.1 0.9 %convert_reduce_fusion = s32[4]{0:T(128)S(1)} fusion(s32[4]{0:T(128)} %shard_map.74), kind=kLoop, calls=%fused_computation.46 | loop fusion | flops 76 | bytes 32 | tf_op jit(solution)/shard_map/reduce_sum | solution.py:123
  40.0 0.6 %multiply_add_fusion.2 = s32[4]{0:T(128)S(1)} fusion(s32[4]{0:T(128)S(1)} %convert_reduce_fusion, s32[4]{0:T(128)} %shard_map.74), kind=kLoop, calls=%fused_computation.55 | loop fusion | flops 8 | bytes 48 | tf_op jit(solution)/shard_map/add | solution.py:123
  40.6 0.1 iota_compare_fusion
  40.7 3.9 %all-to-all-done = bf16[8,2,16,2560]{3,2,1,0:T(8,128)(2,1)S(1)} async-done(((bf16[8,2,16,2560]{3,2,1,0:T(8,128)(2,1)}), bf16[8,2,16,2560]{3,2,1,0:T(8,128)(2,1)S(1)}, u32[]{:S(2)}, u32[]{:S(2)}) %all-to-all-start) | async-done | bytes 1310752 | tf_op jit(solution)/shard_map/all_to_all | solution.py:104
  44.6 0.0 copy-start.1
  44.6 0.7 %select_reduce_fusion = bf16[4,16,2560]{2,1,0:T(8,128)(2,1)S(1)} fusion(pred[4,16]{1,0:T(4,128)(4,1)S(1)} %iota_compare_fusion, bf16[16,16,2560]{2,1,0:T(8,128)(2,1)S(1)} %bitcast.33), kind=kLoop, calls=%fused_computation | loop fusion | flops 5079040 | bytes 1638464 | tf_op jit(solution)/shard_map/reduce_sum | solution.py:129
  45.2 0.6 %fusion.35 = f32[4,16,128]{2,1,0:T(8,128)S(1)} fusion(bf16[4,128,2048]{2,1,0:T(8,128)(2,1)S(1)} %bitcast.31, bf16[4,16,2560]{2,1,0:T(8,128)(2,1)S(1)} %select_reduce_fusion), kind=kOutput, calls=%fused_computation.24 | convolution fusion | flops 33554432 | bytes 2392064 | tf_op jit(solution)/shard_map/nbd,nrd->nrb/dot_general | solution.py:132
  45.9 2.5 %collective-permute-start.9 = (f32[4,16,128]{2,1,0:T(8,128)S(1)}, f32[4,16,128]{2,1,0:T(8,128)S(1)}, u32[]{:S(2)}, u32[]{:S(2)}) collective-permute-start(f32[4,16,128]{2,1,0:T(8,128)S(1)} %fusion.35), channel_id=1, source_target_pairs={{0,3},{1,2},{2,1},{3,0},{4,7},{5,6},{6,5},{7,4},{8,11},{9,10},{10,... | collective-permute-start | bytes 98312 | tf_op jit(solution)/shard_map/ppermute | solution.py:201
  48.4 0.5 collective-permute-start.8
  48.9 1.4 %collective-permute-start.7 = (f32[4,16,128]{2,1,0:T(8,128)S(1)}, f32[4,16,128]{2,1,0:T(8,128)S(1)}, u32[]{:S(2)}, u32[]{:S(2)}) collective-permute-start(f32[4,16,128]{2,1,0:T(8,128)S(1)} %fusion.35), channel_id=1, source_target_pairs={{0,1},{1,0},{2,3},{3,2},{4,5},{5,4},{6,7},{7,6},{8,9},{9,8},{10,11... | collective-permute-start | bytes 98312 | tf_op jit(solution)/shard_map/ppermute | solution.py:201
  50.3 0.0 collective-permute-done.6
  50.3 0.0 collective-permute-done.5
  50.3 0.0 copy-done.1
  50.3 1.4 %multiply_add_fusion = f32[512,512]{1,0:T(8,128)S(1)} fusion(f16[512,512]{1,0:T(8,128)(2,1)} %collective-permute-done.6, f32[512,512]{1,0:T(8,128)S(1)} %copy-done.1, f16[512,512]{1,0:T(8,128)(2,1)} %collective-permute-done.5), kind=kLoop, calls=%fused_computation.21 | loop fusion | flops 1572864 | bytes 3145728 | tf_op jit(solution)/shard_map/add | solution.py:193
  51.7 0.0 collective-permute-done.9
  51.8 1.8 %collective-permute-done.8 = f32[4,16,128]{2,1,0:T(8,128)S(1)} collective-permute-done((f32[4,16,128]{2,1,0:T(8,128)S(1)}, f32[4,16,128]{2,1,0:T(8,128)S(1)}, u32[]{:S(2)}, u32[]{:S(2)}) %collective-permute-start.8) | collective-permute-done | bytes 32800 | tf_op jit(solution)/shard_map/ppermute | solution.py:201
  53.5 0.0 collective-permute-done.7
  53.6 1.2 %fusion.28 = bf16[4,128,512]{2,1,0:T(8,128)(2,1)} fusion(f32[4,128,512]{2,1,0:T(8,128)S(1)} %bitcast.34, pred[4,128]{1,0:T(4,128)(4,1)S(1)} %iota_compare_fusion.2, bf16[4,16,512]{2,1,0:T(8,128)(2,1)S(1)} %slice.9, bf16[4,16,128]{2,1,0:T(8,128)(2,1)S(1)} %get-tuple-element.32, bf16[4,16,128]{2,1,0:T(8,128)(2,1)S(1)} %get-tuple-element.31, ...), kind=kOutput, calls=%fused_computation.18 | convolution fusion | flops 26951680 | bytes 1688064 | tf_op jit(solution)/shard_map/nrb,nro->nbo/dot_general | solution.py:145
  (5 shorter events, 0.0 us)
Async XLA Ops:
  0.0 1.6 %copy-start = (bf16[512,2048]{1,0:T(8,128)(2,1)S(1)}, bf16[512,2048]{1,0:T(8,128)(2,1)}, u32[]{:S(2)}) copy-start(bf16[512,2048]{1,0:T(8,128)(2,1)} %param.7) | copy-start | bytes 6291460
  0.8 4.4 %collective-permute-start = (s32[1,4]{1,0:T(1,128)S(1)}, s32[1,4]{1,0:T(1,128)S(1)}, u32[]{:S(2)}, u32[]{:S(2)}) collective-permute-start(s32[1,4]{1,0:T(1,128)S(1)} %add_bitcast_fusion), channel_id=1, source_target_pairs={{0,4},{4,0},{8,12},{12,8},{16,20},{20,16},{24,28},{28,24},{1,5},{5... | collective-permute-start | bytes 56 | tf_op jit(solution)/shard_map/ppermute | solution.py:75
  5.3 8.7 %collective-permute-start.1 = (s32[2,4]{1,0:T(2,128)S(1)}, s32[2,4]{1,0:T(2,128)S(1)}, u32[]{:S(2)}, u32[]{:S(2)}) collective-permute-start(s32[2,4]{1,0:T(2,128)S(1)} %pad_add_fusion.2), channel_id=1, source_target_pairs={{0,8},{4,12},{8,0},{12,4},{16,24},{20,28},{24,16},{28,20},{1,9},{5... | collective-permute-start | bytes 104 | tf_op jit(solution)/shard_map/ppermute | solution.py:75
  8.3 21.0 %collective-permute-start.3 = (f16[512,512]{1,0:T(8,128)(2,1)}, f16[512,512]{1,0:T(8,128)(2,1)}, u32[]{:S(2)}, u32[]{:S(2)}) collective-permute-start(f16[512,512]{1,0:T(8,128)(2,1)} %fusion.32), channel_id=1, source_target_pairs={{0,1},{3,2},{4,5},{7,6},{8,9},{11,10},{12,13},{15,14},{16,17},{19,... | collective-permute-start | bytes 1572872 | tf_op jit(solution)/shard_map/ppermute | solution.py:175
  12.5 37.7 %collective-permute-start.5 = (f16[512,512]{1,0:T(8,128)(2,1)}, f16[512,512]{1,0:T(8,128)(2,1)}, u32[]{:S(2)}, u32[]{:S(2)}) collective-permute-start(f16[512,512]{1,0:T(8,128)(2,1)} %fusion.32), channel_id=1, source_target_pairs={{1,2},{2,1},{5,6},{6,5},{9,10},{10,9},{13,14},{14,13},{17,18},{18,... | collective-permute-start | bytes 1572872 | tf_op jit(solution)/shard_map/ppermute | solution.py:177
  14.0 5.8 %collective-permute-start.2 = (s32[4,4]{1,0:T(4,128)S(1)}, s32[4,4]{1,0:T(4,128)S(1)}, u32[]{:S(2)}, u32[]{:S(2)}) collective-permute-start(s32[4,4]{1,0:T(4,128)S(1)} %pad_add_fusion.1), channel_id=1, source_target_pairs={{0,16},{4,20},{8,24},{12,28},{16,0},{20,4},{24,8},{28,12},{1,17},{... | collective-permute-start | bytes 200 | tf_op jit(solution)/shard_map/ppermute | solution.py:75
  19.2 16.6 %collective-permute-start.4 = (f16[512,512]{1,0:T(8,128)(2,1)}, f16[512,512]{1,0:T(8,128)(2,1)}, u32[]{:S(2)}, u32[]{:S(2)}) collective-permute-start(f16[512,512]{1,0:T(8,128)(2,1)} %fusion.29), channel_id=1, source_target_pairs={{0,2},{3,1},{1,0},{2,3},{4,6},{7,5},{5,4},{6,7},{8,10},{11,9},{9,8... | collective-permute-start | bytes 1572872 | tf_op jit(solution)/shard_map/ppermute | solution.py:180
  22.8 21.7 %all-to-all-start = ((bf16[8,2,16,2560]{3,2,1,0:T(8,128)(2,1)}), bf16[8,2,16,2560]{3,2,1,0:T(8,128)(2,1)S(1)}, u32[]{:S(2)}, u32[]{:S(2)}) async-start(bf16[8,2,16,2560]{3,2,1,0:T(8,128)(2,1)} %shard_map.73), calls=%async_computation | async-start | bytes 2621440 | tf_op jit(solution)/shard_map/all_to_all | solution.py:104
  31.3 18.9 %collective-permute-start.6 = (f16[512,512]{1,0:T(8,128)(2,1)}, f16[512,512]{1,0:T(8,128)(2,1)}, u32[]{:S(2)}, u32[]{:S(2)}) collective-permute-start(f16[512,512]{1,0:T(8,128)(2,1)} %multiply_convert_fusion), channel_id=1, source_target_pairs={{0,1},{3,2},{1,3},{2,0},{4,5},{7,6},{5,7},{6,4},{8,9},{11,10},{9,1... | collective-permute-start | bytes 1572872 | tf_op jit(solution)/shard_map/ppermute | solution.py:186
  32.9 2.9 %copy-start.2 = (s32[4]{0:T(128)S(1)}, s32[4]{0:T(128)}, u32[]{:S(2)}) copy-start(s32[4]{0:T(128)} %param.13) | copy-start | bytes 52
  44.6 5.7 %copy-start.1 = (f32[512,512]{1,0:T(8,128)S(1)}, f32[512,512]{1,0:T(8,128)}, u32[]{:S(2)}) copy-start(f32[512,512]{1,0:T(8,128)} %multiply_add_fusion.1) | copy-start | bytes 3145732
  45.9 5.9 %collective-permute-start.9 = (f32[4,16,128]{2,1,0:T(8,128)S(1)}, f32[4,16,128]{2,1,0:T(8,128)S(1)}, u32[]{:S(2)}, u32[]{:S(2)}) collective-permute-start(f32[4,16,128]{2,1,0:T(8,128)S(1)} %fusion.35), channel_id=1, source_target_pairs={{0,3},{1,2},{2,1},{3,0},{4,7},{5,6},{6,5},{7,4},{8,11},{9,10},{10,... | collective-permute-start | bytes 98312 | tf_op jit(solution)/shard_map/ppermute | solution.py:201
  48.4 5.2 %collective-permute-start.8 = (f32[4,16,128]{2,1,0:T(8,128)S(1)}, f32[4,16,128]{2,1,0:T(8,128)S(1)}, u32[]{:S(2)}, u32[]{:S(2)}) collective-permute-start(f32[4,16,128]{2,1,0:T(8,128)S(1)} %fusion.35), channel_id=1, source_target_pairs={{0,2},{1,3},{2,0},{3,1},{4,6},{5,7},{6,4},{7,5},{8,10},{9,11},{10,... | collective-permute-start | bytes 98312 | tf_op jit(solution)/shard_map/ppermute | solution.py:201
  48.9 4.7 %collective-permute-start.7 = (f32[4,16,128]{2,1,0:T(8,128)S(1)}, f32[4,16,128]{2,1,0:T(8,128)S(1)}, u32[]{:S(2)}, u32[]{:S(2)}) collective-permute-start(f32[4,16,128]{2,1,0:T(8,128)S(1)} %fusion.35), channel_id=1, source_target_pairs={{0,1},{1,0},{2,3},{3,2},{4,5},{5,4},{6,7},{7,6},{8,9},{9,8},{10,11... | collective-permute-start | bytes 98312 | tf_op jit(solution)/shard_map/ppermute | solution.py:201
